TPU v7x, 32 devices: a whole 2x2x4 slice. The times are simulated.
32 devices in a mesh: pass: 2 (over y), rows: 16 (over z, x, core).
Axes of the slice: x: 2, y: 2, z: 4, core: 2. Of those that a mesh axis runs over, the one named last changes fastest.
Arguments:
- stream: bfloat16 [2, 16, 1024, 768], P('pass', 'rows'), may hold values from -6 to 6
- lengths: int32 [16], P('rows'), may hold values from 256 to 1024, as said below
- pass_embed: bfloat16 [2, 768], replicated, may hold values from -3 to 3
- first_gain: bfloat16 [2, 768], replicated, may hold values from 0.5 to 1.5
- first_bias: bfloat16 [2, 768], replicated, may hold values from -1.5 to 1.5
- triple_weight: bfloat16 [2, 768, 2304], replicated, may hold values from -0.21875 to 0.21875
- merge_weight: bfloat16 [2, 768, 768], replicated, may hold values from -6 to 6
- second_gain: bfloat16 [2, 768], replicated, may hold values from 0.5 to 1.5
- second_bias: bfloat16 [2, 768], replicated, may hold values from -1.5 to 1.5
- up_weight: bfloat16 [2, 768, 3072], replicated, may hold values from -0.21875 to 0.21875
- down_weight: bfloat16 [2, 3072, 768], replicated, may hold values from -0.109375 to 0.109375
- cotangent: bfloat16 [2, 16, 1024, 768], P('pass', 'rows'), may hold values from -6 to 6
Outputs:
- output: bfloat16 [2, 16, 1024, 768], P('pass', 'rows')
- input_grad: bfloat16 [2, 16, 1024, 768], P('pass', 'rows')
- pass_embed_grad: float32 [2, 768], P(None, 'rows')
- first_gain_grad: float32 [2, 768], P(None, 'rows')
- first_bias_grad: float32 [2, 768], P(None, 'rows')
- triple_grad: float32 [2, 768, 2304], P(None, 'rows')
- merge_grad: float32 [2, 768, 768], P(None, 'rows')
- second_gain_grad: float32 [2, 768], P(None, 'rows')
- second_bias_grad: float32 [2, 768], P(None, 'rows')
- up_grad: float32 [2, 768, 3072], P(None, 'rows')
- down_grad: float32 [2, 3072, 768], P(None, 'rows')
Inputs may be any that keep to these rules, and one draw needn't show every extreme that they name: `lengths`: each is at least 256; in every draw some sequence has exactly 1024.
All inputs are finite; a program needn't handle non-finite values.
Results may differ from a plain program's by a relative error of at most 0.015.
Values may be sent and summed in bfloat16 or wider, within the bound.
A program may use at most 320 MiB of HBM per device.

v0:
```python
import jax
import jax.numpy as jnp
from jax import lax
from jax.sharding import PartitionSpec as P

HEAD_DIM = 64


epsilon = 1e-05


def norm_forward(hidden, gain, bias):
    row_mean = jnp.mean(hidden, -1, keepdims=True)
    centred = hidden - row_mean
    inverse = lax.rsqrt(jnp.mean(centred * centred, -1, keepdims=True) + epsilon)
    scaled = centred * inverse
    return (scaled * gain + bias, scaled, inverse)


def norm_backward(grad_out, scaled, inverse, gain):
    grad_scaled = grad_out * gain
    grad_in = inverse * (
        grad_scaled
        - jnp.mean(grad_scaled, -1, keepdims=True)
        - scaled * jnp.mean(grad_scaled * scaled, -1, keepdims=True)
    )
    return (grad_in, jnp.sum(grad_out * scaled, 0), jnp.sum(grad_out, 0))


def project(left, right):
    return jnp.dot(left, right, preferred_element_type=jnp.float32)


def weight_grad(left, right):
    return lax.dot_general(
        left, right, (((0,), (0,)), ((), ())), preferred_element_type=jnp.float32
    )


def back_project(grad, weight):
    return lax.dot_general(
        grad, weight, (((1,), (1,)), ((), ())), preferred_element_type=jnp.float32
    )


def heads_first(block, head_count):
    return block.reshape(block.shape[0], head_count, -1).transpose(1, 0, 2)


def heads_last(block):
    return block.transpose(1, 0, 2).reshape(block.shape[1], -1)


def allowed_mask(own_pass, passes, block_start, block_rows, window, row_length):
    query_pos = block_start + jnp.arange(block_rows)
    key_pos = jnp.tile(jnp.arange(window), passes)
    key_pass = jnp.repeat(jnp.arange(passes), window)
    earlier = key_pos[None, :] < query_pos[:, None]
    same_step = (key_pos[None, :] == query_pos[:, None]) & (key_pass[None, :] <= own_pass)
    return (earlier | same_step) & (key_pos[None, :] < row_length)


def attend_forward(triple, kv_all, lengths, own_pass, head_count, score_scale):
    seq_count, slot_count, triple_width = triple.shape
    model_width = triple_width // 3
    passes = kv_all.shape[0]
    block_rows = min(512, slot_count)
    outputs, totals = ([], [])
    seq_out = []
    seq_total = []
    for block_start in range(0, slot_count, block_rows):
        window = block_start + block_rows
        allowed = allowed_mask(own_pass, passes, block_start, block_rows, window, lengths[0])
        queries = heads_first(triple[0, block_start:window, :model_width], head_count)
        key_block = heads_first(
            kv_all[:, 0, :window, :model_width].reshape(-1, model_width), head_count
        )
        value_block = heads_first(
            kv_all[:, 0, :window, model_width:].reshape(-1, model_width), head_count
        )

        def head_forward(operands):
            head_query, head_key, head_value = operands
            raw_score = (
                jnp.einsum("qd,kd->qk", head_query, head_key, preferred_element_type=jnp.float32)
                * score_scale
            )
            masked = jnp.where(allowed, raw_score, -jnp.inf)
            row_max = jnp.max(masked, -1, keepdims=True)
            exponent = jnp.exp(masked - row_max)
            row_total = jnp.sum(exponent, -1, keepdims=True)
            softmax = (exponent / row_total).astype(jnp.bfloat16)
            head_out = jnp.dot(softmax, head_value, preferred_element_type=jnp.float32)
            return (head_out, row_max[:, 0] + jnp.log(row_total[:, 0]))

        head_out, head_total = lax.map(head_forward, (queries, key_block, value_block))
        seq_out.append(heads_last(head_out))
        seq_total.append(head_total)
    outputs.append(jnp.concatenate(seq_out, 0))
    totals.append(jnp.concatenate(seq_total, 1))
    return (jnp.stack(outputs), jnp.stack(totals))


def attend_backward(
    triple, kv_all, log_total, grad_mixed, lengths, own_pass, head_count, score_scale
):
    seq_count, slot_count, triple_width = triple.shape
    model_width = triple_width // 3
    passes = kv_all.shape[0]
    block_rows = min(512, slot_count)
    grad_kv = jnp.zeros((passes, seq_count, slot_count, 2 * model_width), jnp.float32)
    seq_grad = []
    for block_start in range(0, slot_count, block_rows):
        window = block_start + block_rows
        allowed = allowed_mask(own_pass, passes, block_start, block_rows, window, lengths[0])
        queries = heads_first(triple[0, block_start:window, :model_width], head_count)
        key_block = heads_first(
            kv_all[:, 0, :window, :model_width].reshape(-1, model_width), head_count
        )
        value_block = heads_first(
            kv_all[:, 0, :window, model_width:].reshape(-1, model_width), head_count
        )
        grad_block = heads_first(grad_mixed[0, block_start:window], head_count)
        total_block = log_total[0][:, block_start:window]

        def head_backward(operands):
            head_query, head_key, head_value, head_grad, head_total = operands
            raw_score = (
                jnp.einsum("qd,kd->qk", head_query, head_key, preferred_element_type=jnp.float32)
                * score_scale
            )
            masked = jnp.where(allowed, raw_score, -jnp.inf)
            softmax = jnp.exp(masked - head_total[:, None])
            grad_prob = jnp.einsum(
                "qd,kd->qk", head_grad, head_value, preferred_element_type=jnp.float32
            )
            inner = jnp.sum(softmax * grad_prob, -1, keepdims=True)
            grad_score = (softmax * (grad_prob - inner)).astype(jnp.bfloat16)
            grad_query = (
                jnp.dot(grad_score, head_key, preferred_element_type=jnp.float32) * score_scale
            )
            grad_key = (
                jnp.einsum("qk,qd->kd", grad_score, head_query, preferred_element_type=jnp.float32)
                * score_scale
            )
            grad_value = jnp.einsum(
                "qk,qd->kd",
                softmax.astype(jnp.bfloat16),
                head_grad,
                preferred_element_type=jnp.float32,
            )
            return (grad_query, grad_key, grad_value)

        head_query_grad, head_key_grad, head_value_grad = lax.map(
            head_backward, (queries, key_block, value_block, grad_block, total_block)
        )
        seq_grad.append(heads_last(head_query_grad))
        piece = jnp.concatenate([heads_last(head_key_grad), heads_last(head_value_grad)], -1)
        grad_kv = grad_kv.at[:, 0, :window].add(piece.reshape(passes, window, 2 * model_width))
    grad_queries = [jnp.concatenate(seq_grad, 0)]
    return (jnp.stack(grad_queries), grad_kv)


def local(
    stream,
    lengths,
    pass_embed,
    first_gain,
    first_bias,
    triple_weight,
    merge_weight,
    second_gain,
    second_bias,
    up_weight,
    down_weight,
    cotangent,
):
    own_pass = lax.axis_index("pass")
    seq_count, slot_count, model_width = (stream.shape[1], stream.shape[2], stream.shape[3])
    head_count = model_width // HEAD_DIM
    score_scale = HEAD_DIM ** (-0.5)
    layers = triple_weight.shape[0]
    passes = pass_embed.shape[0]
    token_count = seq_count * slot_count
    valid_rows = (
        (jnp.arange(slot_count)[None, :] < lengths[:, None])
        .astype(jnp.float32)
        .reshape(token_count, 1)
    )
    pass_pick = (jnp.arange(passes) == own_pass).astype(jnp.float32)
    embed_row = jnp.sum(pass_pick[:, None] * pass_embed.astype(jnp.float32), 0)
    hidden = stream[0].reshape(token_count, model_width).astype(jnp.float32) + embed_row
    stored = []
    for depth in range(layers):
        normed, scaled_one, inverse_one = norm_forward(
            hidden, first_gain[depth].astype(jnp.float32), first_bias[depth].astype(jnp.float32)
        )
        normed = normed.astype(jnp.bfloat16)
        triple = (
            project(normed, triple_weight[depth])
            .astype(jnp.bfloat16)
            .reshape(seq_count, slot_count, 3 * model_width)
        )
        kv_all = lax.all_gather(triple[None, :, :, model_width:], "pass", axis=0, tiled=True)
        mixed_out, log_total = attend_forward(
            triple, kv_all, lengths, own_pass, head_count, score_scale
        )
        mixed_out = mixed_out.reshape(token_count, model_width).astype(jnp.bfloat16)
        hidden_mid = hidden + project(mixed_out, merge_weight[depth])
        normed_two, scaled_two, inverse_two = norm_forward(
            hidden_mid,
            second_gain[depth].astype(jnp.float32),
            second_bias[depth].astype(jnp.float32),
        )
        normed_two = normed_two.astype(jnp.bfloat16)
        pre_act = project(normed_two, up_weight[depth])
        activation = jax.nn.gelu(pre_act, approximate=True).astype(jnp.bfloat16)
        hidden = hidden_mid + project(activation, down_weight[depth])
        stored.append(
            (
                normed,
                scaled_one,
                inverse_one,
                triple,
                kv_all,
                log_total,
                mixed_out,
                normed_two,
                scaled_two,
                inverse_two,
                pre_act,
                activation,
            )
        )
    output = (
        (hidden * valid_rows).astype(jnp.bfloat16).reshape(1, seq_count, slot_count, model_width)
    )
    grad_hidden = cotangent[0].reshape(token_count, model_width).astype(jnp.float32) * valid_rows
    grads_triple, grads_merge, grads_up, grads_down = ([], [], [], [])
    grads_gain_one, grads_bias_one, grads_gain_two, grads_bias_two = ([], [], [], [])
    for depth in reversed(range(layers)):
        (
            normed,
            scaled_one,
            inverse_one,
            triple,
            kv_all,
            log_total,
            mixed_out,
            normed_two,
            scaled_two,
            inverse_two,
            pre_act,
            activation,
        ) = stored[depth]
        grad_down = grad_hidden.astype(jnp.bfloat16)
        grads_down.append(weight_grad(activation, grad_down))
        grad_act = back_project(grad_down, down_weight[depth])
        _, gelu_pull = jax.vjp(lambda value_in: jax.nn.gelu(value_in, approximate=True), pre_act)
        grad_pre = gelu_pull(grad_act)[0].astype(jnp.bfloat16)
        grads_up.append(weight_grad(normed_two, grad_pre))
        grad_normed_two = back_project(grad_pre, up_weight[depth])
        grad_norm_two, gain_two, bias_two = norm_backward(
            grad_normed_two, scaled_two, inverse_two, second_gain[depth].astype(jnp.float32)
        )
        grads_gain_two.append(gain_two)
        grads_bias_two.append(bias_two)
        grad_mid = grad_hidden + grad_norm_two
        grad_branch = grad_mid.astype(jnp.bfloat16)
        grads_merge.append(weight_grad(mixed_out, grad_branch))
        grad_mixed = back_project(grad_branch, merge_weight[depth]).astype(jnp.bfloat16)
        grad_query, grad_kv_all = attend_backward(
            triple,
            kv_all,
            log_total,
            grad_mixed.reshape(seq_count, slot_count, model_width),
            lengths,
            own_pass,
            head_count,
            score_scale,
        )
        grad_kv = lax.psum_scatter(
            grad_kv_all.astype(jnp.bfloat16), "pass", scatter_dimension=0, tiled=True
        ).astype(jnp.float32)
        grad_triple = jnp.concatenate([grad_query, grad_kv[0]], -1).astype(jnp.bfloat16)
        grad_triple = grad_triple.reshape(token_count, 3 * model_width)
        grads_triple.append(weight_grad(normed, grad_triple))
        grad_normed = back_project(grad_triple, triple_weight[depth])
        grad_norm_one, gain_one, bias_one = norm_backward(
            grad_normed, scaled_one, inverse_one, first_gain[depth].astype(jnp.float32)
        )
        grads_gain_one.append(gain_one)
        grads_bias_one.append(bias_one)
        grad_hidden = grad_mid + grad_norm_one
    input_grad = grad_hidden.astype(jnp.bfloat16).reshape(1, seq_count, slot_count, model_width)
    pass_grad = pass_pick[:, None] * jnp.sum(grad_hidden, 0)[None, :]
    triple_sum = jnp.stack(grads_triple[::-1])
    merge_sum = jnp.stack(grads_merge[::-1])
    up_sum = jnp.stack(grads_up[::-1])
    down_sum = jnp.stack(grads_down[::-1])
    gain_one_sum = jnp.stack(grads_gain_one[::-1])
    bias_one_sum = jnp.stack(grads_bias_one[::-1])
    gain_two_sum = jnp.stack(grads_gain_two[::-1])
    bias_two_sum = jnp.stack(grads_bias_two[::-1])
    shares = (
        lax.psum_scatter(pass_grad, "rows", scatter_dimension=1, tiled=True),
        lax.psum_scatter(gain_one_sum, "rows", scatter_dimension=1, tiled=True),
        lax.psum_scatter(bias_one_sum, "rows", scatter_dimension=1, tiled=True),
        lax.psum_scatter(triple_sum, "rows", scatter_dimension=1, tiled=True),
        lax.psum_scatter(merge_sum, "rows", scatter_dimension=1, tiled=True),
        lax.psum_scatter(gain_two_sum, "rows", scatter_dimension=1, tiled=True),
        lax.psum_scatter(bias_two_sum, "rows", scatter_dimension=1, tiled=True),
        lax.psum_scatter(up_sum, "rows", scatter_dimension=1, tiled=True),
        lax.psum_scatter(down_sum, "rows", scatter_dimension=1, tiled=True),
    )
    totals = (
        lax.psum(shares[0].astype(jnp.bfloat16), "pass").astype(jnp.float32),
        lax.psum(shares[1].astype(jnp.bfloat16), "pass").astype(jnp.float32),
        lax.psum(shares[2].astype(jnp.bfloat16), "pass").astype(jnp.float32),
        lax.psum(shares[3].astype(jnp.bfloat16), "pass").astype(jnp.float32),
        lax.psum(shares[4].astype(jnp.bfloat16), "pass").astype(jnp.float32),
        lax.psum(shares[5].astype(jnp.bfloat16), "pass").astype(jnp.float32),
        lax.psum(shares[6].astype(jnp.bfloat16), "pass").astype(jnp.float32),
        lax.psum(shares[7].astype(jnp.bfloat16), "pass").astype(jnp.float32),
        lax.psum(shares[8].astype(jnp.bfloat16), "pass").astype(jnp.float32),
    )
    return (
        output,
        input_grad,
        totals[0],
        totals[1],
        totals[2],
        totals[3],
        totals[4],
        totals[5],
        totals[6],
        totals[7],
        totals[8],
    )


def solution(mesh):
    in_specs = (
        P("pass", "rows", None, None),
        P("rows"),
        P(),
        P(),
        P(),
        P(),
        P(),
        P(),
        P(),
        P(),
        P(),
        P("pass", "rows", None, None),
    )
    out_specs = (
        P("pass", "rows", None, None),
        P("pass", "rows", None, None),
        P(None, "rows"),
        P(None, "rows"),
        P(None, "rows"),
        P(None, "rows", None),
        P(None, "rows", None),
        P(None, "rows"),
        P(None, "rows"),
        P(None, "rows", None),
        P(None, "rows", None),
    )
    return jax.shard_map(local, mesh=mesh, in_specs=in_specs, out_specs=out_specs, check_vma=False)
```

profile of v0, /device:TPU:0, one launch (start us, length us, event | category | flops | bytes accessed | tf_op | source)
XLA Modules:
  0.0 2609.4 jit_solution(2629079393254379028)
XLA Ops:
  27.9 76.3 %all-gather.5.cloned.1.call-done = bf16[2,1024,1536]{2,1,0:T(8,128)(2,1)} async-done(((bf16[1,1024,1536]{2,1,0:T(8,128)(2,1)}), bf16[2,1024,1536]{2,1,0:T(8,128)(2,1)}) %all-gather.5.cloned.1.call-update) | async-done | bytes 6291472 | tf_op jit(solution)/shard_map/all_gather | solution.py:204
  127.2 50.6 %while.116 = (s32[]{:T(128)}, bf16[12,512,64]{1,2,0:T(8,128)(2,1)S(1)}, f32[12,512]{1,0:T(8,128)S(1)}, bf16[12,512,64]{2,1,0:T(8,128)(2,1)}, bf16[12,1024,64]{2,...) while((s32[]{:T(128)}, ...), condition=%wide.region_6.7_spmd.clone, body=%wide.region_3.6_spmd.clone.sunk | while | flops 141032960 | bytes 7106673 | solution.py:96
  215.5 107.9 %while.117 = (s32[]{:T(128)}, bf16[12,512,64]{1,2,0:T(8,128)(2,1)S(1)}, f32[12,512]{1,0:T(8,128)S(1)}, bf16[12,512,64]{2,1,0:T(8,128)(2,1)}, bf16[12,2048,64]{2,...) while((s32[]{:T(128)}, ...), condition=%wide.region_10.11_spmd.clone, body=%wide.region_7.10_spmd.clone.sunk | while | flops 282066432 | bytes 30707860 | solution.py:96
  327.5 10.9 fusion.209
  361.6 11.4 fusion.195
  378.3 61.5 %all-gather.7.cloned.1.call-done = bf16[2,1024,1536]{2,1,0:T(8,128)(2,1)} async-done(((bf16[1,1024,1536]{2,1,0:T(8,128)(2,1)}), bf16[2,1024,1536]{2,1,0:T(8,128)(2,1)}) %all-gather.7.cloned.1.call-update) | async-done | bytes 6291472 | tf_op jit(solution)/shard_map/all_gather | solution.py:204
  462.9 50.6 %while.118 = (s32[]{:T(128)}, bf16[12,512,64]{1,2,0:T(8,128)(2,1)S(1)}, f32[12,512]{1,0:T(8,128)S(1)}, bf16[12,512,64]{2,1,0:T(8,128)(2,1)}, bf16[12,1024,64]{2,...) while((s32[]{:T(128)}, ...), condition=%wide.region_18.19_spmd.clone, body=%wide.region_15.18_spmd.clone.sunk | while | flops 141032960 | bytes 7106673 | solution.py:96
  550.5 107.9 %while.119 = (s32[]{:T(128)}, bf16[12,512,64]{1,2,0:T(8,128)(2,1)S(1)}, f32[12,512]{1,0:T(8,128)S(1)}, bf16[12,512,64]{2,1,0:T(8,128)(2,1)}, bf16[12,2048,64]{2,...) while((s32[]{:T(128)}, ...), condition=%wide.region_22.23_spmd.clone, body=%wide.region_19.22_spmd.clone.sunk | while | flops 282066432 | bytes 30707860 | solution.py:96
  664.4 20.7 fusion.189
  711.3 112.2 %while.120 = (s32[]{:T(128)}, bf16[12,512,64]{1,2,0:T(8,128)(2,1)}, f32[12,1024,64]{1,2,0:T(8,128)S(1)}, f32[12,1024,64]{1,2,0:T(8,128)}, bf16[12,512,64]{2,1,0:...) while((s32[]{:T(128)}, bf16[12,512,64]{1,2,0:T(8,128)(2,1)}, ...), condition=%wide.region_29.30_spmd.clone, body=%wide.region_27.29_spmd.clone.sunk | while | flops 342982144 | bytes 17716352 | solution.py:154
  833.4 145.1 %while.121 = (s32[]{:T(128)}, bf16[12,512,64]{1,2,0:T(8,128)(2,1)S(1)}, f32[12,2048,64]{1,2,0:T(8,128)}, f32[12,2048,64]{1,2,0:T(8,128)}, bf16[12,512,64]{2,1,0:...) while((s32[]{:T(128)}, ...), condition=%wide.region_32.33_spmd.clone, body=%wide.region_30.32_spmd.clone.sunk | while | flops 685932032 | bytes 34763912 | solution.py:154
  1023.3 17.2 fusion.192
  1049.8 16.2 copy.267
  1069.3 74.0 %reduce-scatter.22.cloned.1.call-done = bf16[1,1,1024,1536]{3,2,1,0:T(8,128)(2,1)} async-done(((bf16[2,1,1024,1536]{3,2,1,0:T(8,128)(2,1)}), bf16[1,1,1024,1536]{3,2,1,0:T(8,128)(2,1)}) %reduce-scatter.22.cloned.1.call-update) | async-done | bytes 3145744 | tf_op jit(solution)/shard_map/reduce_scatter | solution.py:282
  1160.9 17.8 fusion.182
  1206.7 141.3 %while.123 = (s32[]{:T(128)}, bf16[12,512,64]{1,2,0:T(8,128)(2,1)S(1)}, f32[12,2048,64]{1,2,0:T(8,128)}, f32[12,2048,64]{1,2,0:T(8,128)}, bf16[12,512,64]{2,1,0:...) while((s32[]{:T(128)}, ...), condition=%wide.region_43.44_spmd.clone, body=%wide.region_41.43_spmd.clone.sunk | while | flops 685932032 | bytes 34763912 | solution.py:154
  1353.0 120.8 %while.122 = (s32[]{:T(128)}, bf16[12,512,64]{1,2,0:T(8,128)(2,1)}, f32[12,1024,64]{1,2,0:T(8,128)S(1)}, f32[12,1024,64]{1,2,0:T(8,128)}, bf16[12,512,64]{2,1,0:...) while((s32[]{:T(128)}, bf16[12,512,64]{1,2,0:T(8,128)(2,1)}, ...), condition=%wide.region_40.41_spmd.clone, body=%wide.region_38.40_spmd.clone.sunk | while | flops 342982144 | bytes 17716352 | solution.py:154
  1531.9 11.0 fusion.191
  1552.4 11.9 convolution_bitcast_fusion.6
  1564.3 11.0 convolution_bitcast_fusion.7
  1629.8 12.3 pad_maximum_fusion.2
  1668.4 31.0 %reduce-scatter.28.cloned.1.call-done = f32[2,48,768]{2,1,0:T(8,128)} async-done(((f32[2,768,768]{2,1,0:T(8,128)}), f32[2,48,768]{2,1,0:T(8,128)}) %reduce-scatter.28.cloned.1.call-update) | async-done | bytes 294928 | tf_op jit(solution)/shard_map/reduce_scatter | solution.py:310
  1701.1 196.9 %reduce-scatter.32.cloned.1.call-done = f32[2,192,768]{2,1,0:T(8,128)} async-done(((f32[2,3072,768]{2,1,0:T(8,128)}), f32[2,192,768]{2,1,0:T(8,128)}) %reduce-scatter.32.cloned.1.call-update) | async-done | bytes 1179664 | tf_op jit(solution)/shard_map/reduce_scatter | solution.py:314
  1900.1 196.4 %reduce-scatter.30.cloned.1.call-done = f32[2,48,3072]{2,1,0:T(8,128)} async-done(((f32[2,768,3072]{2,1,0:T(8,128)}), f32[2,48,3072]{2,1,0:T(8,128)}) %reduce-scatter.30.cloned.1.call-update) | async-done | bytes 1179664 | tf_op jit(solution)/shard_map/reduce_scatter | solution.py:313
  2098.7 147.3 %reduce-scatter.26.cloned.1.call-done = f32[2,48,2304]{2,1,0:T(8,128)} async-done(((f32[2,768,2304]{2,1,0:T(8,128)}), f32[2,48,2304]{2,1,0:T(8,128)}) %reduce-scatter.26.cloned.1.call-update) | async-done | bytes 884752 | tf_op jit(solution)/shard_map/reduce_scatter | solution.py:309
  2248.0 11.2 fusion.279
  2261.9 42.7 %reduce-scatter.42.cloned.1.call-done = f32[48,2]{1,0:T(8,128)} async-done(((f32[768,2]{1,0:T(8,128)}), f32[48,2]{1,0:T(8,128)}) %reduce-scatter.42.cloned.1.call-update) | async-done | bytes 400
  2305.4 57.1 %reduce-scatter.40.cloned.1.call-done = f32[48,2]{1,0:T(8,128)} async-done(((f32[768,2]{1,0:T(8,128)}), f32[48,2]{1,0:T(8,128)}) %reduce-scatter.40.cloned.1.call-update) | async-done | bytes 400
  2364.9 56.2 %reduce-scatter.38.cloned.1.call-done = f32[48,2]{1,0:T(8,128)} async-done(((f32[768,2]{1,0:T(8,128)}), f32[48,2]{1,0:T(8,128)}) %reduce-scatter.38.cloned.1.call-update) | async-done | bytes 400
  2421.9 57.1 %reduce-scatter.36.cloned.1.call-done = f32[48,2]{1,0:T(8,128)} async-done(((f32[768,2]{1,0:T(8,128)}), f32[48,2]{1,0:T(8,128)}) %reduce-scatter.36.cloned.1.call-update) | async-done | bytes 400
  2479.9 57.7 %reduce-scatter.34.cloned.1.call-done = f32[48,2]{1,0:T(8,128)} async-done(((f32[768,2]{1,0:T(8,128)}), f32[48,2]{1,0:T(8,128)}) %reduce-scatter.34.cloned.1.call-update) | async-done | bytes 400
  2546.2 50.3 %all-reduce.5.cloned.1.call-done = (bf16[2,48,2304]{2,1,0:T(8,128)(2,1)}, bf16[2,48,768]{2,1,0:T(8,128)(2,1)}, bf16[2,48,3072]{2,1,0:T(8,128)(2,1)}, bf16[2,192,768]{2,1,0:T(8,128)(2,1)}) async-done(((bf16[2,48,2304]{2,1,0:T(8,128)(2,1)}, bf16[2,48,768]{2,1,0:T(8,128)(2,1)}, bf16[2,48,3072]{2,1,0:T(8,128)(2,1)}, bf16[2,192,768]{2,1,0:T(8,128)(2,1)}), (bf16[2,48,2304]{2,1,0:T(8,128)(2,1)}, ...) | async-done | bytes 1769488 | tf_op jit(solution)/shard_map/psum | solution.py:320
  (1094 shorter events, 1332.0 us)
Async XLA Ops:
  7.2 97.1 %all-gather.5.cloned.1.call-start = ((), (), s32[]{:S(2)}) async-start(), calls=%async_computation.17 | async-start | bytes 9437184 | tf_op jit(solution)/shard_map/all_gather | solution.py:204
  9.1 314.3 %copy-start.50 = (f32[768]{0:T(1024)}, f32[768]{0:T(1024)S(1)}, u32[]{:S(2)}) copy-start(f32[768]{0:T(1024)S(1)} %multiply_reduce_fusion.17) | copy-start | bytes 9220
  10.2 337.9 %copy-start.68 = (f32[768]{0:T(1024)}, f32[768]{0:T(1024)S(1)}, u32[]{:S(2)}) copy-start(f32[768]{0:T(1024)S(1)} %get-tuple-element.1332) | copy-start | bytes 9220
  10.2 337.9 %copy-start.97 = (f32[768]{0:T(1024)}, f32[768]{0:T(1024)S(1)}, u32[]{:S(2)}) copy-start(f32[768]{0:T(1024)S(1)} %get-tuple-element.1092) | copy-start | bytes 9220
  21.1 418.8 %all-gather.7.cloned.1.call-start = ((), (), s32[]{:S(2)}) async-start(), calls=%async_computation.18 | async-start | bytes 9437184 | tf_op jit(solution)/shard_map/all_gather | solution.py:204
  27.9 299.2 %copy-start.71 = (f32[768]{0:T(1024)}, f32[768]{0:T(1024)S(1)}, u32[]{:S(2)}) copy-start(f32[768]{0:T(1024)S(1)} %get-tuple-element.1333) | copy-start | bytes 9220
  27.9 299.2 %copy-start.99 = (f32[768]{0:T(1024)}, f32[768]{0:T(1024)S(1)}, u32[]{:S(2)}) copy-start(f32[768]{0:T(1024)S(1)} %get-tuple-element.1089) | copy-start | bytes 9220
  27.9 673.9 %copy-start.87 = (f32[1024]{0:T(1024)}, f32[1024]{0:T(1024)S(1)}, u32[]{:S(2)}) copy-start(f32[1024]{0:T(1024)S(1)} %get-tuple-element.1329) | copy-start | bytes 12292
  215.5 107.9 %copy-start.3 = (bf16[1,1,1024,768]{2,3,1,0:T(8,128)(2,1)S(1)}, bf16[1,1,1024,768]{2,3,1,0:T(8,128)(2,1)}, u32[]{:S(2)}) copy-start(bf16[1,1,1024,768]{2,3,1,0:T(8,128)(2,1)} %copy-done.2) | copy-start | bytes 4718596
  215.5 107.9 %copy-start.42 = (bf16[12,512,64]{1,2,0:T(8,128)(2,1)S(1)}, bf16[12,512,64]{1,2,0:T(8,128)(2,1)}, u32[]{:S(2)}) copy-start(bf16[12,512,64]{1,2,0:T(8,128)(2,1)} %copy-done.41) | copy-start | bytes 2359300
  359.3 784.0 %reduce-scatter.22.cloned.1.call-start = ((), (), s32[]{:S(2)}) async-start(), calls=%async_computation.11 | async-start | bytes 9437184 | tf_op jit(solution)/shard_map/reduce_scatter | solution.py:282
  659.3 25.8 slice-start
  663.6 38.2 %copy-start.5 = (f32[1024,768]{0,1:T(8,128)}, f32[1024,768]{0,1:T(8,128)S(1)}, u32[]{:S(2)}) copy-start(f32[1024,768]{0,1:T(8,128)S(1)} %get-tuple-element.1318) | copy-start | bytes 9437188
  663.7 38.1 %copy-start.60 = (f32[1024]{0:T(1024)}, f32[1024]{0:T(1024)S(1)}, u32[]{:S(2)}) copy-start(f32[1024]{0:T(1024)S(1)} %broadcast_multiply_fusion.9) | copy-start | bytes 12292
  664.1 37.7 %copy-start.82 = (f32[1024]{0:T(1024)}, f32[1024]{0:T(1024)S(1)}, u32[]{:S(2)}) copy-start(f32[1024]{0:T(1024)S(1)} %add_rsqrt_fusion) | copy-start | bytes 12292
  664.4 20.8 slice-start.1
  664.4 20.8 slice-start.2
  1066.1 554.2 %reduce-scatter.24.cloned.1.call-start = ((), (), s32[]{:S(2)}) async-start(), calls=%async_computation.12 | async-start | bytes 9437184 | tf_op jit(solution)/shard_map/reduce_scatter | solution.py:282
  1069.3 83.1 %copy-start.38 = (bf16[1024,768]{1,0:T(8,128)(2,1)}, bf16[1024,768]{1,0:T(8,128)(2,1)S(1)}, u32[]{:S(2)}) copy-start(bf16[1024,768]{1,0:T(8,128)(2,1)S(1)} %copy.268) | copy-start | bytes 4718596
  1159.9 18.8 slice-start.3
  1543.0 156.5 %reduce-scatter.28.cloned.1.call-start = ((), (), s32[]{:S(2)}) async-start(), calls=%async_computation.14 | async-start | bytes 5013504 | tf_op jit(solution)/shard_map/reduce_scatter | solution.py:310
  1551.0 347.0 %reduce-scatter.32.cloned.1.call-start = ((), (), s32[]{:S(2)}) async-start(), calls=%async_computation.16 | async-start | bytes 20054016 | tf_op jit(solution)/shard_map/reduce_scatter | solution.py:314
  1582.1 514.5 %reduce-scatter.30.cloned.1.call-start = ((), (), s32[]{:S(2)}) async-start(), calls=%async_computation.15 | async-start | bytes 20054016 | tf_op jit(solution)/shard_map/reduce_scatter | solution.py:313
  1606.0 640.0 %reduce-scatter.26.cloned.1.call-start = ((), (), s32[]{:S(2)}) async-start(), calls=%async_computation.13 | async-start | bytes 15040512 | tf_op jit(solution)/shard_map/reduce_scatter | solution.py:309
  1642.1 662.5 %reduce-scatter.42.cloned.1.call-start = ((), (), s32[]{:S(2)}) async-start(), calls=%async_computation.23 | async-start | bytes 417792
  1643.8 718.8 %reduce-scatter.40.cloned.1.call-start = ((), (), s32[]{:S(2)}) async-start(), calls=%async_computation.22 | async-start | bytes 417792
  1644.8 776.3 %reduce-scatter.38.cloned.1.call-start = ((), (), s32[]{:S(2)}) async-start(), calls=%async_computation.21 | async-start | bytes 417792
  1661.3 817.7 %reduce-scatter.36.cloned.1.call-start = ((), (), s32[]{:S(2)}) async-start(), calls=%async_computation.20 | async-start | bytes 417792
  1662.6 875.0 %reduce-scatter.34.cloned.1.call-start = ((), (), s32[]{:S(2)}) async-start(), calls=%async_computation.19 | async-start | bytes 417792
  1668.4 928.1 %all-reduce.5.cloned.1.call-start = ((), (), s32[]{:S(2)}) async-start(), calls=%async_computation.24 | async-start | bytes 3538944 | tf_op jit(solution)/shard_map/psum | solution.py:320
  1701.1 546.9 %copy-start.7 = (f32[1024,768]{0,1:T(8,128)S(1)}, f32[1024,768]{0,1:T(8,128)}, u32[]{:S(2)}) copy-start(f32[1024,768]{0,1:T(8,128)} %copy-done.5) | copy-start | bytes 9437188
  2259.2 104.1 %copy-start.30 = (bf16[1024,768]{0,1:T(8,128)(2,1)S(1)}, bf16[1024,768]{0,1:T(8,128)(2,1)}, u32[]{:S(2)}) copy-start(bf16[1024,768]{0,1:T(8,128)(2,1)} %get-tuple-element.1280) | copy-start | bytes 4718596
  (128 other events, 563.2 us)
Sparse Core Ops, SparseCore 0:
  21.2 83.0 all-gather.4
  359.4 80.3 all-gather.6
  1066.2 77.0 reduce-scatter.21
  1543.1 77.0 reduce-scatter.23
  1623.9 75.5 reduce-scatter.27
  1703.9 193.9 reduce-scatter.31
  1902.6 193.8 reduce-scatter.29
  2101.3 144.6 reduce-scatter.25
  2249.9 54.6 reduce-scatter.41
  2308.0 54.5 reduce-scatter.39
  2366.4 54.6 reduce-scatter.37
  2424.5 54.5 reduce-scatter.35
  2483.0 54.6 reduce-scatter.33
  2541.1 55.3 all-reduce.4
where the time goes:
time: 2630 us; the launch traced here: 2610 us
  waiting for transfers between devices  1100 us (42%)
  matrix products  922 us (35%)
  local copies, waits for them, and re-layouts  400 us (15%)
  other arithmetic  156 us (6%)
    unnamed x19, waiting for transfers between devices  271 us
    reduce_scatter x1, waiting for transfers between devices, local(): lax.psum_scatter(down_sum, 'rows', scatter_dimension=1, tiled=True)  197 us
    reduce_scatter x1, waiting for transfers between devices, local(): lax.psum_scatter(up_sum, 'rows', scatter_dimension=1, tiled=True)  196 us
    reduce_scatter x1, waiting for transfers between devices, local(): lax.psum_scatter(triple_sum, 'rows', scatter_dimension=1, tiled=True)  147 us
    dot_general x48, matrix products, head_backward(): jnp.einsum('qd,kd->qk', head_query, head_key, preferred_element_type=jnp....  140 us
    all_gather x2, waiting for transfers between devices, local(): lax.all_gather(triple[None, :, :, model_width:], 'pass', axis=0, tiled=True)  138 us
    dot_general x48, matrix products, head_forward(): jnp.einsum('qd,kd->qk', head_query, head_key, preferred_element_type=jnp....  119 us
    dot_general x48, matrix products, head_forward(): head_out = jnp.dot(softmax, head_value, preferred_element_type=jnp.float32)  116 us
  transfers between devices with their start and end apart: 14, of which 13 were waited for; matrix products, arithmetic and copies ran while one was open for 7% of the time, Pallas kernels for 0%

commit v1 on v0

v1 whole, which is shorter than its diff:
```python
import functools
import math

import jax
import jax.numpy as jnp
from jax import lax
from jax.experimental import pallas as pl
from jax.experimental.pallas import tpu as pltpu
from jax.sharding import PartitionSpec as P

HEAD_DIM = 64
EPSILON = 1e-05
SCALE = HEAD_DIM**-0.5
MESH = pl.DeviceIdType.MESH
NN = (((1,), (0,)), ((), ()))
NT = (((1,), (1,)), ((), ()))
TN = (((0,), (0,)), ((), ()))
BLOCK = 256
LANES = 128
BF16 = jnp.bfloat16
F32 = jnp.float32
VMEM_LIMIT = 60 * 2**20
ANY = pl.BlockSpec(memory_space=pl.ANY)


def dot(left, right, dims=NN):
    return lax.dot_general(left, right, dims, preferred_element_type=F32)


def sds(shape, dtype):
    return jax.ShapeDtypeStruct(shape, dtype)


def params(collective_id=None):
    return pltpu.CompilerParams(
        vmem_limit_bytes=VMEM_LIMIT,
        collective_id=collective_id,
        has_side_effects=collective_id is not None,
    )


def whole(shape):
    zeros = (0,) * len(shape)
    return pl.BlockSpec(shape, lambda *_: zeros, pipeline_mode=pl.Buffered(1))


def norm(hidden, gain, bias):
    centred = hidden - jnp.mean(hidden, -1, keepdims=True)
    inverse = lax.rsqrt(jnp.mean(centred * centred, -1, keepdims=True) + EPSILON)
    scaled = centred * inverse
    return (scaled * gain + bias).astype(BF16), scaled, inverse


def norm_back(grad, scaled, inverse, gain):
    e = grad * gain
    return inverse * (
        e - jnp.mean(e, -1, keepdims=True) - scaled * jnp.mean(e * scaled, -1, keepdims=True)
    )


def partner():
    rows = lax.axis_index("rows")
    return rows + 1 - 2 * (rows % 2)


def greet():
    barrier = pltpu.get_barrier_semaphore()
    pl.semaphore_signal(barrier, inc=1, device_id={"rows": partner()}, device_id_type=MESH)
    pl.semaphore_wait(barrier, 1)


def qkv_kernel(
    hidden_ref, embed_ref, gain_ref, bias_ref, weight_ref,
    full_ref, normed_ref, scaled_ref, inverse_ref, query_ref, kv_ref,
    held, local_sem, send_sem, recv_sem,
):
    step = pl.program_id(0)
    own = lax.axis_index("rows") % 2
    width = hidden_ref.shape[1]
    rows = hidden_ref.shape[0]

    @pl.when(step == 0)
    def _():
        greet()

    hidden = hidden_ref[...].astype(F32) + embed_ref[...]
    full_ref[...] = hidden
    normed, scaled, inverse = norm(hidden, gain_ref[...], bias_ref[...])
    normed_ref[...] = normed
    scaled_ref[...] = scaled.astype(BF16)
    inverse_ref[...] = inverse
    keys = dot(normed, weight_ref[:, width:])
    held[step] = keys.astype(BF16)

    def copies(i):
        there = pltpu.make_async_remote_copy(
            src_ref=held.at[i], dst_ref=kv_ref.at[i, own],
            send_sem=send_sem.at[i], recv_sem=recv_sem.at[i],
            device_id={"rows": partner()}, device_id_type=MESH,
        )
        here = pltpu.make_async_copy(held.at[i], kv_ref.at[i, own], local_sem.at[i])
        return there, here

    there, here = copies(step)
    there.start()
    here.start()
    queries = dot(normed, weight_ref[:, :width])
    query_ref[...] = (queries.astype(BF16).astype(F32) * SCALE).astype(BF16)

    @pl.when(step == pl.num_programs(0) - 1)
    def _():
        for i in range(held.shape[0]):
            there, here = copies(i)
            there.wait()
            here.wait()


def qkv(hidden, embed, gain, bias, weight, collective_id):
    tokens, width = hidden.shape
    steps = tokens // BLOCK
    tile = pl.BlockSpec((BLOCK, width), lambda i: (i, 0))
    return pl.pallas_call(
        qkv_kernel,
        grid=(steps,),
        in_specs=[tile, whole((1, width)), whole((1, width)), whole((1, width)), whole(weight.shape)],
        out_specs=[tile, tile, tile, pl.BlockSpec((BLOCK, 1), lambda i: (i, 0)), tile, ANY],
        out_shape=[
            sds((tokens, width), F32),
            sds((tokens, width), BF16),
            sds((tokens, width), BF16),
            sds((tokens, 1), F32),
            sds((tokens, width), BF16),
            sds((steps, 2, BLOCK, 2 * width), BF16),
        ],
        scratch_shapes=[
            pltpu.VMEM((steps, BLOCK, 2 * width), BF16),
            pltpu.SemaphoreType.DMA((steps,)),
            pltpu.SemaphoreType.DMA((steps,)),
            pltpu.SemaphoreType.DMA((steps,)),
        ],
        compiler_params=params(collective_id),
        name="qkv",
    )(hidden, embed, gain, bias, weight)


def tile_index(blocks, key_block, query_block):
    return key_block * blocks - key_block * (key_block - 1) // 2 + query_block - key_block


def attend_kernel(length_ref, query_ref, key_ref, value_ref, mixed_ref, total_ref, exp_ref):
    own = lax.axis_index("rows") % 2
    tokens = query_ref.shape[0]
    blocks = tokens // BLOCK
    pair = 2 * BLOCK
    lane = lax.broadcasted_iota(jnp.int32, (BLOCK, LANES), 1)
    query_at = lax.broadcasted_iota(jnp.int32, (BLOCK, pair), 0)
    column = lax.broadcasted_iota(jnp.int32, (BLOCK, pair), 1)
    key_pass = column // BLOCK
    key_at = column - key_pass * BLOCK
    causal = (key_at < query_at) | ((key_at == query_at) & (key_pass <= own))
    length = length_ref[0]
    ones = jnp.ones((tokens * 2, LANES), BF16)
    values = jnp.concatenate([value_ref[...], ones], 1)
    for block in range(blocks):
        rows = pl.ds(block * BLOCK, BLOCK)

        @pl.when(block * BLOCK < length)
        def _():
            allowed = causal & (key_at < length - block * BLOCK)
            query = query_ref[rows, :]
            outs = []
            for head in range(2):
                chosen = jnp.where(lane // HEAD_DIM == head, query, jnp.zeros_like(query))
                raw = dot(chosen, key_ref[: (block + 1) * pair, :], NT)
                last = jnp.where(allowed, raw[:, block * pair :], -jnp.inf)
                top = jnp.max(last, -1, keepdims=True)
                if block:
                    top = jnp.maximum(top, jnp.max(raw[:, : block * pair], -1, keepdims=True))
                parts = [jnp.exp(raw[:, k * pair : (k + 1) * pair] - top).astype(BF16) for k in range(block)]
                parts.append(jnp.exp(last - top).astype(BF16))
                for k, part in enumerate(parts):
                    exp_ref[head, tile_index(blocks, k, block)] = part
                mixed = dot(jnp.concatenate(parts, 1), values[: (block + 1) * pair])
                inverse = 1.0 / mixed[:, LANES : LANES + 1]
                total_ref[0, rows, head : head + 1] = inverse
                outs.append(mixed[:, :LANES] * inverse)
            mixed_ref[rows, :] = jnp.where(lane < HEAD_DIM, outs[0], outs[1]).astype(BF16)

        @pl.when(block * BLOCK >= length)
        def _():
            mixed_ref[rows, :] = jnp.zeros((BLOCK, LANES), BF16)
            total_ref[0, rows, :] = jnp.zeros((BLOCK, 2), F32)
            for head in range(2):
                for k in range(block + 1):
                    exp_ref[head, tile_index(blocks, k, block)] = jnp.zeros((BLOCK, pair), BF16)


def attend(length, query, kv):
    tokens, width = query.shape
    blocks = tokens // BLOCK
    tiles = blocks * (blocks + 1) // 2
    pairs = width // LANES
    column = pl.BlockSpec((tokens, LANES), lambda h: (0, h))
    return pl.pallas_call(
        attend_kernel,
        grid=(pairs,),
        in_specs=[
            pl.BlockSpec(memory_space=pltpu.SMEM),
            column,
            pl.BlockSpec((2 * tokens, LANES), lambda h: (0, h)),
            pl.BlockSpec((2 * tokens, LANES), lambda h: (0, h + pairs)),
        ],
        out_specs=[
            column,
            pl.BlockSpec((1, tokens, 2), lambda h: (h, 0, 0)),
            pl.BlockSpec((2, tiles, BLOCK, 2 * BLOCK), lambda h: (h, 0, 0, 0)),
        ],
        out_shape=[
            sds((tokens, width), BF16),
            sds((pairs, tokens, 2), F32),
            sds((2 * pairs, tiles, BLOCK, 2 * BLOCK), BF16),
        ],
        compiler_params=params(),
        name="attend",
    )(length, query, kv, kv)


def attend_back_kernel(
    query_ref, key_ref, value_ref, grad_ref, mixed_ref, total_ref, exp_ref,
    grad_query_ref, own_ref, recv_ref,
    query_sum, held, send_sem, recv_sem,
):
    step = pl.program_id(0)
    own = lax.axis_index("rows") % 2
    tokens = query_ref.shape[0]
    blocks = tokens // BLOCK
    pair = 2 * BLOCK
    lane = lax.broadcasted_iota(jnp.int32, (tokens, LANES), 1)

    @pl.when(step == 0)
    def _():
        greet()

    grad = grad_ref[...].astype(F32)
    product = grad * mixed_ref[...].astype(F32)
    query = query_ref[...]
    zero = jnp.zeros_like(query)
    sums = []
    for head in range(2):
        mine = lane // HEAD_DIM == head
        inverse = total_ref[0, :, head : head + 1]
        scaled = jnp.where(mine, grad * inverse, 0.0).astype(BF16)
        inner = jnp.sum(jnp.where(mine, product, 0.0), -1, keepdims=True) * inverse
        chosen = jnp.where(mine, query, zero)
        for block in range(blocks):
            first = block * BLOCK
            keys = pl.ds(block * pair, pair)
            start = tile_index(blocks, block, block)
            prob = exp_ref[head, start : start + blocks - block].reshape(tokens - first, pair)
            grad_prob = dot(scaled[first:], value_ref[keys, :], NT)
            score = (prob.astype(F32) * (grad_prob - inner[first:])).astype(BF16)
            grad_value = dot(prob, scaled[first:], TN)
            grad_key = dot(score, chosen[first:], TN)
            grad_query = dot(score, key_ref[keys, :])
            if block == 0:
                query_sum[head] = grad_query
            else:
                query_sum[head, first:, :] += grad_query
            sums.append((grad_key, grad_value))
    for block in range(blocks):
        for which in range(2):
            total = (sums[block][which] + sums[blocks + block][which]).astype(BF16)
            for p in range(2):
                held[step % 2, p, which, pl.ds(block * BLOCK, BLOCK), :] = total[p * BLOCK : (p + 1) * BLOCK]
    grad_query_ref[...] = (jnp.where(lane < HEAD_DIM, query_sum[0], query_sum[1]) * SCALE).astype(BF16)
    own_ref[0] = held[step % 2, own, 0]
    own_ref[1] = held[step % 2, own, 1]

    def copy(i):
        return pltpu.make_async_remote_copy(
            src_ref=held.at[i % 2, 1 - own], dst_ref=recv_ref.at[i],
            send_sem=send_sem.at[i], recv_sem=recv_sem.at[i],
            device_id={"rows": partner()}, device_id_type=MESH,
        )

    copy(step).start()

    @pl.when(step > 0)
    def _():
        copy(step - 1).wait_send()

    @pl.when(step == pl.num_programs(0) - 1)
    def _():
        copy(step).wait_send()
        for i in range(recv_ref.shape[0]):
            copy(i).wait_recv()


def attend_back(query, kv, grad_mixed, mixed, total, exps, collective_id):
    tokens, width = query.shape
    pairs = width // LANES
    tiles = exps.shape[1]
    column = pl.BlockSpec((tokens, LANES), lambda h: (0, h))
    return pl.pallas_call(
        attend_back_kernel,
        grid=(pairs,),
        in_specs=[
            column,
            pl.BlockSpec((2 * tokens, LANES), lambda h: (0, h)),
            pl.BlockSpec((2 * tokens, LANES), lambda h: (0, h + pairs)),
            column,
            column,
            pl.BlockSpec((1, tokens, 2), lambda h: (h, 0, 0)),
            pl.BlockSpec((2, tiles, BLOCK, 2 * BLOCK), lambda h: (h, 0, 0, 0)),
        ],
        out_specs=[column, pl.BlockSpec((2, tokens, LANES), lambda h: (0, 0, h)), ANY],
        out_shape=[
            sds((tokens, width), BF16),
            sds((2, tokens, width), BF16),
            sds((pairs, 2, tokens, LANES), BF16),
        ],
        scratch_shapes=[
            pltpu.VMEM((2, tokens, LANES), F32),
            pltpu.VMEM((2, 2, 2, tokens, LANES), BF16),
            pltpu.SemaphoreType.DMA((pairs,)),
            pltpu.SemaphoreType.DMA((pairs,)),
        ],
        compiler_params=params(collective_id),
        name="attend_back",
    )(query, kv, kv, grad_mixed, mixed, total, exps)


def gelu_both(v):
    root = math.sqrt(2.0 / math.pi)
    square = v * v
    t = jnp.tanh(v * (root + (root * 0.044715) * square))
    half = 0.5 * (1.0 + t)
    slope = half + 0.5 * v * (1.0 - t * t) * (root + (3.0 * root * 0.044715) * square)
    return v * half, slope


def ffn_kernel(
    hidden_ref, mixed_ref, merge_ref, gain_ref, bias_ref, up_ref, down_ref,
    next_ref, normed_ref, scaled_ref, inverse_ref, act_ref, slope_ref,
):
    mid = hidden_ref[...] + dot(mixed_ref[...], merge_ref[...])
    normed, scaled, inverse = norm(mid, gain_ref[...], bias_ref[...])
    normed_ref[...] = normed
    scaled_ref[...] = scaled.astype(BF16)
    inverse_ref[...] = inverse
    total = mid
    hidden_units = up_ref.shape[1]
    part = mid.shape[1]
    for first in range(0, hidden_units, part):
        act, slope = gelu_both(dot(normed, up_ref[:, first : first + part]))
        act = act.astype(BF16)
        act_ref[:, first : first + part] = act
        slope_ref[:, first : first + part] = slope.astype(BF16)
        total = total + dot(act, down_ref[first : first + part, :])
    next_ref[...] = total


def ffn(hidden, mixed, merge, gain, bias, up, down):
    tokens, width = hidden.shape
    units = up.shape[1]
    tile = pl.BlockSpec((BLOCK, width), lambda i: (i, 0))
    wide = pl.BlockSpec((BLOCK, units), lambda i: (i, 0))
    return pl.pallas_call(
        ffn_kernel,
        grid=(tokens // BLOCK,),
        in_specs=[
            tile, tile, whole(merge.shape), whole((1, width)), whole((1, width)),
            whole(up.shape), whole(down.shape),
        ],
        out_specs=[tile, tile, tile, pl.BlockSpec((BLOCK, 1), lambda i: (i, 0)), wide, wide],
        out_shape=[
            sds((tokens, width), F32),
            sds((tokens, width), BF16),
            sds((tokens, width), BF16),
            sds((tokens, 1), F32),
            sds((tokens, units), BF16),
            sds((tokens, units), BF16),
        ],
        compiler_params=params(),
        name="ffn",
    )(hidden, mixed, merge, gain, bias, up, down)


def ffn_back_kernel(
    grad_ref, act_ref, slope_ref, normed_ref, scaled_ref, inverse_ref, mixed_ref,
    gain_ref, up_ref, down_ref, merge_ref,
    down_grad_ref, up_grad_ref, merge_grad_ref, mid_ref, grad_mixed_ref, small_ref,
    total, low, branch,
):
    step = pl.program_id(0)
    tokens = grad_ref.shape[0]

    @pl.when(step == 0)
    def _():
        low[...] = grad_ref[...].astype(BF16)
        total[...] = jnp.zeros_like(total)

    grad_low = low[...]
    down_grad_ref[...] = dot(act_ref[...], grad_low, TN).astype(BF16)
    grad_act = dot(grad_low, down_ref[...], NT)
    grad_pre = (slope_ref[...].astype(F32) * grad_act).astype(BF16)
    up_grad_ref[...] = dot(normed_ref[...], grad_pre, TN).astype(BF16)
    total[...] += dot(grad_pre, up_ref[...], NT)

    @pl.when(step == pl.num_programs(0) - 1)
    def _():
        def rows(i, sums):
            at = pl.ds(pl.multiple_of(i * BLOCK, BLOCK), BLOCK)
            grad = total[at, :]
            scaled = scaled_ref[at, :].astype(F32)
            mid = grad_ref[at, :] + norm_back(grad, scaled, inverse_ref[at, :], gain_ref[...])
            mid_ref[at, :] = mid
            low_mid = mid.astype(BF16)
            branch[at, :] = low_mid
            grad_mixed_ref[at, :] = dot(low_mid, merge_ref[...], NT).astype(BF16)
            return (
                sums[0] + jnp.sum(grad * scaled, 0, keepdims=True),
                sums[1] + jnp.sum(grad, 0, keepdims=True),
            )

        empty = jnp.zeros((1, grad_ref.shape[1]), F32)
        gain_sum, bias_sum = lax.fori_loop(0, tokens // BLOCK, rows, (empty, empty))
        small_ref[0:1, :] = gain_sum
        small_ref[1:2, :] = bias_sum
        merge_grad_ref[...] = dot(mixed_ref[...], branch[...], TN).astype(BF16)


def ffn_back(grad, act, slope, normed, scaled, inverse, mixed, gain, up, down, merge):
    tokens, width = grad.shape
    units = up.shape[1]
    part = 512
    full = whole((tokens, width))
    return pl.pallas_call(
        ffn_back_kernel,
        grid=(units // part,),
        in_specs=[
            full,
            pl.BlockSpec((tokens, part), lambda i: (0, i)),
            pl.BlockSpec((tokens, part), lambda i: (0, i)),
            full, full, whole((tokens, 1)), full, whole((1, width)),
            pl.BlockSpec((width, part), lambda i: (0, i)),
            pl.BlockSpec((part, width), lambda i: (i, 0)),
            whole(merge.shape),
        ],
        out_specs=[
            pl.BlockSpec((part, width), lambda i: (i, 0)),
            pl.BlockSpec((width, part), lambda i: (0, i)),
            whole(merge.shape), full, full, whole((2, width)),
        ],
        out_shape=[
            sds(down.shape, BF16),
            sds(up.shape, BF16),
            sds(merge.shape, BF16),
            sds((tokens, width), F32),
            sds((tokens, width), BF16),
            sds((2, width), F32),
        ],
        scratch_shapes=[
            pltpu.VMEM((tokens, width), F32),
            pltpu.VMEM((tokens, width), BF16),
            pltpu.VMEM((tokens, width), BF16),
        ],
        compiler_params=params(),
        name="ffn_back",
    )(grad, act, slope, normed, scaled, inverse, mixed, gain, up, down, merge)


def qkv_back_kernel(
    grad_query_ref, own_ref, recv_ref, normed_ref, scaled_ref, inverse_ref, mid_ref, gain_ref, weight_ref,
    weight_grad_ref, hidden_ref, small_ref,
    total, grads,
):
    step = pl.program_id(0)
    tokens, width = mid_ref.shape

    @pl.when(step == 0)
    def _():
        grads[...] = grad_query_ref[...]
        total[...] = jnp.zeros_like(total)

    @pl.when(step > 0)
    def _():
        for pair in range(width // LANES):
            lanes = slice(pair * LANES, (pair + 1) * LANES)
            grads[:, lanes] = (
                own_ref[0, :, lanes].astype(F32) + recv_ref[pair, 0].astype(F32)
            ).astype(BF16)

    weight_grad_ref[...] = dot(normed_ref[...], grads[...], TN).astype(BF16)
    total[...] += dot(grads[...], weight_ref[...], NT)

    @pl.when(step == pl.num_programs(0) - 1)
    def _():
        def rows(i, sums):
            at = pl.ds(pl.multiple_of(i * BLOCK, BLOCK), BLOCK)
            grad = total[at, :]
            scaled = scaled_ref[at, :].astype(F32)
            hidden = mid_ref[at, :] + norm_back(grad, scaled, inverse_ref[at, :], gain_ref[...])
            hidden_ref[at, :] = hidden
            return (
                sums[0] + jnp.sum(grad * scaled, 0, keepdims=True),
                sums[1] + jnp.sum(grad, 0, keepdims=True),
                sums[2] + jnp.sum(hidden, 0, keepdims=True),
            )

        empty = jnp.zeros((1, width), F32)
        sums = lax.fori_loop(0, tokens // BLOCK, rows, (empty, empty, empty))
        for i in range(3):
            small_ref[i : i + 1, :] = sums[i]


def qkv_back(grad_query, own, recv, normed, scaled, inverse, mid, gain, weight):
    tokens, width = mid.shape
    pairs = width // LANES
    full = whole((tokens, width))
    which = lambda i: jnp.maximum(i - 1, 0)
    return pl.pallas_call(
        qkv_back_kernel,
        grid=(3,),
        in_specs=[
            full,
            pl.BlockSpec((1, tokens, width), lambda i: (which(i), 0, 0)),
            pl.BlockSpec((pairs, 1, tokens, LANES), lambda i: (0, which(i), 0, 0)),
            full, full, whole((tokens, 1)), full, whole((1, width)),
            pl.BlockSpec((width, width), lambda i: (0, i)),
        ],
        out_specs=[pl.BlockSpec((width, width), lambda i: (0, i)), full, whole((3, width))],
        out_shape=[sds(weight.shape, BF16), sds((tokens, width), F32), sds((3, width), F32)],
        scratch_shapes=[pltpu.VMEM((tokens, width), F32), pltpu.VMEM((tokens, width), BF16)],
        compiler_params=params(),
        name="qkv_back",
    )(grad_query, own, recv, normed, scaled, inverse, mid, gain, weight)


def local(
    stream, lengths, pass_embed, first_gain, first_bias, triple_weight, merge_weight,
    second_gain, second_bias, up_weight, down_weight, cotangent,
):
    row_count = lax.axis_size("rows")
    own_row = lax.axis_index("rows")
    core = own_row % 2
    tokens, width = stream.shape[2], stream.shape[3]
    layers = triple_weight.shape[0]

    def holder(p, r):
        return p * row_count + r if p == r % 2 else (1 - p) * row_count + (r ^ 1)

    swaps = [(p * row_count + r, holder(p, r)) for p in range(2) for r in range(row_count)]

    def swap(x):
        return lax.ppermute(x, ("pass", "rows"), swaps)

    valid = (jnp.arange(tokens) < lengths[0]).astype(F32)[:, None]
    hidden = swap(stream.reshape(tokens, width))
    length = swap(lengths)
    grad_hidden = swap((cotangent.reshape(tokens, width).astype(F32) * valid).astype(BF16))
    embed = jnp.where(core == 0, pass_embed[0:1], pass_embed[1:2]).astype(F32)
    nothing = jnp.zeros_like(embed)

    def vector(array, depth):
        return array[depth : depth + 1].astype(F32)

    kept = []
    for depth in range(layers):
        hidden, normed, scaled, inverse, query, kv = qkv(
            hidden, nothing if depth else embed, vector(first_gain, depth), vector(first_bias, depth),
            triple_weight[depth], depth,
        )
        kv = kv.reshape(2 * tokens, 2 * width)
        mixed, total, exps = attend(length, query, kv)
        hidden, normed_two, scaled_two, inverse_two, act, slope = ffn(
            hidden, mixed, merge_weight[depth], vector(second_gain, depth), vector(second_bias, depth),
            up_weight[depth], down_weight[depth],
        )
        kept.append(
            (normed, scaled, inverse, query, kv, mixed, total, exps, normed_two, scaled_two, inverse_two, act, slope)
        )
    output = (swap(hidden.astype(BF16)).astype(F32) * valid).astype(BF16).reshape(stream.shape)

    grad_hidden = grad_hidden.astype(F32)
    grads = [None] * layers
    smalls = [None] * layers
    for depth in reversed(range(layers)):
        (normed, scaled, inverse, query, kv, mixed, total, exps, normed_two, scaled_two, inverse_two, act, slope) = kept[depth]
        down_grad, up_grad, merge_grad, mid, grad_mixed, small_two = ffn_back(
            grad_hidden, act, slope, normed_two, scaled_two, inverse_two, mixed, vector(second_gain, depth),
            up_weight[depth], down_weight[depth], merge_weight[depth],
        )
        grad_query, own, recv = attend_back(
            query, kv, grad_mixed, mixed, total, exps, layers + depth
        )
        triple_grad, grad_hidden, small_one = qkv_back(
            grad_query, own, recv, normed, scaled, inverse, mid, vector(first_gain, depth), triple_weight[depth],
        )
        grads[depth] = (triple_grad, merge_grad, up_grad, down_grad)
        smalls[depth] = jnp.concatenate([small_one[:2], small_two], 0)
    input_grad = swap(grad_hidden.astype(BF16)).reshape(stream.shape)

    def reduce(per_layer):
        shares = [
            lax.psum_scatter(g, "rows", scatter_dimension=0, tiled=True) for g in per_layer
        ]
        return lax.psum(jnp.stack(shares), "pass").astype(F32)

    weight_grads = [reduce([grads[depth][i] for depth in range(layers)]) for i in range(4)]
    hidden_sum = small_one[2:3]
    pass_rows = jnp.where(jnp.arange(2)[:, None] == core, hidden_sum, 0.0)
    small = jnp.concatenate([pass_rows, *smalls], 0)
    small = lax.psum(small, ("pass", "rows"))
    share = width // row_count
    small = lax.dynamic_slice_in_dim(small, own_row * share, share, 1)
    pass_grad = small[:2]
    by_layer = small[2:].reshape(layers, 4, share)
    return (
        output, input_grad, pass_grad, by_layer[:, 0], by_layer[:, 1], weight_grads[0], weight_grads[1],
        by_layer[:, 2], by_layer[:, 3], weight_grads[2], weight_grads[3],
    )


def solution(mesh):
    token = P("pass", "rows", None, None)
    matrix = P(None, "rows", None)
    rows = P(None, "rows")
    in_specs = (token, P("rows")) + (P(),) * 9 + (token,)
    out_specs = (token, token, rows, rows, rows, matrix, matrix, rows, rows, matrix, matrix)
    return jax.shard_map(local, mesh=mesh, in_specs=in_specs, out_specs=out_specs, check_vma=False)
```

time: 2630 us -> 995 us (0.38)
  matrix products: 922 us -> 0 us
  waiting for transfers between devices: 1100 us -> 472 us
  local copies, waits for them, and re-layouts: 400 us -> 27 us
  Pallas kernels: 0 us -> 362 us
  other arithmetic: 156 us -> 23.3 us
  blocking collectives: 4.93 us -> 71.1 us
    dot_general x360 -> x0, matrix products: 922 us -> none  [the longest x48 140 us: head_backward(): jnp.einsum('qd,kd->qk', head_query, head_key, preferred_element_type=jnp....]
    pallas_call x0 -> x12, Pallas kernels: none -> 362 us  [the longest x2 127 us: attend_back(): pl.pallas_call(attend_back_kernel, grid=(pairs,), in_specs=[column, pl.Bl...]
    unnamed x19 -> x9, waiting for transfers between devices: 271 us -> 3.2 us
    reduce_scatter x6 -> x8, waiting for transfers between devices: 646 us -> 468 us  [reduce(): lax.psum_scatter(g, 'rows', scatter_dimension=0, tiled=True)]
    all_gather x2 -> x0, waiting for transfers between devices: 138 us -> none  [local(): lax.all_gather(triple[None, :, :, model_width:], 'pass', axis=0, tiled=True)]
    concatenate x15 -> x1, local copies, waits for them, and re-layouts: 97 us -> 0.04 us  [local(): small = jnp.concatenate([pass_rows, *smalls], 0)]
    unnamed x275 -> x27, local copies, waits for them, and re-layouts: 89.8 us -> 2.23 us
    psum x1, blocking collectives: 4.93 us -> 71.1 us  [local(): small = lax.psum(small, ('pass', 'rows'))]
  transfers between devices with their start and end apart: 14 -> 14, of which waited for: 13 -> 7; matrix products, arithmetic and copies ran while one was open for 7% -> 3% of each run, Pallas kernels for 0% -> 21%
where the time goes in v1:
time: 995 us; the launch traced here: 990 us
  waiting for transfers between devices  472 us (47%)
  Pallas kernels  362 us (36%)
  blocking collectives  71.1 us (7%)
  local copies, waits for them, and re-layouts  27 us (3%)
  other arithmetic  23.3 us (2%)
  starting transfers between devices  19.7 us (2%)
  between operations  15 us (2%)
    reduce_scatter x8, waiting for transfers between devices, reduce(): lax.psum_scatter(g, 'rows', scatter_dimension=0, tiled=True)  468 us
    pallas_call x2, Pallas kernels, attend_back(): pl.pallas_call(attend_back_kernel, grid=(pairs,), in_specs=[column, pl.Bl...  127 us
    psum x1, blocking collectives, local(): small = lax.psum(small, ('pass', 'rows'))  71.1 us
    pallas_call x2, Pallas kernels, ffn_back(): pl.pallas_call(ffn_back_kernel, grid=(units // part,), in_specs=[full, pl...  69.2 us
    pallas_call x2, Pallas kernels, attend(): pl.pallas_call(attend_kernel, grid=(pairs,), in_specs=[pl.BlockSpec(memor...  58.7 us
    pallas_call x2, Pallas kernels, ffn(): pl.pallas_call(ffn_kernel, grid=(tokens // BLOCK,), in_specs=[tile, tile,...  45.4 us
    pallas_call x2, Pallas kernels, qkv_back(): pl.pallas_call(qkv_back_kernel, grid=(3,), in_specs=[full, pl.BlockSpec((...  35.9 us
    pallas_call x2, Pallas kernels, qkv(): pl.pallas_call(qkv_kernel, grid=(steps,), in_specs=[tile, whole((1, width...  25.4 us
  transfers between devices with their start and end apart: 14, of which 7 were waited for; matrix products, arithmetic and copies ran while one was open for 3% of the time, Pallas kernels for 21%

profile of v1, /device:TPU:0, one launch (start us, length us, event | category | flops | bytes accessed | tf_op | source)
XLA Modules:
  0.0 989.7 jit_solution(4049365655036430094)
XLA Ops:
  7.2 13.3 %collective-permute-start = (bf16[1024,768]{1,0:T(8,128)(2,1)}, bf16[1024,768]{1,0:T(8,128)(2,1)}, u32[]{:S(2)}, u32[]{:S(2)}) collective-permute-start(bf16[1024,768]{1,0:T(8,128)(2,1)} %bitcast.70), channel_id=1, source_target_pairs={{0,0},{1,16},{2,2},{3,18},{4,4},{5,20},{6,6},{7,22},{8,8},{9,24},{... | collective-permute-start | bytes 4718600 | tf_op jit(solution)/shard_map/ppermute | solution.py:556
  22.4 7.3 slice_bitcast_fusion.4
  30.7 4.4 slice_bitcast_fusion.1
  36.9 3.2 slice_bitcast_fusion.6
  40.1 8.0 slice_bitcast_fusion
  48.1 12.6 %qkv.2 = (f32[1024,768]{1,0:T(8,128)}, bf16[1024,768]{1,0:T(8,128)(2,1)}, bf16[1024,768]{1,0:T(8,128)(2,1)}, f32[1024,1]{1,0:T(8,128)}, bf16[1024,768]{1,0:T(8,128)(2,1)}, /*index=5*/bf16[4,2,256,1536]{3,2,1,0:T(8,128)(2,1)}) custom-call(bf16[1024,768]{1,0:T(8,128)(2,1)} %collective-permute-done.hidden_ref, f32[1,768]{1,0:T(1,128)} %get-tuple-element.145.embed_ref, ...), custom_call_target="tpu_custom_call" | custom-call | tf_op jit(solution)/shard_map/qkv/pallas_call | solution.py:122
  60.7 29.4 %attend.2 = (bf16[1024,768]{1,0:T(8,128)(2,1)}, f32[6,1024,2]{2,1,0:T(8,128)}, bf16[12,10,256,512]{3,2,1,0:T(8,128)(2,1)}) custom-call(s32[1]{0:T(128)} %collective-permute-done.1.length_ref, bf16[1024,768]{1,0:T(8,128)(2,1)} %get-tuple-element.66.query_ref, bf16[2048,1536]{1,0:T(8,128)(2,1)} %bitcast.48, bf16[2048,1536]{1,0:T(8,128)(2,1)} %bitcast.49), custom_call_target="tpu_custom_call" | custom-call | tf_op jit(solution)/shard_map/attend/pallas_call | solution.py:204
  90.1 22.7 %ffn.2 = (f32[1024,768]{1,0:T(8,128)}, bf16[1024,768]{1,0:T(8,128)(2,1)}, bf16[1024,768]{1,0:T(8,128)(2,1)}, f32[1024,1]{1,0:T(8,128)}, bf16[1024,3072]{1,0:T(8,128)(2,1)}, /*index=5*/bf16[1024,3072]{1,0:T(8,128)(2,1)}) custom-call(f32[1024,768]{1,0:T(8,128)} %get-tuple-element.65.hidden_ref, bf16[1024,768]{1,0:T(8,128)(2,1)} %get-tuple-element.68.mixed_ref, ...), custom_call_target="tpu_custom_call" | custom-call | tf_op jit(solution)/shard_map/ffn/pallas_call | solution.py:368
  113.4 12.9 %qkv.3 = (f32[1024,768]{1,0:T(8,128)}, bf16[1024,768]{1,0:T(8,128)(2,1)}, bf16[1024,768]{1,0:T(8,128)(2,1)}, f32[1024,1]{1,0:T(8,128)}, bf16[1024,768]{1,0:T(8,128)(2,1)}, /*index=5*/bf16[4,2,256,1536]{3,2,1,0:T(8,128)(2,1)}) custom-call(f32[1024,768]{1,0:T(8,128)} %get-tuple-element.69.hidden_ref, f32[1,768]{1,0:T(1,128)} %broadcast_in_dim.27.embed_ref, ...), custom_call_target="tpu_custom_call" | custom-call | tf_op jit(solution)/shard_map/qkv/pallas_call | solution.py:122
  126.2 29.3 %attend.3 = (bf16[1024,768]{1,0:T(8,128)(2,1)}, f32[6,1024,2]{2,1,0:T(8,128)}, bf16[12,10,256,512]{3,2,1,0:T(8,128)(2,1)}) custom-call(s32[1]{0:T(128)} %collective-permute-done.1.length_ref, bf16[1024,768]{1,0:T(8,128)(2,1)} %get-tuple-element.71.query_ref, bf16[2048,1536]{1,0:T(8,128)(2,1)} %bitcast.52, bf16[2048,1536]{1,0:T(8,128)(2,1)} %bitcast.53), custom_call_target="tpu_custom_call" | custom-call | tf_op jit(solution)/shard_map/attend/pallas_call | solution.py:204
  155.5 22.7 %ffn.3 = (f32[1024,768]{1,0:T(8,128)}, bf16[1024,768]{1,0:T(8,128)(2,1)}, bf16[1024,768]{1,0:T(8,128)(2,1)}, f32[1024,1]{1,0:T(8,128)}, bf16[1024,3072]{1,0:T(8,128)(2,1)}, /*index=5*/bf16[1024,3072]{1,0:T(8,128)(2,1)}) custom-call(f32[1024,768]{1,0:T(8,128)} %get-tuple-element.70.hidden_ref, bf16[1024,768]{1,0:T(8,128)(2,1)} %get-tuple-element.73.mixed_ref, ...), custom_call_target="tpu_custom_call" | custom-call | tf_op jit(solution)/shard_map/ffn/pallas_call | solution.py:368
  178.3 2.2 convert_element_type.83
  184.8 2.0 convert_element_type.90.grad_ref
  186.8 34.5 %ffn_back.2 = (bf16[3072,768]{1,0:T(8,128)(2,1)}, bf16[768,3072]{1,0:T(8,128)(2,1)}, bf16[768,768]{1,0:T(8,128)(2,1)}, f32[1024,768]{1,0:T(8,128)}, bf16[1024,768]{1,0:T(8,128)(2,1)}, /*index=5*/f32[2,768]{1,0:T(2,128)}) custom-call(f32[1024,768]{1,0:T(8,128)} %convert_element_type.90.grad_ref, bf16[1024,3072]{1,0:T(8,128)(2,1)} %get-tuple-element.75.act_ref, ...), custom_call_target="tpu_custom_call" | custom-call | tf_op jit(solution)/shard_map/ffn_back/pallas_call | solution.py:438
  221.5 83.9 %attend_back.2 = (bf16[1024,768]{1,0:T(8,128)(2,1)}, bf16[2,1024,768]{2,1,0:T(8,128)(2,1)}, bf16[6,2,1024,128]{3,2,1,0:T(8,128)(2,1)}) custom-call(bf16[1024,768]{1,0:T(8,128)(2,1)} %get-tuple-element.71.query_ref, bf16[2048,1536]{1,0:T(8,128)(2,1)} %bitcast.54, bf16[2048,1536]{1,0:T(8,128)(2,1)} %bitcast.55, bf16[1024,768]{1,0:T(8,128)(2,1)} %get-tuple-element.80.grad_ref, ...), custom_call_target="tpu_custom_call" | custom-call | tf_op jit(solution)/shard_map/attend_back/pallas_call | solution.py:304
  305.4 18.0 %qkv_back.2 = (bf16[768,2304]{1,0:T(8,128)(2,1)}, f32[1024,768]{1,0:T(8,128)}, f32[3,768]{1,0:T(4,128)}) custom-call(bf16[1024,768]{1,0:T(8,128)(2,1)} %get-tuple-element.83.grad_query_ref, bf16[2,1024,768]{2,1,0:T(8,128)(2,1)} %get-tuple-element.84.own_ref, bf16[6,2,1024,128]{3,2,1,0:T(8,128)(2,1)} %get-tuple-element.85.recv_ref, ...), custom_call_target="tpu_custom_call" | custom-call | tf_op jit(solution)/shard_map/qkv_back/pallas_call | solution.py:522
  323.5 34.7 %ffn_back.3 = (bf16[3072,768]{1,0:T(8,128)(2,1)}, bf16[768,3072]{1,0:T(8,128)(2,1)}, bf16[768,768]{1,0:T(8,128)(2,1)}, f32[1024,768]{1,0:T(8,128)}, bf16[1024,768]{1,0:T(8,128)(2,1)}, /*index=5*/f32[2,768]{1,0:T(2,128)}) custom-call(f32[1024,768]{1,0:T(8,128)} %get-tuple-element.90.grad_ref, bf16[1024,3072]{1,0:T(8,128)(2,1)} %get-tuple-element.91.act_ref, ...), custom_call_target="tpu_custom_call" | custom-call | tf_op jit(solution)/shard_map/ffn_back/pallas_call | solution.py:438
  359.0 43.4 %attend_back.3 = (bf16[1024,768]{1,0:T(8,128)(2,1)}, bf16[2,1024,768]{2,1,0:T(8,128)(2,1)}, bf16[6,2,1024,128]{3,2,1,0:T(8,128)(2,1)}) custom-call(bf16[1024,768]{1,0:T(8,128)(2,1)} %get-tuple-element.66.query_ref, bf16[2048,1536]{1,0:T(8,128)(2,1)} %bitcast.50, bf16[2048,1536]{1,0:T(8,128)(2,1)} %bitcast.51, bf16[1024,768]{1,0:T(8,128)(2,1)} %get-tuple-element.96.grad_ref, ...), custom_call_target="tpu_custom_call" | custom-call | tf_op jit(solution)/shard_map/attend_back/pallas_call | solution.py:304
  402.4 17.9 %qkv_back.3 = (bf16[768,2304]{1,0:T(8,128)(2,1)}, f32[1024,768]{1,0:T(8,128)}, f32[3,768]{1,0:T(4,128)}) custom-call(bf16[1024,768]{1,0:T(8,128)(2,1)} %get-tuple-element.99.grad_query_ref, bf16[2,1024,768]{2,1,0:T(8,128)(2,1)} %get-tuple-element.100.own_ref, bf16[6,2,1024,128]{3,2,1,0:T(8,128)(2,1)} %get-tuple-element.101.recv_ref, ...), custom_call_target="tpu_custom_call" | custom-call | tf_op jit(solution)/shard_map/qkv_back/pallas_call | solution.py:522
  423.1 17.5 %reduce-scatter.13.cloned.1.call-done = bf16[48,768]{1,0:T(8,128)(2,1)} async-done(((bf16[768,768]{1,0:T(8,128)(2,1)}), bf16[48,768]{1,0:T(8,128)(2,1)}) %reduce-scatter.13.cloned.1.call-update) | async-done | bytes 73744 | tf_op jit(solution)/shard_map/reduce_scatter | solution.py:606
  442.2 69.4 %reduce-scatter.11.cloned.1.call-done = bf16[48,2304]{1,0:T(8,128)(2,1)} async-done(((bf16[768,2304]{1,0:T(8,128)(2,1)}), bf16[48,2304]{1,0:T(8,128)(2,1)}) %reduce-scatter.11.cloned.1.call-update) | async-done | bytes 221200 | tf_op jit(solution)/shard_map/reduce_scatter | solution.py:606
  511.5 70.7 %reduce-scatter.9.cloned.1.call-done = bf16[48,2304]{1,0:T(8,128)(2,1)} async-done(((bf16[768,2304]{1,0:T(8,128)(2,1)}), bf16[48,2304]{1,0:T(8,128)(2,1)}) %reduce-scatter.9.cloned.1.call-update) | async-done | bytes 221200 | tf_op jit(solution)/shard_map/reduce_scatter | solution.py:606
  584.1 76.3 %reduce-scatter.19.cloned.1.call-done = bf16[48,3072]{1,0:T(8,128)(2,1)} async-done(((bf16[768,3072]{1,0:T(8,128)(2,1)}), bf16[48,3072]{1,0:T(8,128)(2,1)}) %reduce-scatter.19.cloned.1.call-update) | async-done | bytes 294928 | tf_op jit(solution)/shard_map/reduce_scatter | solution.py:606
  660.4 78.9 %reduce-scatter.17.cloned.1.call-done = bf16[48,3072]{1,0:T(8,128)(2,1)} async-done(((bf16[768,3072]{1,0:T(8,128)(2,1)}), bf16[48,3072]{1,0:T(8,128)(2,1)}) %reduce-scatter.17.cloned.1.call-update) | async-done | bytes 294928 | tf_op jit(solution)/shard_map/reduce_scatter | solution.py:606
  739.3 1.9 pad_maximum_fusion
  741.2 76.6 %reduce-scatter.23.cloned.1.call-done = bf16[192,768]{1,0:T(8,128)(2,1)} async-done(((bf16[3072,768]{1,0:T(8,128)(2,1)}), bf16[192,768]{1,0:T(8,128)(2,1)}) %reduce-scatter.23.cloned.1.call-update) | async-done | bytes 294928 | tf_op jit(solution)/shard_map/reduce_scatter | solution.py:606
  817.9 79.0 %reduce-scatter.21.cloned.1.call-done = bf16[192,768]{1,0:T(8,128)(2,1)} async-done(((bf16[3072,768]{1,0:T(8,128)(2,1)}), bf16[192,768]{1,0:T(8,128)(2,1)}) %reduce-scatter.21.cloned.1.call-update) | async-done | bytes 294928 | tf_op jit(solution)/shard_map/reduce_scatter | solution.py:606
  896.9 1.9 pad_maximum_fusion.1
  900.1 2.1 collective-permute-start.4
  902.4 71.1 %psum.35 = f32[10,768]{1,0:T(8,128)S(1)} all-reduce(f32[10,768]{1,0:T(8,128)S(1)} %concatenate.3), channel_id=1, replica_groups=mesh['pass'=2,'rows'=16] {'pass','rows'}, use_global_device_ids=true, to_apply=%region_0.1 | all-reduce | flops 7680 | bytes 61440 | tf_op jit(solution)/shard_map/psum | solution.py:614
  974.8 2.0 convert_element_type.92
  978.5 2.2 convert_element_type.94
  (75 shorter events, 22.8 us)
Async XLA Ops:
  7.2 415.9 %reduce-scatter.15.cloned.1.call-start = ((), (), s32[]{:S(2)}) async-start(), calls=%async_computation.11 | async-start | bytes 1253376 | tf_op jit(solution)/shard_map/reduce_scatter | solution.py:606
  7.2 40.9 %collective-permute-start = (bf16[1024,768]{1,0:T(8,128)(2,1)}, bf16[1024,768]{1,0:T(8,128)(2,1)}, u32[]{:S(2)}, u32[]{:S(2)}) collective-permute-start(bf16[1024,768]{1,0:T(8,128)(2,1)} %bitcast.70), channel_id=1, source_target_pairs={{0,0},{1,16},{2,2},{3,18},{4,4},{5,20},{6,6},{7,22},{8,8},{9,24},{... | collective-permute-start | bytes 4718600 | tf_op jit(solution)/shard_map/ppermute | solution.py:556
  20.5 40.2 %collective-permute-start.1 = (s32[1]{0:T(128)}, s32[1]{0:T(128)}, u32[]{:S(2)}, u32[]{:S(2)}) collective-permute-start(s32[1]{0:T(128)} %param.13), channel_id=1, source_target_pairs={{0,0},{1,16},{2,2},{3,18},{4,4},{5,20},{6,6},{7,22},{8,8},{9,24},{... | collective-permute-start | bytes 20 | tf_op jit(solution)/shard_map/ppermute | solution.py:556
  22.4 8.3 copy-start
  30.7 4.4 copy-start.5
  30.7 4.4 copy-start.6
  30.7 5.0 copy-start.4
  30.7 5.6 copy-start.7
  30.7 5.6 copy-start.8
  178.3 3.6 copy-start.2
  180.4 1.4 collective-permute-start.2
  183.6 1.2 collective-permute-start.3
  221.3 219.2 %reduce-scatter.13.cloned.1.call-start = ((), (), s32[]{:S(2)}) async-start(), calls=%async_computation.10 | async-start | bytes 1253376 | tf_op jit(solution)/shard_map/reduce_scatter | solution.py:606
  358.2 153.4 %reduce-scatter.11.cloned.1.call-start = ((), (), s32[]{:S(2)}) async-start(), calls=%async_computation.9 | async-start | bytes 3760128 | tf_op jit(solution)/shard_map/reduce_scatter | solution.py:606
  358.9 223.3 %reduce-scatter.9.cloned.1.call-start = ((), (), s32[]{:S(2)}) async-start(), calls=%async_computation.8 | async-start | bytes 3760128 | tf_op jit(solution)/shard_map/reduce_scatter | solution.py:606
  420.3 240.1 %reduce-scatter.19.cloned.1.call-start = ((), (), s32[]{:S(2)}) async-start(), calls=%async_computation.13 | async-start | bytes 5013504 | tf_op jit(solution)/shard_map/reduce_scatter | solution.py:606
  420.9 318.4 %reduce-scatter.17.cloned.1.call-start = ((), (), s32[]{:S(2)}) async-start(), calls=%async_computation.12 | async-start | bytes 5013504 | tf_op jit(solution)/shard_map/reduce_scatter | solution.py:606
  421.5 396.4 %reduce-scatter.23.cloned.1.call-start = ((), (), s32[]{:S(2)}) async-start(), calls=%async_computation.15 | async-start | bytes 5013504 | tf_op jit(solution)/shard_map/reduce_scatter | solution.py:606
  422.2 474.6 %reduce-scatter.21.cloned.1.call-start = ((), (), s32[]{:S(2)}) async-start(), calls=%async_computation.14 | async-start | bytes 5013504 | tf_op jit(solution)/shard_map/reduce_scatter | solution.py:606
  423.0 475.8 %copy-start.1 = (f32[1024,768]{1,0:T(8,128)S(1)}, f32[1024,768]{1,0:T(8,128)}, u32[]{:S(2)}) copy-start(f32[1024,768]{1,0:T(8,128)} %get-tuple-element.106) | copy-start | bytes 9437188
  423.0 551.8 %all-reduce.3.cloned.1.call-start = ((), (), s32[]{:S(2)}) async-start(), calls=%async_computation.16 | async-start | bytes 3538944 | tf_op jit(solution)/shard_map/psum | solution.py:608
  898.8 3.4 copy-start.9
  898.8 3.4 copy-start.12
  898.8 3.5 copy-start.10
  898.8 3.5 copy-start.11
  900.1 74.7 %collective-permute-start.4 = (bf16[1024,768]{1,0:T(8,128)(2,1)}, bf16[1024,768]{1,0:T(8,128)(2,1)S(1)}, u32[]{:S(2)}, u32[]{:S(2)}) collective-permute-start(bf16[1024,768]{1,0:T(8,128)(2,1)} %convert_element_type.91), channel_id=1, source_target_pairs={{0,0},{1,16},{2,2},{3,18},{4,4},{5,20},{6,6},{7,22},{8,8},{9,24},{... | collective-permute-start | bytes 4718600 | tf_op jit(solution)/shard_map/ppermute | solution.py:556
  974.8 5.9 copy-start.3
Sparse Core Ops, SparseCore 0:
  221.4 122.7 reduce-scatter.14
  358.3 82.2 reduce-scatter.12
  444.4 67.0 reduce-scatter.10
  515.3 66.9 reduce-scatter.8
  586.0 74.4 reduce-scatter.18
  664.6 74.6 reduce-scatter.16
  743.2 74.6 reduce-scatter.22
  822.2 74.6 reduce-scatter.20
  900.5 65.5 all-reduce.2

commit v2 on v1

v2 whole, which is shorter than its diff:
```python
import functools
import math

import jax
import jax.numpy as jnp
from jax import lax
from jax.experimental import pallas as pl
from jax.experimental.pallas import tpu as pltpu
from jax.sharding import PartitionSpec as P

HEAD_DIM = 64
EPSILON = 1e-05
SCALE = HEAD_DIM**-0.5
MESH = pl.DeviceIdType.MESH
NN = (((1,), (0,)), ((), ()))
NT = (((1,), (1,)), ((), ()))
TN = (((0,), (0,)), ((), ()))
BLOCK = 256
LANES = 128
BF16 = jnp.bfloat16
F32 = jnp.float32
VMEM_LIMIT = 62 * 2**20
ANY = pl.BlockSpec(memory_space=pl.ANY)


def dot(left, right, dims=NN):
    return lax.dot_general(left, right, dims, preferred_element_type=F32)


def sds(shape, dtype):
    return jax.ShapeDtypeStruct(shape, dtype)


def params(collective_id=None):
    return pltpu.CompilerParams(
        vmem_limit_bytes=VMEM_LIMIT,
        collective_id=collective_id,
        has_side_effects=collective_id is not None,
    )


def whole(shape):
    zeros = (0,) * len(shape)
    return pl.BlockSpec(shape, lambda *_: zeros, pipeline_mode=pl.Buffered(1))


def norm(hidden, gain, bias):
    centred = hidden - jnp.mean(hidden, -1, keepdims=True)
    inverse = lax.rsqrt(jnp.mean(centred * centred, -1, keepdims=True) + EPSILON)
    scaled = centred * inverse
    return (scaled * gain + bias).astype(BF16), scaled, inverse


def norm_back(grad, scaled, inverse, gain):
    e = grad * gain
    return inverse * (
        e - jnp.mean(e, -1, keepdims=True) - scaled * jnp.mean(e * scaled, -1, keepdims=True)
    )


def partner():
    rows = lax.axis_index("rows")
    return rows + 1 - 2 * (rows % 2)


def greet():
    barrier = pltpu.get_barrier_semaphore()
    pl.semaphore_signal(barrier, inc=1, device_id={"rows": partner()}, device_id_type=MESH)
    pl.semaphore_wait(barrier, 1)


def bits():
    row = lax.axis_index("rows")
    return row, row % 2, (row // 2) % 2, (row // 4) % 2, (row // 8) % 2, lax.axis_index("pass")


def send(src, dst, send_sem, recv_sem, device):
    return pltpu.make_async_remote_copy(
        src_ref=src, dst_ref=dst, send_sem=send_sem, recv_sem=recv_sem,
        device_id=device, device_id_type=MESH,
    )


def qkv_kernel(
    depth, kept, hidden_ref, embed_ref, gain_ref, bias_ref, weight_ref, *refs,
):
    full_ref, normed_ref, scaled_ref, inverse_ref, query_ref, kv_ref = refs[kept : kept + 6]
    held, local_sem, send_sem, recv_sem = refs[kept + 6 :]
    step = pl.program_id(0)
    own = lax.axis_index("rows") % 2
    width = hidden_ref.shape[1]

    @pl.when(step == 0)
    def _():
        greet()

    hidden = hidden_ref[...].astype(F32) + embed_ref[...]
    full_ref[...] = hidden
    normed, scaled, inverse = norm(hidden, gain_ref[...], bias_ref[...])
    normed_ref[0, 0] = normed
    scaled_ref[0, 0] = scaled.astype(BF16)
    inverse_ref[0, 0] = inverse
    keys = dot(normed, weight_ref[0, :, width:])
    held[step] = keys.astype(BF16)

    def copies(i):
        there = send(held.at[i], kv_ref.at[depth, i, own], send_sem.at[i], recv_sem.at[i], {"rows": partner()})
        here = pltpu.make_async_copy(held.at[i], kv_ref.at[depth, i, own], local_sem.at[i])
        return there, here

    there, here = copies(step)
    there.start()
    here.start()
    queries = dot(normed, weight_ref[0, :, :width])
    query_ref[0] = (queries.astype(BF16).astype(F32) * SCALE).astype(BF16)

    @pl.when(step == pl.num_programs(0) - 1)
    def _():
        for i in range(held.shape[0]):
            there, here = copies(i)
            there.wait()
            here.wait()


def qkv(depth, layers, hidden, embed, gain, bias, weight, kept):
    tokens, width = hidden.shape
    steps = tokens // BLOCK
    tile = pl.BlockSpec((BLOCK, width), lambda i: (i, 0))
    own = pl.BlockSpec((1, 1, BLOCK, width), lambda i: (depth, 1, i, 0))
    return pl.pallas_call(
        functools.partial(qkv_kernel, depth, len(kept)),
        grid=(steps,),
        in_specs=[
            tile, whole((1, width)), whole((1, width)), whole((1, width)),
            pl.BlockSpec((1,) + weight.shape[1:], lambda i: (depth, 0, 0), pipeline_mode=pl.Buffered(1)),
        ] + [ANY] * len(kept),
        out_specs=[
            tile, own, own,
            pl.BlockSpec((1, 1, BLOCK, 1), lambda i: (depth, 1, i, 0)),
            pl.BlockSpec((1, BLOCK, width), lambda i: (depth, i, 0)),
            ANY,
        ],
        out_shape=[
            sds((tokens, width), F32),
            sds((layers, 2, tokens, width), BF16),
            sds((layers, 2, tokens, width), BF16),
            sds((layers, 2, tokens, 1), F32),
            sds((layers, tokens, width), BF16),
            sds((layers, steps, 2, BLOCK, 2 * width), BF16),
        ],
        input_output_aliases={5 + i: 1 + i for i in range(len(kept))},
        scratch_shapes=[
            pltpu.VMEM((steps, BLOCK, 2 * width), BF16),
            pltpu.SemaphoreType.DMA((steps,)),
            pltpu.SemaphoreType.DMA((steps,)),
            pltpu.SemaphoreType.DMA((steps,)),
        ],
        compiler_params=params(depth),
        name="qkv",
    )(hidden, embed, gain, bias, weight, *kept)


def tile_index(blocks, key_block, query_block):
    return key_block * blocks - key_block * (key_block - 1) // 2 + query_block - key_block


def attend_kernel(kept, length_ref, query_ref, key_ref, value_ref, *refs):
    mixed_ref, total_ref, exp_ref = refs[kept:]
    own = lax.axis_index("rows") % 2
    tokens = query_ref.shape[1]
    blocks = tokens // BLOCK
    pair = 2 * BLOCK
    lane = lax.broadcasted_iota(jnp.int32, (BLOCK, LANES), 1)
    query_at = lax.broadcasted_iota(jnp.int32, (BLOCK, pair), 0)
    column = lax.broadcasted_iota(jnp.int32, (BLOCK, pair), 1)
    key_pass = column // BLOCK
    key_at = column - key_pass * BLOCK
    causal = (key_at < query_at) | ((key_at == query_at) & (key_pass <= own))
    length = length_ref[0]
    ones = jnp.ones((tokens * 2, LANES), BF16)
    values = jnp.concatenate([value_ref[0], ones], 1)
    for block in range(blocks):
        rows = pl.ds(block * BLOCK, BLOCK)

        @pl.when(block * BLOCK < length)
        def _():
            allowed = causal & (key_at < length - block * BLOCK)
            query = query_ref[0, rows, :]
            outs = []
            for head in range(2):
                chosen = jnp.where(lane // HEAD_DIM == head, query, jnp.zeros_like(query))
                raw = dot(chosen, key_ref[0, : (block + 1) * pair, :], NT)
                last = jnp.where(allowed, raw[:, block * pair :], -jnp.inf)
                top = jnp.max(last, -1, keepdims=True)
                if block:
                    top = jnp.maximum(top, jnp.max(raw[:, : block * pair], -1, keepdims=True))
                parts = [jnp.exp(raw[:, k * pair : (k + 1) * pair] - top).astype(BF16) for k in range(block)]
                parts.append(jnp.exp(last - top).astype(BF16))
                for k, part in enumerate(parts):
                    exp_ref[0, head, tile_index(blocks, k, block)] = part
                mixed = dot(jnp.concatenate(parts, 1), values[: (block + 1) * pair])
                inverse = 1.0 / mixed[:, LANES : LANES + 1]
                total_ref[0, 0, rows, head : head + 1] = inverse
                outs.append(mixed[:, :LANES] * inverse)
            mixed_ref[0, rows, :] = jnp.where(lane < HEAD_DIM, outs[0], outs[1]).astype(BF16)

        @pl.when(block * BLOCK >= length)
        def _():
            mixed_ref[0, rows, :] = jnp.zeros((BLOCK, LANES), BF16)
            total_ref[0, 0, rows, :] = jnp.zeros((BLOCK, 2), F32)
            for head in range(2):
                for k in range(block + 1):
                    exp_ref[0, head, tile_index(blocks, k, block)] = jnp.zeros((BLOCK, pair), BF16)


def attend(depth, length, query, kv, kept):
    layers, tokens, width = query.shape
    blocks = tokens // BLOCK
    tiles = blocks * (blocks + 1) // 2
    pairs = width // LANES
    column = pl.BlockSpec((1, tokens, LANES), lambda h: (depth, 0, h))
    return pl.pallas_call(
        functools.partial(attend_kernel, len(kept)),
        grid=(pairs,),
        in_specs=[
            pl.BlockSpec(memory_space=pltpu.SMEM),
            column,
            pl.BlockSpec((1, 2 * tokens, LANES), lambda h: (depth, 0, h)),
            pl.BlockSpec((1, 2 * tokens, LANES), lambda h: (depth, 0, h + pairs)),
        ] + [ANY] * len(kept),
        out_specs=[
            column,
            pl.BlockSpec((1, 1, tokens, 2), lambda h: (depth, h, 0, 0)),
            pl.BlockSpec((1, 2, tiles, BLOCK, 2 * BLOCK), lambda h: (depth, h, 0, 0, 0)),
        ],
        out_shape=[
            sds((layers, tokens, width), BF16),
            sds((layers, pairs, tokens, 2), F32),
            sds((layers, 2 * pairs, tiles, BLOCK, 2 * BLOCK), BF16),
        ],
        input_output_aliases={4 + i: i for i in range(len(kept))},
        compiler_params=params(),
        name="attend",
    )(length, query, kv, kv, *kept)


def gelu_both(v):
    root = math.sqrt(2.0 / math.pi)
    square = v * v
    t = jnp.tanh(v * (root + (root * 0.044715) * square))
    half = 0.5 * (1.0 + t)
    slope = half + 0.5 * v * (1.0 - t * t) * (root + (3.0 * root * 0.044715) * square)
    return v * half, slope


def ffn_kernel(
    kept, hidden_ref, mixed_ref, merge_ref, gain_ref, bias_ref, up_ref, down_ref, *refs,
):
    next_ref, normed_ref, scaled_ref, inverse_ref, act_ref, slope_ref = refs[kept:]
    mid = hidden_ref[...] + dot(mixed_ref[0], merge_ref[0])
    normed, scaled, inverse = norm(mid, gain_ref[...], bias_ref[...])
    normed_ref[0, 0] = normed
    scaled_ref[0, 0] = scaled.astype(BF16)
    inverse_ref[0, 0] = inverse
    total = mid
    hidden_units = up_ref.shape[2]
    part = mid.shape[1]
    for first in range(0, hidden_units, part):
        act, slope = gelu_both(dot(normed, up_ref[0, :, first : first + part]))
        act = act.astype(BF16)
        act_ref[0, :, first : first + part] = act
        slope_ref[0, :, first : first + part] = slope.astype(BF16)
        total = total + dot(act, down_ref[0, first : first + part, :])
    next_ref[...] = total


def ffn(depth, hidden, mixed, merge, gain, bias, up, down, kept):
    tokens, width = hidden.shape
    layers, _, units = up.shape
    tile = pl.BlockSpec((BLOCK, width), lambda i: (i, 0))
    own = pl.BlockSpec((1, 1, BLOCK, width), lambda i: (depth, 0, i, 0))
    wide = pl.BlockSpec((1, BLOCK, units), lambda i: (depth, i, 0))

    def layer(weight):
        return pl.BlockSpec((1,) + weight.shape[1:], lambda i: (depth, 0, 0), pipeline_mode=pl.Buffered(1))

    return pl.pallas_call(
        functools.partial(ffn_kernel, len(kept)),
        grid=(tokens // BLOCK,),
        in_specs=[
            tile, pl.BlockSpec((1, BLOCK, width), lambda i: (depth, i, 0)), layer(merge),
            whole((1, width)), whole((1, width)), layer(up), layer(down),
        ] + [ANY] * len(kept),
        out_specs=[tile, own, own, pl.BlockSpec((1, 1, BLOCK, 1), lambda i: (depth, 0, i, 0)), wide, wide],
        out_shape=[
            sds((tokens, width), F32),
            sds((layers, 2, tokens, width), BF16),
            sds((layers, 2, tokens, width), BF16),
            sds((layers, 2, tokens, 1), F32),
            sds((layers, tokens, units), BF16),
            sds((layers, tokens, units), BF16),
        ],
        input_output_aliases={7 + i: 1 + i for i in range(len(kept))},
        compiler_params=params(),
        name="ffn",
    )(hidden, mixed, merge, gain, bias, up, down, *kept)


FFN_STEPS = 4
PAIRS = 6
STEPS = FFN_STEPS + PAIRS + 3
NO_PIECE = 9
STAGES = 5
ROWS = 16
SHARE = 48
SMALL = 16


def back_kernel(
    layers, hosted,
    cot_ref, act_ref, slope_ref, normed_ref, scaled_ref, inverse_ref, mixed_ref, up_ref, down_ref, merge_ref,
    first_gain_ref, second_gain_ref, query_ref, key_ref, value_ref, total_ref, exp_ref, weight_ref,
    out_ref, small_ref, input_ref,
    grad, low, total, grads, pending, landing, exps,
    staged, sums0, sums1, sums2, sums3, got0, got1, got2, got3, got4, final, small, small_got,
    exp_sem, cot_sem, kv_send, kv_recv, stage_send, stage_recv, out_sem, small_send, small_recv, swap_send, swap_recv,
    here_sem,
):
    t = pl.program_id(0)
    j = t % STEPS
    layer = layers - 1 - t // STEPS
    row, core, x, z0, z1, own_pass = bits()
    tokens, width = grad.shape
    blocks = tokens // BLOCK
    pair = 2 * BLOCK
    busy = t < layers * STEPS
    core_mate = {"rows": row + 1 - 2 * core}
    mates = [
        core_mate, {"rows": row + 2 - 4 * x}, {"rows": row + 4 - 8 * z0}, {"rows": row + 8 - 16 * z1},
        {"pass": 1 - own_pass},
    ]
    diagonal = {"pass": 1 - own_pass, "rows": row + 1 - 2 * core}
    swapped = own_pass != core

    @pl.when(t == 0)
    def _():
        barrier = pltpu.get_barrier_semaphore()
        greeted = mates if hosted else mates[:1]
        for mate in greeted:
            pl.semaphore_signal(barrier, inc=1, device_id=mate, device_id_type=MESH)

        @pl.when(swapped)
        def _():
            pl.semaphore_signal(barrier, inc=1, device_id=diagonal, device_id_type=MESH)

        pl.semaphore_wait(barrier, len(greeted) + jnp.where(swapped, 1, 0))
        load = pltpu.make_async_copy(cot_ref, low, cot_sem)
        load.start()
        load.wait()
        grad[...] = low[...].astype(F32)
        small[...] = jnp.zeros_like(small)


    def exp_copy(head):
        return pltpu.make_async_copy(exp_ref.at[layer, head], exps.at[head % 2], exp_sem.at[head % 2])

    def put(slot, r, value):
        staged[slot, r % 2, (r // 2) % 2, (r // 4) % 2, (r // 8) % 2] = value

    @pl.when(busy & (j < FFN_STEPS))
    def _():
        @pl.when(j == 0)
        def _():
            total[...] = jnp.zeros_like(total)

        grad_low = low[...]
        down_grad = dot(act_ref[0], grad_low, TN).astype(BF16)
        for q in range(4):
            for i in range(4):
                first = q * 4 * SHARE + i * SHARE
                staged[i, q % 2, q // 2, j % 2, (j // 2) % 2] = down_grad[first : first + SHARE]
        grad_act = dot(grad_low, down_ref[0], NT)
        grad_pre = (slope_ref[0].astype(F32) * grad_act).astype(BF16)
        up_grad = dot(normed_ref[0, 0], grad_pre, TN).astype(BF16)
        for r in range(ROWS):
            put(4 + j % 2, r, up_grad[r * SHARE : (r + 1) * SHARE])
        total[...] += dot(grad_pre, up_ref[0], NT)

        @pl.when(j == FFN_STEPS - 1)
        def _():
            exp_copy(0).start()

            def rows(i, sums):
                at = pl.ds(pl.multiple_of(i * BLOCK, BLOCK), BLOCK)
                part = total[at, :]
                scaled = scaled_ref[0, 0, at, :].astype(F32)
                mid = grad[at, :] + norm_back(part, scaled, inverse_ref[0, 0, at, :], second_gain_ref[0])
                grad[at, :] = mid
                low_mid = mid.astype(BF16)
                low[at, :] = low_mid
                grads[0, at, :] = dot(low_mid, merge_ref[0], NT).astype(BF16)
                return (
                    sums[0] + jnp.sum(part * scaled, 0, keepdims=True),
                    sums[1] + jnp.sum(part, 0, keepdims=True),
                )

            empty = jnp.zeros((1, width), F32)
            gain_sum, bias_sum = lax.fori_loop(0, blocks, rows, (empty, empty))
            small[pl.ds(4 + 4 * layer, 1), :] = gain_sum
            small[pl.ds(5 + 4 * layer, 1), :] = bias_sum
            merge_grad = dot(mixed_ref[0], low[...], TN).astype(BF16)
            for r in range(ROWS):
                put(6, r, merge_grad[r * SHARE : (r + 1) * SHARE])


    def kv_copy(p):
        return send(
            pending.at[p % 2], landing.at[p % 2], kv_send.at[p % 2], kv_recv.at[p % 2], core_mate,
        )

    def take(p):
        kv_copy(p).wait()
        lanes = pl.ds(pl.multiple_of(p * LANES, LANES), LANES)
        for which in range(2):
            grads[1 + which, :, lanes] = (
                grads[1 + which, :, lanes].astype(F32) + landing[p % 2, which].astype(F32)
            ).astype(BF16)

    @pl.when(busy & (j >= FFN_STEPS) & (j < FFN_STEPS + PAIRS))
    def _():
        p = j - FFN_STEPS
        lanes = pl.ds(pl.multiple_of(p * LANES, LANES), LANES)
        lane = lax.broadcasted_iota(jnp.int32, (tokens, LANES), 1)
        out_grad = grads[0, :, lanes].astype(F32)
        product = out_grad * mixed_ref[0, :, lanes].astype(F32)
        query = query_ref[0]
        sums = []
        for head in range(2):
            if head:
                @pl.when(p < PAIRS - 1)
                def _():
                    exp_copy(2 * p + 2).start()
            else:
                exp_copy(2 * p + 1).start()
            exp_copy(2 * p + head).wait()
            mine = lane // HEAD_DIM == head
            inverse = total_ref[0, 0, :, head : head + 1]
            scaled = jnp.where(mine, out_grad * inverse, 0.0).astype(BF16)
            inner = jnp.sum(jnp.where(mine, product, 0.0), -1, keepdims=True) * inverse
            chosen = jnp.where(mine, query, jnp.zeros_like(query))
            mine_lanes = slice(head * LANES, (head + 1) * LANES)
            for block in range(blocks):
                first = block * BLOCK
                keys = pl.ds(block * pair, pair)
                start = tile_index(blocks, block, block)
                prob = exps[head, start : start + blocks - block].reshape(tokens - first, pair)
                grad_prob = dot(scaled[first:], value_ref[0, keys, :], NT)
                score = (prob.astype(F32) * (grad_prob - inner[first:])).astype(BF16)
                grad_value = dot(prob, scaled[first:], TN)
                grad_key = dot(score, chosen[first:], TN)
                grad_query = dot(score, key_ref[0, keys, :])
                if block == 0:
                    total[:, mine_lanes] = grad_query
                else:
                    total[first:, mine_lanes] += grad_query
                if head == 0:
                    sums.append((grad_key, grad_value))
                else:
                    for which, value in enumerate((grad_key, grad_value)):
                        both = sums[block][which] + value
                        zero, one = both[:BLOCK], both[BLOCK:]
                        at = pl.ds(first, BLOCK)
                        grads[1 + which, at, lanes] = jnp.where(core == 0, zero, one).astype(BF16)
                        pending[p % 2, which, at, :] = jnp.where(core == 0, one, zero).astype(BF16)
        grads[0, :, lanes] = (
            jnp.where(lane < HEAD_DIM, total[:, :LANES], total[:, LANES : 2 * LANES]) * SCALE
        ).astype(BF16)

        @pl.when(p > 0)
        def _():
            take(p - 1)

        kv_copy(p).start()


    @pl.when(busy & (j >= FFN_STEPS + PAIRS))
    def _():
        n = j - FFN_STEPS - PAIRS

        @pl.when(n == 0)
        def _():
            total[...] = jnp.zeros_like(total)

        @pl.when(n == 0)
        def _():
            take(PAIRS - 1)

        part = grads[n]
        triple_grad = dot(normed_ref[0, 0], part, TN).astype(BF16)
        for r in range(ROWS):
            put(4 + n, r, triple_grad[r * SHARE : (r + 1) * SHARE])
        total[...] += dot(part, weight_ref[0], NT)

        @pl.when(n == 2)
        def _():
            def rows(i, sums):
                at = pl.ds(pl.multiple_of(i * BLOCK, BLOCK), BLOCK)
                part = total[at, :]
                scaled = scaled_ref[0, 0, at, :].astype(F32)
                hidden = grad[at, :] + norm_back(part, scaled, inverse_ref[0, 0, at, :], first_gain_ref[0])
                grad[at, :] = hidden
                low[at, :] = hidden.astype(BF16)
                return (
                    sums[0] + jnp.sum(part * scaled, 0, keepdims=True),
                    sums[1] + jnp.sum(part, 0, keepdims=True),
                    sums[2] + jnp.sum(hidden, 0, keepdims=True),
                )

            empty = jnp.zeros((1, width), F32)
            gain_sum, bias_sum, hidden_sum = lax.fori_loop(0, blocks, rows, (empty, empty, empty))
            small[pl.ds(2 + 4 * layer, 1), :] = gain_sum
            small[pl.ds(3 + 4 * layer, 1), :] = bias_sum

            @pl.when(layer == 0)
            def _():
                small[pl.ds(core, 1), :] = hidden_sum


    last = layers * STEPS - 1

    def slot(v):
        i = v % STEPS
        return jnp.where(
            i < 4, 4 + i % 2, jnp.where(i < 8, i - 4, jnp.where(i == 8, 6, i - FFN_STEPS - PAIRS + 4))
        )

    def whether(v):
        return (v >= 0) & (v <= last) & (v % STEPS != NO_PIECE)

    def half(v):
        return (v - v // STEPS - jnp.where(v % STEPS > NO_PIECE, 1, 0)) % 2

    def out_copy(v):
        h = half(v)
        return pltpu.make_async_copy(final.at[h], out_ref.at[v], out_sem.at[h])

    def stage(s, v):
        h = half(v)
        src = (staged.at[slot(v), 1 - core], sums0.at[h, 1 - x], sums1.at[h, 1 - z0], sums2.at[h, 1 - z1], sums3.at[h])[s]
        dst = (got0, got1, got2, got3, got4)[s].at[h]
        return send(src, dst, stage_send.at[s, h], stage_recv.at[s, h], mates[s])

    def add(a, b):
        return (a.astype(F32) + b.astype(F32)).astype(BF16)

    if hosted:
        @pl.when(whether(t - 6))
        def _():
            out_copy(t - 6).wait()

        @pl.when(whether(t - 5))
        def _():
            v = t - 5
            h = half(v)
            stage(4, v).wait()
            final[h] = sums3[h].astype(F32) + got4[h].astype(F32)
            out_copy(v).start()

        @pl.when(whether(t - 4))
        def _():
            v = t - 4
            h = half(v)
            stage(3, v).wait()
            sums3[h] = add(sums2[h, z1], got3[h])
            stage(4, v).start()

        @pl.when(whether(t - 3))
        def _():
            v = t - 3
            h = half(v)
            stage(2, v).wait()
            sums2[h] = add(sums1[h, z0], got2[h])
            stage(3, v).start()

        @pl.when(whether(t - 2))
        def _():
            v = t - 2
            h = half(v)
            stage(1, v).wait()
            sums1[h] = add(sums0[h, x], got1[h])
            stage(2, v).start()

        @pl.when(whether(t - 1))
        def _():
            v = t - 1
            h = half(v)
            stage(0, v).wait()
            sums0[h] = add(staged[slot(v), core], got0[h])
            stage(1, v).start()

        @pl.when(whether(t))
        def _():
            stage(0, t).start()

        for s in range(STAGES + 1):
            def small_copy(s):
                return send(small, small_got.at[s], small_send.at[s], small_recv.at[s], mates[s])

            @pl.when(t == last + s)
            def _():
                if s:
                    small_copy(s - 1).wait()
                    small[...] += small_got[s - 1]
                if s < STAGES:
                    small_copy(s).start()
    else:
        def piece_copy(v):
            return pltpu.make_async_copy(staged.at[slot(v)], out_ref.at[v], out_sem.at[v % 2])

        @pl.when(whether(t - 1))
        def _():
            piece_copy(t - 1).wait()

        @pl.when(whether(t))
        def _():
            piece_copy(t).start()


    def swap_copy():
        return send(low, input_ref, swap_send, swap_recv, diagonal)

    def here_copy():
        return pltpu.make_async_copy(low, input_ref, here_sem)

    @pl.when((t == last) & swapped)
    def _():
        swap_copy().start()

    @pl.when((t == last) & jnp.logical_not(swapped))
    def _():
        here_copy().start()

    @pl.when(t == pl.num_programs(0) - 1)
    def _():
        @pl.when(swapped)
        def _():
            swap_copy().wait()

        @pl.when(jnp.logical_not(swapped))
        def _():
            here_copy().wait()

        small_ref[...] = small[...]


def back(cotangent, act, slope, normeds, scaleds, inverses, mixed, up, down, merge, first_gain, second_gain, query, kv,
         total, exps, weight, hosted):
    layers, tokens, width = query.shape
    tiles = exps.shape[2]
    steps = layers * STEPS + (STAGES + 2 if hosted else 1)
    piece = (2, 2, 2, 2, SHARE, width)

    def at(t):
        t = jnp.minimum(t, layers * STEPS - 1)
        return layers - 1 - t // STEPS, t % STEPS

    def tile_of(t):
        layer, j = at(t)
        return layer, jnp.minimum(j, FFN_STEPS - 1)

    def head_of(t):
        layer, j = at(t)
        return layer, jnp.clip(j - FFN_STEPS, 0, PAIRS - 1)

    def part_of(t):
        layer, j = at(t)
        return layer, jnp.clip(j - FFN_STEPS - PAIRS, 0, 2)

    def kind_of(t):
        layer, j = at(t)
        return layer, (j >= FFN_STEPS).astype(jnp.int32), 0, 0

    once = dict(pipeline_mode=pl.Buffered(1))

    def of_layer(shape):
        return pl.BlockSpec((1,) + shape, lambda t: (at(t)[0],) + (0,) * len(shape), **once)

    units = pl.BlockSpec((1, tokens, width), lambda t: (tile_of(t)[0], 0, tile_of(t)[1]))
    in_specs = [
        ANY, units, units,
        pl.BlockSpec((1, 1, tokens, width), kind_of, **once),
        pl.BlockSpec((1, 1, tokens, width), kind_of, **once),
        pl.BlockSpec((1, 1, tokens, 1), kind_of, **once),
        of_layer((tokens, width)),
        pl.BlockSpec((1, width, width), lambda t: (tile_of(t)[0], 0, tile_of(t)[1])),
        pl.BlockSpec((1, width, width), lambda t: (tile_of(t)[0], tile_of(t)[1], 0)),
        of_layer((width, width)),
        of_layer((1, width)), of_layer((1, width)),
        pl.BlockSpec((1, tokens, LANES), lambda t: (head_of(t)[0], 0, head_of(t)[1])),
        pl.BlockSpec((1, 2 * tokens, LANES), lambda t: (head_of(t)[0], 0, head_of(t)[1])),
        pl.BlockSpec((1, 2 * tokens, LANES), lambda t: (head_of(t)[0], 0, head_of(t)[1] + PAIRS)),
        pl.BlockSpec((1, 1, tokens, 2), lambda t: (head_of(t)[0], head_of(t)[1], 0, 0)),
        ANY,
        pl.BlockSpec((1, width, width), lambda t: (part_of(t)[0], 0, part_of(t)[1]), **once),
    ]
    out_piece = sds((layers * STEPS, SHARE, width), F32) if hosted else sds((layers * STEPS,) + piece, BF16)
    dma = pltpu.SemaphoreType.DMA

    def some(*shape):
        return pltpu.VMEM(shape, BF16)

    return pl.pallas_call(
        functools.partial(back_kernel, layers, hosted),
        grid=(steps,),
        in_specs=in_specs,
        out_specs=[ANY, whole((SMALL, width)), ANY],
        out_shape=[out_piece, sds((SMALL, width), F32), sds((tokens, width), BF16)],
        scratch_shapes=[
            pltpu.VMEM((tokens, width), F32),
            some(tokens, width),
            pltpu.VMEM((tokens, width), F32),
            some(3, tokens, width),
            some(2, 2, tokens, LANES),
            some(2, 2, tokens, LANES),
            some(2, tiles, BLOCK, 2 * BLOCK),
            some(7, *piece),
            some(2, *piece[1:]), some(2, *piece[2:]), some(2, *piece[3:]), some(2, *piece[4:]),
            some(2, *piece[1:]), some(2, *piece[2:]), some(2, *piece[3:]), some(2, *piece[4:]), some(2, *piece[4:]),
            pltpu.VMEM((2, SHARE, width), F32),
            pltpu.VMEM((SMALL, width), F32),
            pltpu.VMEM((STAGES, SMALL, width), F32),
            dma((2,)), dma, dma((2,)), dma((2,)), dma((STAGES, 2)), dma((STAGES, 2)), dma((2,)),
            dma((STAGES,)), dma((STAGES,)), dma, dma, dma,
        ],
        compiler_params=params(layers),
        name="back",
    )(cotangent, act, slope, normeds, scaleds, inverses, mixed, up, down, merge, first_gain, second_gain, query, kv, kv,
      total, exps, weight)


def local(
    stream, lengths, pass_embed, first_gain, first_bias, triple_weight, merge_weight,
    second_gain, second_bias, up_weight, down_weight, cotangent,
):
    row_count = lax.axis_size("rows")
    own_row = lax.axis_index("rows")
    core = own_row % 2
    tokens, width = stream.shape[2], stream.shape[3]
    layers = triple_weight.shape[0]
    hosted = row_count == ROWS

    def holder(p, r):
        return p * row_count + r if p == r % 2 else (1 - p) * row_count + (r ^ 1)

    swaps = [(p * row_count + r, holder(p, r)) for p in range(2) for r in range(row_count)]

    def swap(x):
        return lax.ppermute(x, ("pass", "rows"), swaps)

    valid = (jnp.arange(tokens) < lengths[0]).astype(F32)[:, None]
    hidden = swap(stream.reshape(tokens, width))
    length = swap(lengths)
    cotangent = swap((cotangent.reshape(tokens, width).astype(F32) * valid).astype(BF16))
    embed = jnp.where(core == 0, pass_embed[0:1], pass_embed[1:2]).astype(F32)
    nothing = jnp.zeros_like(embed)

    def vector(array, depth):
        return array[depth : depth + 1].astype(F32)

    qkv_kept, attend_kept, ffn_kept = [], [], []
    for depth in range(layers):
        hidden, *qkv_kept = qkv(
            depth, layers, hidden, nothing if depth else embed, vector(first_gain, depth), vector(first_bias, depth),
            triple_weight, qkv_kept,
        )
        normeds, scaleds, inverses, query, kv_blocks = qkv_kept
        kv = kv_blocks.reshape(layers, 2 * tokens, 2 * width)
        attend_kept = attend(depth, length, query, kv, attend_kept)
        hidden, *ffn_kept = ffn(
            depth, hidden, attend_kept[0], merge_weight, vector(second_gain, depth), vector(second_bias, depth),
            up_weight, down_weight, [normeds, scaleds, inverses, *ffn_kept[3:]],
        )
        qkv_kept = [*ffn_kept[:3], query, kv_blocks]
    normeds, scaleds, inverses, act, slope = ffn_kept
    mixed, total, exps = attend_kept
    output = (swap(hidden.astype(BF16)).astype(F32) * valid).astype(BF16).reshape(stream.shape)

    pieces, small, input_grad = back(
        cotangent, act, slope, normeds, scaleds, inverses, mixed, up_weight, down_weight, merge_weight,
        first_gain.astype(F32)[:, None], second_gain.astype(F32)[:, None], query, kv, total, exps, triple_weight, hosted,
    )
    input_grad = input_grad.reshape(stream.shape)
    if hosted:
        pieces = pieces.reshape(layers, STEPS, SHARE, width)
    else:
        pieces = pieces.reshape(layers, STEPS, 2, 2, 2, 2, SHARE, width).transpose(0, 1, 5, 4, 3, 2, 6, 7)
    pieces = pieces[::-1]

    def columns(first, last):
        some = pieces[:, first:last]
        some = some.reshape(layers, last - first, -1, width)
        return some.transpose(0, 2, 1, 3).reshape(layers, -1, (last - first) * width)

    up_grad = columns(0, 4)
    merge_grad = columns(8, 9)
    triple_grad = columns(10, 13)
    down_grad = pieces[:, 4:8]
    if hosted:
        down_grad = down_grad.reshape(layers, 4 * SHARE, width)
    else:
        down_grad = down_grad.reshape(layers, 4, ROWS, SHARE, width).transpose(0, 2, 1, 3, 4).reshape(layers, -1, width)

        def reduce(gradient):
            share = lax.psum_scatter(gradient, "rows", scatter_dimension=1, tiled=True)
            return lax.psum(share, "pass").astype(F32)

        up_grad, merge_grad, triple_grad, down_grad = map(reduce, (up_grad, merge_grad, triple_grad, down_grad))
        small = lax.psum(small, ("pass", "rows"))
    share = width // row_count
    small = lax.dynamic_slice_in_dim(small, own_row * share, share, 1)
    by_layer = small[2 : 2 + 4 * layers].reshape(layers, 4, share)
    return (
        output, input_grad, small[:2], by_layer[:, 0], by_layer[:, 1], triple_grad, merge_grad,
        by_layer[:, 2], by_layer[:, 3], up_grad, down_grad,
    )


def solution(mesh):
    token = P("pass", "rows", None, None)
    matrix = P(None, "rows", None)
    rows = P(None, "rows")
    in_specs = (token, P("rows")) + (P(),) * 9 + (token,)
    out_specs = (token, token, rows, rows, rows, matrix, matrix, rows, rows, matrix, matrix)
    return jax.shard_map(local, mesh=mesh, in_specs=in_specs, out_specs=out_specs, check_vma=False)
```

time: 995 us -> 496 us (0.50)
  waiting for transfers between devices: 472 us -> 0.01 us
  Pallas kernels: 362 us -> 459 us
  blocking collectives: 71.1 us -> 0 us
  other arithmetic: 23.3 us -> 8.48 us
  between operations: 15 us -> 1.62 us
  starting transfers between devices: 19.7 us -> 6.75 us
    reduce_scatter x8 -> x0, waiting for transfers between devices: 468 us -> none  [reduce(): lax.psum_scatter(g, 'rows', scatter_dimension=0, tiled=True)]
    pallas_call x12 -> x7, Pallas kernels: 362 us -> 459 us  [the longest x1 334 us: back(): pl.pallas_call(functools.partial(back_kernel, layers, hosted), grid=(step...]
    psum x1 -> x0, blocking collectives: 71.1 us -> none  [local(): small = lax.psum(small, ('pass', 'rows'))]
    squeeze x4 -> x0, local copies, waits for them, and re-layouts: 22.8 us -> none  [the longest x1 8 us: local(): down_weight[depth]]
    ppermute x5 -> x4, starting transfers between devices: 19.1 us -> 6.75 us  [swap(): return lax.ppermute(x, ('pass', 'rows'), swaps)]
    convert_element_type x6 -> x0, other arithmetic: 10.2 us -> none  [the longest x4 6.95 us: reduce(): return lax.psum(jnp.stack(shares), 'pass').astype(F32)]
  transfers between devices with their start and end apart: 14 -> 4, of which waited for: 7 -> 0; matrix products, arithmetic and copies ran while one was open for 3% -> 1% of each run, Pallas kernels for 21% -> 6%
where the time goes in v2:
time: 496 us; the launch traced here: 493 us
  Pallas kernels  459 us (93%)
  local copies, waits for them, and re-layouts  17.3 us (3%)
  other arithmetic  8.48 us (2%)
  starting transfers between devices  6.75 us (1%)
    pallas_call x1, Pallas kernels, back(): pl.pallas_call(functools.partial(back_kernel, layers, hosted), grid=(step...  334 us
    pallas_call x2, Pallas kernels, ffn(): pl.pallas_call(functools.partial(ffn_kernel, len(kept)), grid=(tokens //...  45.5 us
    pallas_call x2, Pallas kernels, qkv(): pl.pallas_call(functools.partial(qkv_kernel, depth, len(kept)), grid=(ste...  40.1 us
    pallas_call x2, Pallas kernels, attend(): pl.pallas_call(functools.partial(attend_kernel, len(kept)), grid=(pairs,)...  39.7 us
  transfers between devices with their start and end apart: 4, of which 0 were waited for; matrix products, arithmetic and copies ran while one was open for 1% of the time, Pallas kernels for 6%

profile of v2, /device:TPU:0, one launch (start us, length us, event | category | flops | bytes accessed | tf_op | source)
XLA Modules:
  0.0 493.2 jit_solution(4688626627184049653)
XLA Ops:
  0.6 2.1 collective-permute-start
  2.7 1.9 collective-permute-start.1
  4.6 1.3 slice_convert_fusion.3
  5.9 1.4 slice_convert_fusion.2
  7.3 1.4 slice_convert_fusion
  8.7 1.1 copy-done.3
  9.8 27.3 %qkv.2 = (f32[1024,768]{1,0:T(8,128)}, bf16[2,2,1024,768]{3,2,1,0:T(8,128)(2,1)}, bf16[2,2,1024,768]{3,2,1,0:T(8,128)(2,1)}, f32[2,2,1024,1]{3,2,1,0:T(8,128)}, ...) custom-call(bf16[1024,768]{1,0:T(8,128)(2,1)} %copy-done.3, f32[1,768]{1,0:T(1,128)} %get-tuple-element.93.embed_ref, ...), custom_call_target="tpu_custom_call" | custom-call | tf_op jit(solution)/shard_map/qkv/pallas_call | solution.py:130
  37.1 19.9 %attend.2 = (bf16[2,1024,768]{2,1,0:T(8,128)(2,1)}, f32[2,6,1024,2]{3,2,1,0:T(8,128)}, bf16[2,12,10,256,512]{4,3,2,1,0:T(8,128)(2,1)}) custom-call(s32[1]{0:T(128)} %collective-permute-done.1.length_ref, bf16[2,1024,768]{2,1,0:T(8,128)(2,1)} %get-tuple-element.45.query_ref.refs_3_, bf16[2,2048,1536]{2,1,0:T(8,128)(2,1)} %bitcast.36, ...), custom_call_target="tpu_custom_call" | custom-call | tf_op jit(solution)/shard_map/attend/pallas_call | solution.py:222
  57.0 22.8 %ffn.2 = (f32[1024,768]{1,0:T(8,128)}, bf16[2,2,1024,768]{3,2,1,0:T(8,128)(2,1)}, bf16[2,2,1024,768]{3,2,1,0:T(8,128)(2,1)}, f32[2,2,1024,1]{3,2,1,0:T(8,128)}, ...) custom-call(f32[1024,768]{1,0:T(8,128)} %get-tuple-element.44.hidden, ...), custom_call_target="tpu_custom_call", output_to_operand_aliasing={{1}: (7, {}), {2}: (8, {}), {3}: (9, {})} | custom-call | tf_op jit(solution)/shard_map/ffn/pallas_call | solution.py:287
  79.9 0.6 broadcast_in_dim.14.embed_ref
  80.4 12.8 %qkv.3 = (f32[1024,768]{1,0:T(8,128)}, bf16[2,2,1024,768]{3,2,1,0:T(8,128)(2,1)}, bf16[2,2,1024,768]{3,2,1,0:T(8,128)(2,1)}, f32[2,2,1024,1]{3,2,1,0:T(8,128)}, ...) custom-call(f32[1024,768]{1,0:T(8,128)} %get-tuple-element.51.hidden, ...), custom_call_target="tpu_custom_call", output_to_operand_aliasing={{1}: (5, {}), {2}: (6, {}), {3}: (7, {}), {4}: (8, {}), {5}... | custom-call | tf_op jit(solution)/shard_map/qkv/pallas_call | solution.py:130
  93.2 19.8 %attend.3 = (bf16[2,1024,768]{2,1,0:T(8,128)(2,1)}, f32[2,6,1024,2]{3,2,1,0:T(8,128)}, bf16[2,12,10,256,512]{4,3,2,1,0:T(8,128)(2,1)}) custom-call(s32[1]{0:T(128)} %collective-permute-done.1.length_ref, bf16[2,1024,768]{2,1,0:T(8,128)(2,1)} %get-tuple-element.56.query_ref, ...), custom_call_target="tpu_custom_call", output_to_operand_aliasing={{0}: (4, {}), {1}: (5, {}), {2}: (6, {})} | custom-call | tf_op jit(solution)/shard_map/attend/pallas_call | solution.py:222
  113.0 22.7 %ffn.3 = (f32[1024,768]{1,0:T(8,128)}, bf16[2,2,1024,768]{3,2,1,0:T(8,128)(2,1)}, bf16[2,2,1024,768]{3,2,1,0:T(8,128)(2,1)}, f32[2,2,1024,1]{3,2,1,0:T(8,128)}, ...) custom-call(f32[1024,768]{1,0:T(8,128)} %get-tuple-element.55.hidden, ...), custom_call_target="tpu_custom_call", output_to_operand_aliasing={{1}: (7, {}), {2}: (8, {}), {3}: (9, {}), {4}: (10, {}), {5... | custom-call | tf_op jit(solution)/shard_map/ffn/pallas_call | solution.py:287
  135.8 2.2 convert_element_type.63
  137.9 0.8 collective-permute-start.2
  139.4 2.2 fusion
  141.7 2.1 collective-permute-start.3
  143.7 0.6 reshape.71.first_gain_ref
  144.3 0.6 reshape.72.second_gain_ref
  144.9 1.1 copy-done
  146.1 333.7 %back.1 = (f32[26,48,768]{2,1,0:T(8,128)}, f32[16,768]{1,0:T(8,128)}, bf16[1024,768]{1,0:T(8,128)(2,1)}) custom-call(bf16[1024,768]{1,0:T(8,128)(2,1)} %copy-done, bf16[2,1024,3072]{2,1,0:T(8,128)(2,1)} %get-tuple-element.67.act_ref, bf16[2,1024,3072]{2,1,0:T(8,128)(2,1)} %get-tuple-element.68.slope_ref, ...), custom_call_target="tpu_custom_call" | custom-call | tf_op jit(solution)/shard_map/back/pallas_call | solution.py:712
  479.8 1.8 fusion.4
  481.5 1.2 slice.98
  482.8 1.0 slice_bitcast_fusion
  483.9 1.1 copy.59
  485.0 0.6 copy.55
  485.8 1.5 reshape.67
  487.3 1.1 slice.95
  488.4 0.7 reverse_bitcast_fusion.2
  489.2 1.3 constant_dynamic-slice_fusion
  490.5 0.8 dynamic-slice.1
  491.9 1.1 copy.78
  (18 shorter events, 0.9 us)
Async XLA Ops:
  0.6 8.0 %collective-permute-start = (bf16[1024,768]{1,0:T(8,128)(2,1)}, bf16[1024,768]{1,0:T(8,128)(2,1)S(1)}, u32[]{:S(2)}, u32[]{:S(2)}) collective-permute-start(bf16[1024,768]{1,0:T(8,128)(2,1)} %bitcast.53), channel_id=1, source_target_pairs={{0,0},{1,16},{2,2},{3,18},{4,4},{5,20},{6,6},{7,22},{8,8},{9,24},{... | collective-permute-start | bytes 4718600 | tf_op jit(solution)/shard_map/ppermute | solution.py:758
  2.7 34.4 %collective-permute-start.1 = (s32[1]{0:T(128)}, s32[1]{0:T(128)}, u32[]{:S(2)}, u32[]{:S(2)}) collective-permute-start(s32[1]{0:T(128)} %param.13), channel_id=1, source_target_pairs={{0,0},{1,16},{2,2},{3,18},{4,4},{5,20},{6,6},{7,22},{8,8},{9,24},{... | collective-permute-start | bytes 20 | tf_op jit(solution)/shard_map/ppermute | solution.py:758
  8.7 1.1 copy-start.3
  135.8 3.6 copy-start.2
  137.9 1.5 collective-permute-start.2
  139.4 4.3 copy-start.4
  139.4 4.9 copy-start.5
  141.7 3.3 collective-permute-start.3
  144.9 1.1 copy-start
  487.3 4.5 copy-start.1

commit v3 on v2

v3 whole, which is shorter than its diff:
```python
import functools
import math

import jax
import jax.numpy as jnp
from jax import lax
from jax.experimental import pallas as pl
from jax.experimental.pallas import tpu as pltpu
from jax.sharding import PartitionSpec as P

HEAD_DIM = 64
EPSILON = 1e-05
SCALE = HEAD_DIM**-0.5
MESH = pl.DeviceIdType.MESH
NN = (((1,), (0,)), ((), ()))
NT = (((1,), (1,)), ((), ()))
TN = (((0,), (0,)), ((), ()))
BLOCK = 128
TILE = 256
LANES = 128
BF16 = jnp.bfloat16
F32 = jnp.float32
VMEM_LIMIT = 62 * 2**20
ANY = pl.BlockSpec(memory_space=pl.ANY)


def dot(left, right, dims=NN):
    return lax.dot_general(left, right, dims, preferred_element_type=F32)


def sds(shape, dtype):
    return jax.ShapeDtypeStruct(shape, dtype)


def params(collective_id=None):
    return pltpu.CompilerParams(
        vmem_limit_bytes=VMEM_LIMIT,
        collective_id=collective_id,
        has_side_effects=collective_id is not None,
    )


def whole(shape):
    zeros = (0,) * len(shape)
    return pl.BlockSpec(shape, lambda *_: zeros, pipeline_mode=pl.Buffered(1))


def norm(hidden, gain, bias):
    centred = hidden - jnp.mean(hidden, -1, keepdims=True)
    inverse = lax.rsqrt(jnp.mean(centred * centred, -1, keepdims=True) + EPSILON)
    scaled = centred * inverse
    return (scaled * gain + bias).astype(BF16), scaled, inverse


def norm_back(grad, scaled, inverse, gain):
    e = grad * gain
    return inverse * (
        e - jnp.mean(e, -1, keepdims=True) - scaled * jnp.mean(e * scaled, -1, keepdims=True)
    )


def bits():
    row = lax.axis_index("rows")
    return row, row % 2, (row // 2) % 2, (row // 4) % 2, (row // 8) % 2, lax.axis_index("pass")


def send(src, dst, send_sem, recv_sem, device):
    return pltpu.make_async_remote_copy(
        src_ref=src, dst_ref=dst, send_sem=send_sem, recv_sem=recv_sem,
        device_id=device, device_id_type=MESH,
    )


QKV_STEPS = 4
PAIRS = 6
FFN_TILES = 4
FORWARD = QKV_STEPS + PAIRS + FFN_TILES


def tile_index(blocks, key_block, query_block):
    return key_block * blocks - key_block * (key_block - 1) // 2 + query_block - key_block


def gelu_both(v):
    root = math.sqrt(2.0 / math.pi)
    cube = (root * 0.044715) * (v * v)
    half = 0.5 + 0.5 * jnp.tanh(v * (root + cube))
    act = v * half
    return act, half + (act - act * half) * (2.0 * root + 6.0 * cube)


def forward_kernel(
    layers,
    stream_ref, cot_ref, length_ref, embed_ref, first_gain_ref, first_bias_ref, second_gain_ref, second_bias_ref,
    triple_ref, merge_ref, up_ref, down_ref,
    normed_ref, scaled_ref, inverse_ref, query_ref, mixed_ref, total_ref, exp_ref, act_ref, slope_ref, kv_ref,
    out_ref, cot_out_ref, length_out_ref,
    hidden, arrived, length_here, queries, kv, values, mixes, triple, merge, up, down,
    weight_sem, kv_sem, kv_send, kv_recv, free_sem, swap_send, swap_recv, here_sem,
):
    t = pl.program_id(0)
    layer = t // FORWARD
    j = t % FORWARD
    row, core, _, _, _, own_pass = bits()
    tokens, width = hidden.shape
    blocks = tokens // BLOCK
    pair = 2 * BLOCK
    core_mate = {"rows": row + 1 - 2 * core}
    diagonal = {"pass": 1 - own_pass, "rows": row + 1 - 2 * core}
    swapped = own_pass != core


    def moves(i):
        if i < QKV_STEPS:
            rows = pl.ds(i * TILE, TILE)
            ends = stream_ref.at[rows, :], arrived.at[rows, :]
        else:
            ends = ((cot_ref, cot_out_ref), (length_ref, length_here))[i - QKV_STEPS]
        return (
            send(*ends, swap_send.at[i], swap_recv.at[i], diagonal),
            pltpu.make_async_copy(*ends, here_sem.at[i]),
        )

    def move(i, act):
        there, here = moves(i)

        @pl.when(swapped)
        def _():
            getattr(there, act)()

        @pl.when(jnp.logical_not(swapped))
        def _():
            getattr(here, act)()


    def weight_copies(which, of_layer):
        refs = ((triple_ref, triple), (merge_ref, merge), (up_ref, up), (down_ref, down))
        source, target = refs[which]
        return pltpu.make_async_copy(source.at[of_layer], target, weight_sem.at[which])

    @pl.when(t == 0)
    def _():
        barrier = pltpu.get_barrier_semaphore()
        pl.semaphore_signal(barrier, inc=1, device_id=core_mate, device_id_type=MESH)

        @pl.when(swapped)
        def _():
            pl.semaphore_signal(barrier, inc=1, device_id=diagonal, device_id_type=MESH)

        pl.semaphore_wait(barrier, 1 + jnp.where(swapped, 1, 0))
        move(QKV_STEPS + 1, "start")
        for i in range(QKV_STEPS):
            move(i, "start")
        for which in range(4):
            weight_copies(which, 0).start()
        move(QKV_STEPS + 1, "wait")
        length_out_ref[...] = length_here[...]

    for i in range(QKV_STEPS):
        @pl.when(t == i)
        def _():
            move(i, "wait")
            if i == QKV_STEPS - 1:
                move(QKV_STEPS, "start")


    def kv_copy(i):
        part = kv.at[pl.ds(i * (TILE // BLOCK), TILE // BLOCK), core]
        return send(part, part, kv_send.at[i], kv_recv.at[i], core_mate)

    def kv_keep(of_layer):
        return pltpu.make_async_copy(kv, kv_ref.at[of_layer], kv_sem)

    @pl.when(j < QKV_STEPS)
    def _():
        rows = pl.ds(pl.multiple_of(j * TILE, TILE), TILE)

        @pl.when(layer == 0)
        def _():
            hidden[rows, :] = arrived[rows, :].astype(F32) + embed_ref[...]

        @pl.when(j == 0)
        def _():
            weight_copies(0, layer).wait()

        @pl.when((j == 0) & (layer > 0))
        def _():
            pl.semaphore_wait(free_sem, 1)

        normed, scaled, inverse = norm(hidden[rows, :], first_gain_ref[0], first_bias_ref[0])
        normed_ref[0, 0] = normed
        scaled_ref[0, 0] = scaled.astype(BF16)
        inverse_ref[0, 0] = inverse
        keys = dot(normed, triple[:, width:]).astype(BF16)
        for b in range(TILE // BLOCK):
            kv[j * (TILE // BLOCK) + b, core] = keys[b * BLOCK : (b + 1) * BLOCK]
        kv_copy(j).start()
        query = (dot(normed, triple[:, :width]).astype(BF16).astype(F32) * SCALE).astype(BF16)
        queries[rows, :] = query
        query_ref[0] = query


    @pl.when((j >= QKV_STEPS) & (j < QKV_STEPS + PAIRS))
    def _():
        p = j - QKV_STEPS
        lanes = pl.ds(pl.multiple_of(p * LANES, LANES), LANES)
        value_lanes = pl.ds(pl.multiple_of(width + p * LANES, LANES), LANES)

        @pl.when(p == 0)
        def _():
            for i in range(QKV_STEPS):
                kv_copy(i).wait()
            kv_keep(layer).start()

        @pl.when((p == 0) & (layer < layers - 1))
        def _():
            weight_copies(0, layer + 1).start()

        values[:, :LANES] = kv[:, :, :, value_lanes].reshape(2 * tokens, LANES)
        values[:, LANES:] = jnp.ones((2 * tokens, LANES), BF16)
        lane = lax.broadcasted_iota(jnp.int32, (BLOCK, LANES), 1)
        query_at = lax.broadcasted_iota(jnp.int32, (BLOCK, pair), 0)
        column = lax.broadcasted_iota(jnp.int32, (BLOCK, pair), 1)
        key_pass = column // BLOCK
        key_at = column - key_pass * BLOCK
        causal = (key_at < query_at) | ((key_at == query_at) & (key_pass <= core))
        length = length_here[0:1, 0:1]

        def scores(block, head):
            query = queries[pl.ds(block * BLOCK, BLOCK), lanes]
            chosen = jnp.where(lane // HEAD_DIM == head, query, jnp.zeros_like(query))
            keys = kv[: block + 1, :, :, lanes].reshape((block + 1) * pair, LANES)
            return dot(chosen, keys, NT)

        def exponentials(block, head, raw):
            allowed = causal & (key_at + block * BLOCK < length)
            last = jnp.where(allowed, raw[:, block * pair :], -jnp.inf)
            top = jnp.max(last, -1, keepdims=True)
            if block:
                top = jnp.maximum(top, jnp.max(raw[:, : block * pair], -1, keepdims=True))
            parts = []
            for k in range(block + 1):
                source = last if k == block else raw[:, k * pair : (k + 1) * pair]
                part = jnp.exp(source - top).astype(BF16)
                exp_ref[0, head, tile_index(blocks, k, block)] = part
                parts.append(part)
            return jnp.concatenate(parts, 1) if block else parts[0]

        outs = {}

        def mix(block, head, exps):
            both = dot(exps, values[: (block + 1) * pair, :])
            inverse = jnp.where(block * BLOCK < length, 1.0 / both[:, LANES : LANES + 1], 0.0)
            rows = pl.ds(block * BLOCK, BLOCK)
            total_ref[0, 0, rows, head : head + 1] = inverse
            outs[head] = both[:, :LANES] * inverse
            if head == 1:
                value = jnp.where(lane < HEAD_DIM, outs[0], outs[1]).astype(BF16)
                mixes[rows, lanes] = value
                mixed_ref[0, rows, :] = value

        items = [(block, head) for block in range(blocks) for head in range(2)]
        ahead = scores(*items[0])
        behind = None
        for n, item in enumerate(items):
            raw = ahead
            if n + 1 < len(items):
                ahead = scores(*items[n + 1])
            exps = exponentials(*item, raw)
            if behind is not None:
                mix(*behind)
            behind = (*item, exps)
        mix(*behind)

        @pl.when(p == PAIRS - 1)
        def _():
            kv_keep(layer).wait()

        @pl.when((p == PAIRS - 1) & (layer < layers - 1))
        def _():
            pl.semaphore_signal(free_sem, inc=1, device_id=core_mate, device_id_type=MESH)


    @pl.when(j >= QKV_STEPS + PAIRS)
    def _():
        i = j - QKV_STEPS - PAIRS
        rows = pl.ds(pl.multiple_of(i * TILE, TILE), TILE)

        @pl.when(i == 0)
        def _():
            for which in range(1, 4):
                weight_copies(which, layer).wait()

        mid = hidden[rows, :] + dot(mixes[rows, :], merge[...])
        normed, scaled, inverse = norm(mid, second_gain_ref[0], second_bias_ref[0])
        normed_ref[0, 0] = normed
        scaled_ref[0, 0] = scaled.astype(BF16)
        inverse_ref[0, 0] = inverse
        parts = up.shape[1] // width
        sum_next = mid
        ahead = dot(normed, up[:, :width])
        for part in range(parts):
            at = slice(part * width, (part + 1) * width)
            now = ahead
            if part + 1 < parts:
                ahead = dot(normed, up[:, (part + 1) * width : (part + 2) * width])
            act, slope = gelu_both(now)
            act = act.astype(BF16)
            act_ref[0, :, at] = act
            slope_ref[0, :, at] = slope.astype(BF16)
            sum_next = sum_next + dot(act, down[at, :])
        hidden[rows, :] = sum_next

        @pl.when(layer == layers - 1)
        def _():
            position = lax.broadcasted_iota(jnp.int32, (TILE, 1), 0) + i * TILE
            valid = (position < length_here[0:1, 0:1]).astype(F32)
            out_ref[...] = (sum_next * valid).astype(BF16)

        @pl.when((i == FFN_TILES - 1) & (layer < layers - 1))
        def _():
            for which in range(1, 4):
                weight_copies(which, layer + 1).start()

    @pl.when(t == pl.num_programs(0) - 1)
    def _():
        move(QKV_STEPS, "wait")


def forward(stream, cotangent, length, embed, first_gain, first_bias, second_gain, second_bias, triple, merge, up, down):
    tokens, width = stream.shape
    layers, _, units = up.shape
    blocks = tokens // BLOCK
    tiles = blocks * (blocks + 1) // 2

    def phase(t):
        return t // FORWARD, t % FORWARD

    def row_tile(t):
        layer, j = phase(t)
        late = j >= QKV_STEPS + PAIRS
        kind = jnp.where(late, 0, 1)
        return layer, kind, jnp.where(late, j - QKV_STEPS - PAIRS, jnp.minimum(j, QKV_STEPS - 1)), 0

    def query_tile(t):
        layer, j = phase(t)
        return layer, jnp.minimum(j, QKV_STEPS - 1), 0

    def head(t):
        layer, j = phase(t)
        return layer, jnp.clip(j - QKV_STEPS, 0, PAIRS - 1)

    def ffn_tile(t):
        layer, j = phase(t)
        return layer, jnp.maximum(j - QKV_STEPS - PAIRS, 0), 0

    vector = pl.BlockSpec((1, 1, width), lambda t: (t // FORWARD, 0, 0))
    rows = pl.BlockSpec((1, 1, TILE, width), row_tile)
    dma = pltpu.SemaphoreType.DMA
    return pl.pallas_call(
        functools.partial(forward_kernel, layers),
        grid=(layers * FORWARD,),
        in_specs=[ANY, ANY, whole(length.shape), whole((1, width)), vector, vector, vector, vector, ANY, ANY, ANY, ANY],
        out_specs=[
            rows, rows, pl.BlockSpec((1, 1, TILE, 1), row_tile),
            pl.BlockSpec((1, TILE, width), query_tile),
            pl.BlockSpec((1, tokens, LANES), lambda t: (head(t)[0], 0, head(t)[1])),
            pl.BlockSpec((1, 1, tokens, 2), lambda t: (*head(t), 0, 0)),
            pl.BlockSpec((1, 2, tiles, BLOCK, 2 * BLOCK), lambda t: (*head(t), 0, 0, 0)),
            pl.BlockSpec((1, TILE, units), ffn_tile), pl.BlockSpec((1, TILE, units), ffn_tile),
            ANY,
            pl.BlockSpec((TILE, width), lambda t: (jnp.where(phase(t)[0] == layers - 1, ffn_tile(t)[1], 0), 0)),
            ANY, whole(length.shape),
        ],
        out_shape=[
            sds((layers, 2, tokens, width), BF16),
            sds((layers, 2, tokens, width), BF16),
            sds((layers, 2, tokens, 1), F32),
            sds((layers, tokens, width), BF16),
            sds((layers, tokens, width), BF16),
            sds((layers, PAIRS, tokens, 2), F32),
            sds((layers, 2 * PAIRS, tiles, BLOCK, 2 * BLOCK), BF16),
            sds((layers, tokens, units), BF16),
            sds((layers, tokens, units), BF16),
            sds((layers, blocks, 2, BLOCK, 2 * width), BF16),
            sds((tokens, width), BF16),
            sds((tokens, width), BF16),
            sds(length.shape, jnp.int32),
        ],
        scratch_shapes=[
            pltpu.VMEM((tokens, width), F32),
            pltpu.VMEM((tokens, width), BF16),
            pltpu.VMEM(length.shape, jnp.int32),
            pltpu.VMEM((tokens, width), BF16),
            pltpu.VMEM((blocks, 2, BLOCK, 2 * width), BF16),
            pltpu.VMEM((2 * tokens, 2 * LANES), BF16),
            pltpu.VMEM((tokens, width), BF16),
            pltpu.VMEM(triple.shape[1:], BF16),
            pltpu.VMEM(merge.shape[1:], BF16),
            pltpu.VMEM(up.shape[1:], BF16),
            pltpu.VMEM(down.shape[1:], BF16),
            dma((4,)), dma, dma((QKV_STEPS,)), dma((QKV_STEPS,)), pltpu.SemaphoreType.REGULAR,
            dma((QKV_STEPS + 2,)), dma((QKV_STEPS + 2,)), dma((QKV_STEPS + 2,)),
        ],
        compiler_params=params(0),
        name="forward",
    )(stream, cotangent, length, embed, first_gain, first_bias, second_gain, second_bias, triple, merge, up, down)


FFN_STEPS = 4
STEPS = FFN_STEPS + PAIRS + 3
NO_PIECE = 9
STAGES = 5
ROWS = 16
SHARE = 48
SMALL = 16


def back_kernel(
    layers, hosted,
    cot_ref, done_ref, length_ref, act_ref, slope_ref, normed_ref, scaled_ref, inverse_ref, mixed_ref, up_ref, down_ref, merge_ref,
    first_gain_ref, second_gain_ref, query_ref, key_ref, value_ref, total_ref, exp_ref, weight_ref,
    out_ref, small_ref, input_ref, output_ref,
    grad, low, total, grads, pending, landing, exps,
    staged, sums0, sums1, sums2, sums3, got0, got1, got2, got3, got4, final, small, small_got,
    exp_sem, cot_sem, kv_send, kv_recv, stage_send, stage_recv, out_sem, small_send, small_recv, swap_send, swap_recv,
    here_sem,
):
    t = pl.program_id(0)
    j = t % STEPS
    layer = layers - 1 - t // STEPS
    row, core, x, z0, z1, own_pass = bits()
    tokens, width = grad.shape
    blocks = tokens // BLOCK
    pair = 2 * BLOCK
    busy = t < layers * STEPS
    core_mate = {"rows": row + 1 - 2 * core}
    mates = [
        core_mate, {"rows": row + 2 - 4 * x}, {"rows": row + 4 - 8 * z0}, {"rows": row + 8 - 16 * z1},
        {"pass": 1 - own_pass},
    ]
    diagonal = {"pass": 1 - own_pass, "rows": row + 1 - 2 * core}
    swapped = own_pass != core

    @pl.when(t == 0)
    def _():
        barrier = pltpu.get_barrier_semaphore()
        greeted = mates if hosted else mates[:1]
        for mate in greeted:
            pl.semaphore_signal(barrier, inc=1, device_id=mate, device_id_type=MESH)

        @pl.when(swapped)
        def _():
            pl.semaphore_signal(barrier, inc=1, device_id=diagonal, device_id_type=MESH)

        pl.semaphore_wait(barrier, len(greeted) + jnp.where(swapped, 1, 0))
        load = pltpu.make_async_copy(cot_ref, low, cot_sem)
        load.start()
        load.wait()
        position = lax.broadcasted_iota(jnp.int32, (tokens, 1), 0)
        valid = (position < length_ref[0:1, 0:1]).astype(F32)
        masked = low[...].astype(F32) * valid
        grad[...] = masked
        low[...] = masked.astype(BF16)
        small[...] = jnp.zeros_like(small)


    def exp_copy(head):
        return pltpu.make_async_copy(exp_ref.at[layer, head], exps.at[head % 2], exp_sem.at[head % 2])

    def put(slot, r, value):
        staged[slot, r % 2, (r // 2) % 2, (r // 4) % 2, (r // 8) % 2] = value

    @pl.when(busy & (j < FFN_STEPS))
    def _():
        @pl.when(j == 0)
        def _():
            total[...] = jnp.zeros_like(total)

        grad_low = low[...]
        down_grad = dot(act_ref[0], grad_low, TN).astype(BF16)
        for q in range(4):
            for i in range(4):
                first = q * 4 * SHARE + i * SHARE
                staged[i, q % 2, q // 2, j % 2, (j // 2) % 2] = down_grad[first : first + SHARE]
        grad_act = dot(grad_low, down_ref[0], NT)
        grad_pre = (slope_ref[0].astype(F32) * grad_act).astype(BF16)
        up_grad = dot(normed_ref[0, 0], grad_pre, TN).astype(BF16)
        for r in range(ROWS):
            put(4 + j % 2, r, up_grad[r * SHARE : (r + 1) * SHARE])
        total[...] += dot(grad_pre, up_ref[0], NT)

        @pl.when(j == FFN_STEPS - 1)
        def _():
            exp_copy(0).start()

            def rows(i, sums):
                at = pl.ds(pl.multiple_of(i * TILE, TILE), TILE)
                part = total[at, :]
                scaled = scaled_ref[0, 0, at, :].astype(F32)
                mid = grad[at, :] + norm_back(part, scaled, inverse_ref[0, 0, at, :], second_gain_ref[0])
                grad[at, :] = mid
                low_mid = mid.astype(BF16)
                low[at, :] = low_mid
                grads[0, at, :] = dot(low_mid, merge_ref[0], NT).astype(BF16)
                return (
                    sums[0] + jnp.sum(part * scaled, 0, keepdims=True),
                    sums[1] + jnp.sum(part, 0, keepdims=True),
                )

            empty = jnp.zeros((1, width), F32)
            gain_sum, bias_sum = lax.fori_loop(0, tokens // TILE, rows, (empty, empty))
            small[pl.ds(4 + 4 * layer, 1), :] = gain_sum
            small[pl.ds(5 + 4 * layer, 1), :] = bias_sum
            merge_grad = dot(mixed_ref[0], low[...], TN).astype(BF16)
            for r in range(ROWS):
                put(6, r, merge_grad[r * SHARE : (r + 1) * SHARE])


    def kv_copy(p):
        return send(
            pending.at[p % 2], landing.at[p % 2], kv_send.at[p % 2], kv_recv.at[p % 2], core_mate,
        )

    def take(p):
        kv_copy(p).wait()
        lanes = pl.ds(pl.multiple_of(p * LANES, LANES), LANES)
        for which in range(2):
            grads[1 + which, :, lanes] = (
                grads[1 + which, :, lanes].astype(F32) + landing[p % 2, which].astype(F32)
            ).astype(BF16)

    @pl.when(busy & (j >= FFN_STEPS) & (j < FFN_STEPS + PAIRS))
    def _():
        p = j - FFN_STEPS
        lanes = pl.ds(pl.multiple_of(p * LANES, LANES), LANES)
        lane = lax.broadcasted_iota(jnp.int32, (tokens, LANES), 1)
        out_grad = grads[0, :, lanes].astype(F32)
        product = out_grad * mixed_ref[0, :, lanes].astype(F32)
        query = query_ref[0]
        scaled, scaled_across, inner, chosen_across = [], [], [], []
        for head in range(2):
            mine = lane // HEAD_DIM == head
            inverse = total_ref[0, 0, :, head : head + 1]
            part = jnp.where(mine, out_grad * inverse, 0.0)
            scaled.append(part.astype(BF16))
            scaled_across.append(part.T.astype(BF16))
            inner.append(jnp.sum(jnp.where(mine, product, 0.0), -1, keepdims=True) * inverse)
            chosen_across.append(jnp.where(mine, query, jnp.zeros_like(query)).astype(F32).T.astype(BF16))

        def probs_grad(head, block):
            return dot(scaled[head][block * BLOCK :], value_ref[0, block * pair : (block + 1) * pair, :], NT)

        def score_grad(head, block, grad_prob):
            start = tile_index(blocks, block, block)
            prob = exps[head, start : start + blocks - block].reshape(tokens - block * BLOCK, pair)
            return prob, (prob.astype(F32) * (grad_prob - inner[head][block * BLOCK :])).astype(BF16)

        sums = {}

        def products(head, block, prob, score):
            first = block * BLOCK
            pairs = dot(chosen_across[head][:, first:], score), dot(scaled_across[head][:, first:], prob)
            grad_query = dot(score, key_ref[0, block * pair : (block + 1) * pair, :])
            mine_lanes = slice(head * LANES, (head + 1) * LANES)
            if block == 0:
                total[:, mine_lanes] = grad_query
            else:
                total[first:, mine_lanes] += grad_query
            if head == 0:
                sums[block] = pairs
                return
            at = pl.ds(first, BLOCK)
            for which in range(2):
                both = (sums[block][which] + pairs[which]).T
                zero, one = both[:BLOCK], both[BLOCK:]
                grads[1 + which, at, lanes] = jnp.where(core == 0, zero, one).astype(BF16)
                pending[p % 2, which, at, :] = jnp.where(core == 0, one, zero).astype(BF16)

        exp_copy(2 * p + 1).start()
        exp_copy(2 * p).wait()
        exp_copy(2 * p + 1).wait()
        items = [(head, block) for head in range(2) for block in range(blocks)]
        ahead = probs_grad(*items[0])
        behind = None
        for n, item in enumerate(items):
            now = ahead
            if n + 1 < len(items):
                ahead = probs_grad(*items[n + 1])
            both = score_grad(*item, now)
            if behind is not None:
                products(*behind)
            behind = (*item, *both)
        products(*behind)

        @pl.when(p < PAIRS - 1)
        def _():
            exp_copy(2 * p + 2).start()

        grads[0, :, lanes] = (
            jnp.where(lane < HEAD_DIM, total[:, :LANES], total[:, LANES : 2 * LANES]) * SCALE
        ).astype(BF16)

        @pl.when(p > 0)
        def _():
            take(p - 1)

        kv_copy(p).start()


    @pl.when(busy & (j >= FFN_STEPS + PAIRS))
    def _():
        n = j - FFN_STEPS - PAIRS

        @pl.when(n == 0)
        def _():
            total[...] = jnp.zeros_like(total)

        @pl.when(n == 0)
        def _():
            take(PAIRS - 1)

        part = grads[n]
        triple_grad = dot(normed_ref[0, 0], part, TN).astype(BF16)
        for r in range(ROWS):
            put(4 + n, r, triple_grad[r * SHARE : (r + 1) * SHARE])
        total[...] += dot(part, weight_ref[0], NT)

        @pl.when(n == 2)
        def _():
            def rows(i, sums):
                at = pl.ds(pl.multiple_of(i * TILE, TILE), TILE)
                part = total[at, :]
                scaled = scaled_ref[0, 0, at, :].astype(F32)
                hidden = grad[at, :] + norm_back(part, scaled, inverse_ref[0, 0, at, :], first_gain_ref[0])
                grad[at, :] = hidden
                low[at, :] = hidden.astype(BF16)
                return (
                    sums[0] + jnp.sum(part * scaled, 0, keepdims=True),
                    sums[1] + jnp.sum(part, 0, keepdims=True),
                    sums[2] + jnp.sum(hidden, 0, keepdims=True),
                )

            empty = jnp.zeros((1, width), F32)
            gain_sum, bias_sum, hidden_sum = lax.fori_loop(0, tokens // TILE, rows, (empty, empty, empty))
            small[pl.ds(2 + 4 * layer, 1), :] = gain_sum
            small[pl.ds(3 + 4 * layer, 1), :] = bias_sum

            @pl.when(layer == 0)
            def _():
                small[pl.ds(core, 1), :] = hidden_sum


    last = layers * STEPS - 1

    def slot(v):
        i = v % STEPS
        return jnp.where(
            i < 4, 4 + i % 2, jnp.where(i < 8, i - 4, jnp.where(i == 8, 6, i - FFN_STEPS - PAIRS + 4))
        )

    def whether(v):
        return (v >= 0) & (v <= last) & (v % STEPS != NO_PIECE)

    def half(v):
        return (v - v // STEPS - jnp.where(v % STEPS > NO_PIECE, 1, 0)) % 2

    def out_copy(v):
        h = half(v)
        return pltpu.make_async_copy(final.at[h], out_ref.at[v], out_sem.at[h])

    def stage(s, v):
        h = half(v)
        src = (staged.at[slot(v), 1 - core], sums0.at[h, 1 - x], sums1.at[h, 1 - z0], sums2.at[h, 1 - z1], sums3.at[h])[s]
        dst = (got0, got1, got2, got3, got4)[s].at[h]
        return send(src, dst, stage_send.at[s, h], stage_recv.at[s, h], mates[s])

    def add(a, b):
        return (a.astype(F32) + b.astype(F32)).astype(BF16)

    if hosted:
        @pl.when(whether(t - 6))
        def _():
            out_copy(t - 6).wait()

        @pl.when(whether(t - 5))
        def _():
            v = t - 5
            h = half(v)
            stage(4, v).wait()
            final[h] = sums3[h].astype(F32) + got4[h].astype(F32)
            out_copy(v).start()

        @pl.when(whether(t - 4))
        def _():
            v = t - 4
            h = half(v)
            stage(3, v).wait()
            sums3[h] = add(sums2[h, z1], got3[h])
            stage(4, v).start()

        @pl.when(whether(t - 3))
        def _():
            v = t - 3
            h = half(v)
            stage(2, v).wait()
            sums2[h] = add(sums1[h, z0], got2[h])
            stage(3, v).start()

        @pl.when(whether(t - 2))
        def _():
            v = t - 2
            h = half(v)
            stage(1, v).wait()
            sums1[h] = add(sums0[h, x], got1[h])
            stage(2, v).start()

        @pl.when(whether(t - 1))
        def _():
            v = t - 1
            h = half(v)
            stage(0, v).wait()
            sums0[h] = add(staged[slot(v), core], got0[h])
            stage(1, v).start()

        @pl.when(whether(t))
        def _():
            stage(0, t).start()

        for s in range(STAGES + 1):
            def small_copy(s):
                return send(small, small_got.at[s], small_send.at[s], small_recv.at[s], mates[s])

            @pl.when(t == last + s)
            def _():
                if s:
                    small_copy(s - 1).wait()
                    small[...] += small_got[s - 1]
                if s < STAGES:
                    small_copy(s).start()
    else:
        def piece_copy(v):
            return pltpu.make_async_copy(staged.at[slot(v)], out_ref.at[v], out_sem.at[v % 2])

        @pl.when(whether(t - 1))
        def _():
            piece_copy(t - 1).wait()

        @pl.when(whether(t))
        def _():
            piece_copy(t).start()


    def swaps(i, act):
        source, target = ((done_ref, output_ref), (low, input_ref))[i]

        @pl.when(swapped)
        def _():
            getattr(send(source, target, swap_send.at[i], swap_recv.at[i], diagonal), act)()

        @pl.when(jnp.logical_not(swapped))
        def _():
            getattr(pltpu.make_async_copy(source, target, here_sem.at[i]), act)()

    @pl.when(t == 0)
    def _():
        swaps(0, "start")

    @pl.when(t == last)
    def _():
        swaps(1, "start")

    @pl.when(t == pl.num_programs(0) - 1)
    def _():
        swaps(0, "wait")
        swaps(1, "wait")
        small_ref[...] = small[...]


def back(cotangent, done, length, act, slope, normeds, scaleds, inverses, mixed, up, down, merge, first_gain, second_gain, query, kv,
         total, exps, weight, hosted):
    layers, tokens, width = query.shape
    tiles = exps.shape[2]
    steps = layers * STEPS + (STAGES + 2 if hosted else 1)
    piece = (2, 2, 2, 2, SHARE, width)

    def at(t):
        t = jnp.minimum(t, layers * STEPS - 1)
        return layers - 1 - t // STEPS, t % STEPS

    def tile_of(t):
        layer, j = at(t)
        return layer, jnp.minimum(j, FFN_STEPS - 1)

    def head_of(t):
        layer, j = at(t)
        return layer, jnp.clip(j - FFN_STEPS, 0, PAIRS - 1)

    def part_of(t):
        layer, j = at(t)
        return layer, jnp.clip(j - FFN_STEPS - PAIRS, 0, 2)

    def kind_of(t):
        layer, j = at(t)
        return layer, (j >= FFN_STEPS).astype(jnp.int32), 0, 0

    once = dict(pipeline_mode=pl.Buffered(1))

    def of_layer(shape):
        return pl.BlockSpec((1,) + shape, lambda t: (at(t)[0],) + (0,) * len(shape), **once)

    units = pl.BlockSpec((1, tokens, width), lambda t: (tile_of(t)[0], 0, tile_of(t)[1]))
    in_specs = [
        ANY, ANY, whole(length.shape), units, units,
        pl.BlockSpec((1, 1, tokens, width), kind_of, **once),
        pl.BlockSpec((1, 1, tokens, width), kind_of, **once),
        pl.BlockSpec((1, 1, tokens, 1), kind_of, **once),
        of_layer((tokens, width)),
        pl.BlockSpec((1, width, width), lambda t: (tile_of(t)[0], 0, tile_of(t)[1])),
        pl.BlockSpec((1, width, width), lambda t: (tile_of(t)[0], tile_of(t)[1], 0)),
        of_layer((width, width)),
        of_layer((1, width)), of_layer((1, width)),
        pl.BlockSpec((1, tokens, LANES), lambda t: (head_of(t)[0], 0, head_of(t)[1])),
        pl.BlockSpec((1, 2 * tokens, LANES), lambda t: (head_of(t)[0], 0, head_of(t)[1])),
        pl.BlockSpec((1, 2 * tokens, LANES), lambda t: (head_of(t)[0], 0, head_of(t)[1] + PAIRS)),
        pl.BlockSpec((1, 1, tokens, 2), lambda t: (head_of(t)[0], head_of(t)[1], 0, 0)),
        ANY,
        pl.BlockSpec((1, width, width), lambda t: (part_of(t)[0], 0, part_of(t)[1]), **once),
    ]
    out_piece = sds((layers * STEPS, SHARE, width), F32) if hosted else sds((layers * STEPS,) + piece, BF16)
    dma = pltpu.SemaphoreType.DMA

    def some(*shape):
        return pltpu.VMEM(shape, BF16)

    return pl.pallas_call(
        functools.partial(back_kernel, layers, hosted),
        grid=(steps,),
        in_specs=in_specs,
        out_specs=[ANY, whole((SMALL, width)), ANY, ANY],
        out_shape=[
            out_piece, sds((SMALL, width), F32), sds((tokens, width), BF16), sds((tokens, width), BF16),
        ],
        scratch_shapes=[
            pltpu.VMEM((tokens, width), F32),
            some(tokens, width),
            pltpu.VMEM((tokens, width), F32),
            some(3, tokens, width),
            some(2, 2, tokens, LANES),
            some(2, 2, tokens, LANES),
            some(2, tiles, BLOCK, 2 * BLOCK),
            some(7, *piece),
            some(2, *piece[1:]), some(2, *piece[2:]), some(2, *piece[3:]), some(2, *piece[4:]),
            some(2, *piece[1:]), some(2, *piece[2:]), some(2, *piece[3:]), some(2, *piece[4:]), some(2, *piece[4:]),
            pltpu.VMEM((2, SHARE, width), F32),
            pltpu.VMEM((SMALL, width), F32),
            pltpu.VMEM((STAGES, SMALL, width), F32),
            dma((2,)), dma, dma((2,)), dma((2,)), dma((STAGES, 2)), dma((STAGES, 2)), dma((2,)),
            dma((STAGES,)), dma((STAGES,)), dma((2,)), dma((2,)), dma((2,)),
        ],
        compiler_params=params(1),
        name="back",
    )(cotangent, done, length, act, slope, normeds, scaleds, inverses, mixed, up, down, merge, first_gain, second_gain, query, kv, kv,
      total, exps, weight)


def local(
    stream, lengths, pass_embed, first_gain, first_bias, triple_weight, merge_weight,
    second_gain, second_bias, up_weight, down_weight, cotangent,
):
    row_count = lax.axis_size("rows")
    own_row = lax.axis_index("rows")
    core = own_row % 2
    tokens, width = stream.shape[2], stream.shape[3]
    layers = triple_weight.shape[0]
    hosted = row_count == ROWS

    embed = jnp.where(core == 0, pass_embed[0:1], pass_embed[1:2]).astype(F32)
    first_gain, first_bias, second_gain, second_bias = (
        v.astype(F32)[:, None] for v in (first_gain, first_bias, second_gain, second_bias)
    )
    (normeds, scaleds, inverses, query, mixed, total, exps, act, slope, kv, done, cotangent, length) = forward(
        stream.reshape(tokens, width), cotangent.reshape(tokens, width),
        jnp.broadcast_to(lengths.reshape(1, 1), (8, LANES)), embed,
        first_gain, first_bias, second_gain, second_bias, triple_weight, merge_weight, up_weight, down_weight,
    )
    pieces, small, input_grad, output = back(
        cotangent, done, length, act, slope, normeds, scaleds, inverses, mixed, up_weight, down_weight, merge_weight,
        first_gain, second_gain, query, kv.reshape(layers, 2 * tokens, 2 * width), total, exps, triple_weight, hosted,
    )
    input_grad = input_grad.reshape(stream.shape)
    output = output.reshape(stream.shape)
    if hosted:
        pieces = pieces.reshape(layers, STEPS, SHARE, width)
    else:
        pieces = pieces.reshape(layers, STEPS, 2, 2, 2, 2, SHARE, width).transpose(0, 1, 5, 4, 3, 2, 6, 7)
    pieces = pieces[::-1]

    def columns(first, last):
        some = pieces[:, first:last]
        some = some.reshape(layers, last - first, -1, width)
        return some.transpose(0, 2, 1, 3).reshape(layers, -1, (last - first) * width)

    up_grad = columns(0, 4)
    merge_grad = columns(8, 9)
    triple_grad = columns(10, 13)
    down_grad = pieces[:, 4:8]
    if hosted:
        down_grad = down_grad.reshape(layers, 4 * SHARE, width)
    else:
        down_grad = down_grad.reshape(layers, 4, ROWS, SHARE, width).transpose(0, 2, 1, 3, 4).reshape(layers, -1, width)

        def reduce(gradient):
            share = lax.psum_scatter(gradient, "rows", scatter_dimension=1, tiled=True)
            return lax.psum(share, "pass").astype(F32)

        up_grad, merge_grad, triple_grad, down_grad = map(reduce, (up_grad, merge_grad, triple_grad, down_grad))
        small = lax.psum(small, ("pass", "rows"))
    share = width // row_count
    small = lax.dynamic_slice_in_dim(small, own_row * share, share, 1)
    by_layer = small[2 : 2 + 4 * layers].reshape(layers, 4, share)
    return (
        output, input_grad, small[:2], by_layer[:, 0], by_layer[:, 1], triple_grad, merge_grad,
        by_layer[:, 2], by_layer[:, 3], up_grad, down_grad,
    )


def solution(mesh):
    token = P("pass", "rows", None, None)
    matrix = P(None, "rows", None)
    rows = P(None, "rows")
    in_specs = (token, P("rows")) + (P(),) * 9 + (token,)
    out_specs = (token, token, rows, rows, rows, matrix, matrix, rows, rows, matrix, matrix)
    return jax.shard_map(local, mesh=mesh, in_specs=in_specs, out_specs=out_specs, check_vma=False)
```

time: 496 us -> 398 us (0.80)
  Pallas kernels: 459 us -> 373 us
  other arithmetic: 8.48 us -> 1.35 us
  starting transfers between devices: 6.75 us -> 0 us
    pallas_call x1, Pallas kernels: 334 us -> 244 us  [back(): pl.pallas_call(functools.partial(back_kernel, layers, hosted), grid=(step...]
    convert_element_type x6 -> x1, other arithmetic: 8.48 us -> 1.35 us  [local(): embed = jnp.where(core == 0, pass_embed[0:1], pass_embed[1:2]).astype(F32)]
    ppermute x4 -> x0, starting transfers between devices: 6.75 us -> none  [swap(): return lax.ppermute(x, ('pass', 'rows'), swaps)]
    pallas_call x6 -> x1, Pallas kernels: 125 us -> 129 us  [forward(): pl.pallas_call(functools.partial(forward_kernel, layers), grid=(layers *...]
  transfers between devices with their start and end apart: 4 -> 0, of which waited for: 0 -> 0; matrix products, arithmetic and copies ran while one was open for 1% -> 0% of each run, Pallas kernels for 6% -> 0%
where the time goes in v3:
time: 398 us; the launch traced here: 397 us
  Pallas kernels  373 us (94%)
  local copies, waits for them, and re-layouts  20.9 us (5%)
    pallas_call x1, Pallas kernels, back(): pl.pallas_call(functools.partial(back_kernel, layers, hosted), grid=(step...  244 us
    pallas_call x1, Pallas kernels, forward(): pl.pallas_call(functools.partial(forward_kernel, layers), grid=(layers *...  129 us

profile of v3, /device:TPU:0, one launch (start us, length us, event | category | flops | bytes accessed | tf_op | source)
XLA Modules:
  0.0 396.7 jit_solution(15423852920886483004)
XLA Ops:
  0.7 1.3 fusion.embed_ref
  2.0 1.3 reshape.64.first_gain_ref
  3.3 1.3 reshape.66.second_gain_ref
  4.6 1.3 reshape.65.first_bias_ref
  5.8 1.3 reshape.67.second_bias_ref
  7.8 0.6 broadcast_in_dim.28.length_ref
  8.4 129.0 %forward.1 = (bf16[2,2,1024,768]{3,2,1,0:T(8,128)(2,1)}, bf16[2,2,1024,768]{3,2,1,0:T(8,128)(2,1)}, f32[2,2,1024,1]{3,2,1,0:T(8,128)}, bf16[2,1024,768]{2,1,0:T(...) custom-call(bf16[1024,768]{1,0:T(8,128)(2,1)} %bitcast.39, ...), custom_call_target="tpu_custom_call" | custom-call | tf_op jit(solution)/shard_map/forward/pallas_call | solution.py:360
  137.4 244.1 %back.1 = (f32[26,48,768]{2,1,0:T(8,128)}, f32[16,768]{1,0:T(8,128)}, bf16[1024,768]{1,0:T(8,128)(2,1)}, bf16[1024,768]{1,0:T(8,128)(2,1)}) custom-call(bf16[1024,768]{1,0:T(8,128)(2,1)} %get-tuple-element.28.cot_ref, bf16[1024,768]{1,0:T(8,128)(2,1)} %get-tuple-element.29.done_ref, s32[8,128]{1,0:T(8,128)} %get-tuple-element.30.length_ref, ...), custom_call_target="tpu_custom_call" | custom-call | tf_op jit(solution)/shard_map/back/pallas_call | solution.py:836
  381.5 1.8 fusion.1
  383.3 0.1 reverse_bitcast_fusion
  383.4 1.1 copy.43
  384.5 1.2 slice.66
  385.7 0.6 copy.39
  386.3 0.2 reverse_bitcast_fusion.1
  386.5 1.5 reshape.61
  388.1 0.0 copy-start.1
  388.1 1.1 slice.63
  389.2 1.0 slice_bitcast_fusion
  390.2 0.7 reverse_bitcast_fusion.2
  390.9 0.8 dynamic-slice.1
  391.7 0.6 fusion.2
  392.3 1.3 constant_dynamic-slice_fusion
  393.6 0.0 copy-done.1
  393.6 0.0 copy-start
  393.6 1.1 copy.47
  394.7 0.8 copy-done
  395.6 1.1 copy.48
Async XLA Ops:
  388.1 5.5 %copy-start.1 = (bf16[1024,768]{1,0:T(8,128)(2,1)S(1)}, bf16[1024,768]{1,0:T(8,128)(2,1)}, u32[]{:S(2)}) copy-start(bf16[1024,768]{1,0:T(8,128)(2,1)} %get-tuple-element.41) | copy-start | bytes 4718596
  393.6 2.0 copy-start

commit v4 on v3

--- a/solution.py
+++ b/solution.py
@@ -20,7 +20,7 @@
 LANES = 128
 BF16 = jnp.bfloat16
 F32 = jnp.float32
-VMEM_LIMIT = 62 * 2**20
+VMEM_LIMIT = 63 * 2**20 + 3 * 2**18
 ANY = pl.BlockSpec(memory_space=pl.ANY)
 
 
@@ -45,6 +45,10 @@
     return pl.BlockSpec(shape, lambda *_: zeros, pipeline_mode=pl.Buffered(1))
 
 
+def pick(ref, which):
+    return jnp.where(which == 0, ref[0:1, :], ref[1:2, :]).astype(F32)
+
+
 def norm(hidden, gain, bias):
     centred = hidden - jnp.mean(hidden, -1, keepdims=True)
     inverse = lax.rsqrt(jnp.mean(centred * centred, -1, keepdims=True) + EPSILON)
@@ -95,7 +99,7 @@
     triple_ref, merge_ref, up_ref, down_ref,
     normed_ref, scaled_ref, inverse_ref, query_ref, mixed_ref, total_ref, exp_ref, act_ref, slope_ref, kv_ref,
     out_ref, cot_out_ref, length_out_ref,
-    hidden, arrived, length_here, queries, kv, values, mixes, triple, merge, up, down,
+    hidden, arrived, length_mine, length_here, queries, kv, values, mixes, triple, merge, up, down,
     weight_sem, kv_sem, kv_send, kv_recv, free_sem, swap_send, swap_recv, here_sem,
 ):
     t = pl.program_id(0)
@@ -115,7 +119,7 @@
             rows = pl.ds(i * TILE, TILE)
             ends = stream_ref.at[rows, :], arrived.at[rows, :]
         else:
-            ends = ((cot_ref, cot_out_ref), (length_ref, length_here))[i - QKV_STEPS]
+            ends = ((cot_ref, cot_out_ref), (length_mine, length_here))[i - QKV_STEPS]
         return (
             send(*ends, swap_send.at[i], swap_recv.at[i], diagonal),
             pltpu.make_async_copy(*ends, here_sem.at[i]),
@@ -148,6 +152,7 @@
             pl.semaphore_signal(barrier, inc=1, device_id=diagonal, device_id_type=MESH)
 
         pl.semaphore_wait(barrier, 1 + jnp.where(swapped, 1, 0))
+        length_mine[...] = jnp.full(length_mine.shape, length_ref[0], jnp.int32)
         move(QKV_STEPS + 1, "start")
         for i in range(QKV_STEPS):
             move(i, "start")
@@ -177,7 +182,7 @@
 
         @pl.when(layer == 0)
         def _():
-            hidden[rows, :] = arrived[rows, :].astype(F32) + embed_ref[...]
+            hidden[rows, :] = arrived[rows, :].astype(F32) + pick(embed_ref, core)
 
         @pl.when(j == 0)
         def _():
@@ -187,7 +192,9 @@
         def _():
             pl.semaphore_wait(free_sem, 1)
 
-        normed, scaled, inverse = norm(hidden[rows, :], first_gain_ref[0], first_bias_ref[0])
+        normed, scaled, inverse = norm(
+            hidden[rows, :], pick(first_gain_ref, layer), pick(first_bias_ref, layer)
+        )
         normed_ref[0, 0] = normed
         scaled_ref[0, 0] = scaled.astype(BF16)
         inverse_ref[0, 0] = inverse
@@ -292,7 +299,7 @@
                 weight_copies(which, layer).wait()
 
         mid = hidden[rows, :] + dot(mixes[rows, :], merge[...])
-        normed, scaled, inverse = norm(mid, second_gain_ref[0], second_bias_ref[0])
+        normed, scaled, inverse = norm(mid, pick(second_gain_ref, layer), pick(second_bias_ref, layer))
         normed_ref[0, 0] = normed
         scaled_ref[0, 0] = scaled.astype(BF16)
         inverse_ref[0, 0] = inverse
@@ -354,13 +361,13 @@
         layer, j = phase(t)
         return layer, jnp.maximum(j - QKV_STEPS - PAIRS, 0), 0
 
-    vector = pl.BlockSpec((1, 1, width), lambda t: (t // FORWARD, 0, 0))
+    vector = whole((layers, width))
     rows = pl.BlockSpec((1, 1, TILE, width), row_tile)
     dma = pltpu.SemaphoreType.DMA
     return pl.pallas_call(
         functools.partial(forward_kernel, layers),
         grid=(layers * FORWARD,),
-        in_specs=[ANY, ANY, whole(length.shape), whole((1, width)), vector, vector, vector, vector, ANY, ANY, ANY, ANY],
+        in_specs=[ANY, ANY, pl.BlockSpec(memory_space=pltpu.SMEM), whole(embed.shape), vector, vector, vector, vector, ANY, ANY, ANY, ANY],
         out_specs=[
             rows, rows, pl.BlockSpec((1, 1, TILE, 1), row_tile),
             pl.BlockSpec((1, TILE, width), query_tile),
@@ -370,7 +377,7 @@
             pl.BlockSpec((1, TILE, units), ffn_tile), pl.BlockSpec((1, TILE, units), ffn_tile),
             ANY,
             pl.BlockSpec((TILE, width), lambda t: (jnp.where(phase(t)[0] == layers - 1, ffn_tile(t)[1], 0), 0)),
-            ANY, whole(length.shape),
+            ANY, whole((8, LANES)),
         ],
         out_shape=[
             sds((layers, 2, tokens, width), BF16),
@@ -385,12 +392,13 @@
             sds((layers, blocks, 2, BLOCK, 2 * width), BF16),
             sds((tokens, width), BF16),
             sds((tokens, width), BF16),
-            sds(length.shape, jnp.int32),
+            sds((8, LANES), jnp.int32),
         ],
         scratch_shapes=[
             pltpu.VMEM((tokens, width), F32),
             pltpu.VMEM((tokens, width), BF16),
-            pltpu.VMEM(length.shape, jnp.int32),
+            pltpu.VMEM((8, LANES), jnp.int32),
+            pltpu.VMEM((8, LANES), jnp.int32),
             pltpu.VMEM((tokens, width), BF16),
             pltpu.VMEM((blocks, 2, BLOCK, 2 * width), BF16),
             pltpu.VMEM((2 * tokens, 2 * LANES), BF16),
@@ -408,8 +416,8 @@
 
 
 FFN_STEPS = 4
-STEPS = FFN_STEPS + PAIRS + 3
-NO_PIECE = 9
+STEPS = FFN_STEPS + PAIRS + 4
+PIECES = STEPS - 2
 STAGES = 5
 ROWS = 16
 SHARE = 48
@@ -420,12 +428,19 @@
     layers, hosted,
     cot_ref, done_ref, length_ref, act_ref, slope_ref, normed_ref, scaled_ref, inverse_ref, mixed_ref, up_ref, down_ref, merge_ref,
     first_gain_ref, second_gain_ref, query_ref, key_ref, value_ref, total_ref, exp_ref, weight_ref,
-    out_ref, small_ref, input_ref, output_ref,
-    grad, low, total, grads, pending, landing, exps,
-    staged, sums0, sums1, sums2, sums3, got0, got1, got2, got3, got4, final, small, small_got,
-    exp_sem, cot_sem, kv_send, kv_recv, stage_send, stage_recv, out_sem, small_send, small_recv, swap_send, swap_recv,
-    here_sem,
+    *refs,
 ):
+    outs = refs[: 4 if hosted else 1]
+    (
+        small_ref, input_ref, output_ref,
+        grad, total, grads, pending, landing, exps,
+        staged, left0, left1, left2, left3, right0, right1, right2, right3, got0,
+        got_left1, got_left2, got_left3, got_left4, got_right1, got_right2, got_right3, got_late,
+        final, small, small_got,
+        exp_sem, cot_sem, kv_send, kv_recv, core_send, core_recv, left_send, left_recv, right_send, right_recv,
+        late_send, late_recv, out_sem, small_send, small_recv, swap_send, swap_recv, here_sem,
+    ) = refs[len(outs) :]
+    low = grads.at[1]
     t = pl.program_id(0)
     j = t % STEPS
     layer = layers - 1 - t // STEPS
@@ -466,7 +481,8 @@
 
 
     def exp_copy(head):
-        return pltpu.make_async_copy(exp_ref.at[layer, head], exps.at[head % 2], exp_sem.at[head % 2])
+        at = (head // 2) % 2, head % 2
+        return pltpu.make_async_copy(exp_ref.at[layer, head], exps.at[at], exp_sem.at[at])
 
     def put(slot, r, value):
         staged[slot, r % 2, (r // 2) % 2, (r // 4) % 2, (r // 8) % 2] = value
@@ -493,12 +509,13 @@
         @pl.when(j == FFN_STEPS - 1)
         def _():
             exp_copy(0).start()
+            exp_copy(1).start()
 
             def rows(i, sums):
                 at = pl.ds(pl.multiple_of(i * TILE, TILE), TILE)
                 part = total[at, :]
                 scaled = scaled_ref[0, 0, at, :].astype(F32)
-                mid = grad[at, :] + norm_back(part, scaled, inverse_ref[0, 0, at, :], second_gain_ref[0])
+                mid = grad[at, :] + norm_back(part, scaled, inverse_ref[0, 0, at, :], pick(second_gain_ref, layer))
                 grad[at, :] = mid
                 low_mid = mid.astype(BF16)
                 low[at, :] = low_mid
@@ -553,7 +570,7 @@
 
         def score_grad(head, block, grad_prob):
             start = tile_index(blocks, block, block)
-            prob = exps[head, start : start + blocks - block].reshape(tokens - block * BLOCK, pair)
+            prob = exps[p % 2, head, start : start + blocks - block].reshape(tokens - block * BLOCK, pair)
             return prob, (prob.astype(F32) * (grad_prob - inner[head][block * BLOCK :])).astype(BF16)
 
         sums = {}
@@ -577,10 +594,15 @@
                 grads[1 + which, at, lanes] = jnp.where(core == 0, zero, one).astype(BF16)
                 pending[p % 2, which, at, :] = jnp.where(core == 0, one, zero).astype(BF16)
 
-        exp_copy(2 * p + 1).start()
         exp_copy(2 * p).wait()
         exp_copy(2 * p + 1).wait()
-        items = [(head, block) for head in range(2) for block in range(blocks)]
+
+        @pl.when(p < PAIRS - 1)
+        def _():
+            exp_copy(2 * p + 2).start()
+            exp_copy(2 * p + 3).start()
+
+        items = [(head, block) for block in range(blocks) for head in range(2)]
         ahead = probs_grad(*items[0])
         behind = None
         for n, item in enumerate(items):
@@ -593,10 +615,6 @@
             behind = (*item, *both)
         products(*behind)
 
-        @pl.when(p < PAIRS - 1)
-        def _():
-            exp_copy(2 * p + 2).start()
-
         grads[0, :, lanes] = (
             jnp.where(lane < HEAD_DIM, total[:, :LANES], total[:, LANES : 2 * LANES]) * SCALE
         ).astype(BF16)
@@ -608,31 +626,32 @@
         kv_copy(p).start()
 
 
+    @pl.when(busy & (j == FFN_STEPS + PAIRS))
+    def _():
+        total[...] = jnp.zeros_like(total)
+        take(PAIRS - 1)
+
     @pl.when(busy & (j >= FFN_STEPS + PAIRS))
     def _():
         n = j - FFN_STEPS - PAIRS
 
-        @pl.when(n == 0)
-        def _():
-            total[...] = jnp.zeros_like(total)
-
-        @pl.when(n == 0)
-        def _():
-            take(PAIRS - 1)
-
-        part = grads[n]
-        triple_grad = dot(normed_ref[0, 0], part, TN).astype(BF16)
-        for r in range(ROWS):
-            put(4 + n, r, triple_grad[r * SHARE : (r + 1) * SHARE])
-        total[...] += dot(part, weight_ref[0], NT)
-
-        @pl.when(n == 2)
+        @pl.when(n < 3)
+        def _():
+            triple_grad = dot(normed_ref[0, 0], grads[n], TN).astype(BF16)
+            for r in range(ROWS):
+                put(4 + n, r, triple_grad[r * SHARE : (r + 1) * SHARE])
+
+        @pl.when(n > 0)
+        def _():
+            total[...] += dot(grads[n - 1], weight_ref[0], NT)
+
+        @pl.when(n == 3)
         def _():
             def rows(i, sums):
                 at = pl.ds(pl.multiple_of(i * TILE, TILE), TILE)
                 part = total[at, :]
                 scaled = scaled_ref[0, 0, at, :].astype(F32)
-                hidden = grad[at, :] + norm_back(part, scaled, inverse_ref[0, 0, at, :], first_gain_ref[0])
+                hidden = grad[at, :] + norm_back(part, scaled, inverse_ref[0, 0, at, :], pick(first_gain_ref, layer))
                 grad[at, :] = hidden
                 low[at, :] = hidden.astype(BF16)
                 return (
@@ -652,6 +671,7 @@
 
 
     last = layers * STEPS - 1
+    half_width = width // 2
 
     def slot(v):
         i = v % STEPS
@@ -660,72 +680,156 @@
         )
 
     def whether(v):
-        return (v >= 0) & (v <= last) & (v % STEPS != NO_PIECE)
-
-    def half(v):
-        return (v - v // STEPS - jnp.where(v % STEPS > NO_PIECE, 1, 0)) % 2
-
-    def out_copy(v):
-        h = half(v)
-        return pltpu.make_async_copy(final.at[h], out_ref.at[v], out_sem.at[h])
-
-    def stage(s, v):
-        h = half(v)
-        src = (staged.at[slot(v), 1 - core], sums0.at[h, 1 - x], sums1.at[h, 1 - z0], sums2.at[h, 1 - z1], sums3.at[h])[s]
-        dst = (got0, got1, got2, got3, got4)[s].at[h]
-        return send(src, dst, stage_send.at[s, h], stage_recv.at[s, h], mates[s])
+        return (v >= 0) & (v <= last) & (v % STEPS != FFN_STEPS + PAIRS - 1) & (v % STEPS != STEPS - 1)
+
+    def order(v):
+        i = v % STEPS
+        return v // STEPS * PIECES + i - jnp.where(i >= FFN_STEPS + PAIRS, 1, 0)
 
     def add(a, b):
         return (a.astype(F32) + b.astype(F32)).astype(BF16)
 
+    def core_stage(v):
+        h = order(v) % 2
+        return send(staged.at[slot(v), 1 - core], got0.at[h], core_send.at[h], core_recv.at[h], mates[0])
+
+    def left_stage(s, v):
+        h = order(v) % 2
+        src = (left0.at[h, 1 - x], left1.at[h, 1 - z0], left2.at[h, 1 - z1], left3.at[h])[s - 1]
+        dst = (got_left1, got_left2, got_left3, got_left4)[s - 1].at[h]
+        return send(src, dst, left_send.at[s - 1, h], left_recv.at[s - 1, h], mates[s])
+
+    def right_stage(s, v):
+        h = order(v) % 2
+        src = (right0.at[h, 1 - own_pass], right1.at[h, 1 - z0], right2.at[h, 1 - z1])[s - 1]
+        dst = (got_right1, got_right2, got_right3)[s - 1].at[h]
+        return send(src, dst, right_send.at[s - 1, h], right_recv.at[s - 1, h], (mates[4], mates[2], mates[3])[s - 1])
+
+    def late_stage(s, v):
+        k = order(v)
+        return send(right3.at[k % 2], got_late.at[k], late_send.at[s - 4, k], late_recv.at[s - 4, k], (mates[1], mates[4])[s - 4])
+
+    keeps = x == own_pass
+
+    def late_start(s, v):
+        @pl.when(keeps == (s == 5))
+        def _():
+            late_stage(s, v).start()
+
+    def late_wait(s, v, receive):
+        @pl.when(keeps == (s == 5))
+        def _():
+            late_stage(s, v).wait_send()
+
+        @pl.when(keeps != (s == 5))
+        def _():
+            late_stage(s, v).wait_recv()
+            receive()
+
+    def out_copies(v, act):
+        h = order(v) % 2
+        i = v % STEPS
+        at_layer = layers - 1 - v // STEPS
+        triple_out, merge_out, up_out, down_out = outs
+
+        def columns(n):
+            return pl.ds(pl.multiple_of(n * width, width), width)
+
+        def go(target):
+            getattr(pltpu.make_async_copy(final.at[h], target, out_sem.at[h]), act)()
+
+        @pl.when(i < 4)
+        def _():
+            go(up_out.at[at_layer, :, columns(i)])
+
+        @pl.when((i >= 4) & (i < 8))
+        def _():
+            go(down_out.at[at_layer, pl.ds(pl.multiple_of((i - 4) * SHARE, SHARE), SHARE), :])
+
+        @pl.when(i == 8)
+        def _():
+            go(merge_out.at[at_layer])
+
+        @pl.when(i >= FFN_STEPS + PAIRS)
+        def _():
+            go(triple_out.at[at_layer, :, columns(i - FFN_STEPS - PAIRS)])
+
     if hosted:
+        @pl.when(whether(t - 7))
+        def _():
+            out_copies(t - 7, "wait")
+
         @pl.when(whether(t - 6))
         def _():
-            out_copy(t - 6).wait()
+            v = t - 6
+            h = order(v) % 2
+
+            def receive():
+                right3[h] = got_late[order(v)]
+
+            late_wait(5, v, receive)
+            final[h, :, half_width:] = right3[h].astype(F32)
+            out_copies(v, "start")
 
         @pl.when(whether(t - 5))
         def _():
             v = t - 5
-            h = half(v)
-            stage(4, v).wait()
-            final[h] = sums3[h].astype(F32) + got4[h].astype(F32)
-            out_copy(v).start()
+            h = order(v) % 2
+
+            def receive():
+                right3[h] = add(right3[h], got_late[order(v)])
+
+            late_wait(4, v, receive)
+            late_start(5, v)
+            left_stage(4, v).wait()
+            final[h, :, :half_width] = left3[h].astype(F32) + got_left4[h].astype(F32)
 
         @pl.when(whether(t - 4))
         def _():
             v = t - 4
-            h = half(v)
-            stage(3, v).wait()
-            sums3[h] = add(sums2[h, z1], got3[h])
-            stage(4, v).start()
+            h = order(v) % 2
+            right_stage(3, v).wait()
+            right3[h] = add(right2[h, z1], got_right3[h])
+            late_start(4, v)
+            left_stage(3, v).wait()
+            left3[h] = add(left2[h, z1], got_left3[h])
+            left_stage(4, v).start()
 
         @pl.when(whether(t - 3))
         def _():
             v = t - 3
-            h = half(v)
-            stage(2, v).wait()
-            sums2[h] = add(sums1[h, z0], got2[h])
-            stage(3, v).start()
+            h = order(v) % 2
+            right_stage(2, v).wait()
+            right2[h] = add(right1[h, z0], got_right2[h])
+            right_stage(3, v).start()
+            left_stage(2, v).wait()
+            left2[h] = add(left1[h, z0], got_left2[h])
+            left_stage(3, v).start()
 
         @pl.when(whether(t - 2))
         def _():
             v = t - 2
-            h = half(v)
-            stage(1, v).wait()
-            sums1[h] = add(sums0[h, x], got1[h])
-            stage(2, v).start()
+            h = order(v) % 2
+            right_stage(1, v).wait()
+            right1[h] = add(right0[h, own_pass], got_right1[h])
+            right_stage(2, v).start()
+            left_stage(1, v).wait()
+            left1[h] = add(left0[h, x], got_left1[h])
+            left_stage(2, v).start()
 
         @pl.when(whether(t - 1))
         def _():
             v = t - 1
-            h = half(v)
-            stage(0, v).wait()
-            sums0[h] = add(staged[slot(v), core], got0[h])
-            stage(1, v).start()
+            h = order(v) % 2
+            core_stage(v).wait()
+            right0[h] = add(staged[slot(v), core, :, :, :, :, half_width:], got0[h, :, :, :, :, half_width:])
+            right_stage(1, v).start()
+            left0[h] = add(staged[slot(v), core, :, :, :, :, :half_width], got0[h, :, :, :, :, :half_width])
+            left_stage(1, v).start()
 
         @pl.when(whether(t))
         def _():
-            stage(0, t).start()
+            core_stage(t).start()
 
         for s in range(STAGES + 1):
             def small_copy(s):
@@ -740,7 +844,7 @@
                     small_copy(s).start()
     else:
         def piece_copy(v):
-            return pltpu.make_async_copy(staged.at[slot(v)], out_ref.at[v], out_sem.at[v % 2])
+            return pltpu.make_async_copy(staged.at[slot(v)], outs[0].at[v], out_sem.at[v % 2])
 
         @pl.when(whether(t - 1))
         def _():
@@ -781,8 +885,10 @@
          total, exps, weight, hosted):
     layers, tokens, width = query.shape
     tiles = exps.shape[2]
-    steps = layers * STEPS + (STAGES + 2 if hosted else 1)
+    steps = layers * STEPS + (STAGES + 1 if hosted else 1)
     piece = (2, 2, 2, 2, SHARE, width)
+    part = (2, 2, 2, SHARE, width // 2)
+    count = layers * PIECES
 
     def at(t):
         t = jnp.minimum(t, layers * STEPS - 1)
@@ -798,7 +904,7 @@
 
     def part_of(t):
         layer, j = at(t)
-        return layer, jnp.clip(j - FFN_STEPS - PAIRS, 0, 2)
+        return layer, jnp.clip(j - FFN_STEPS - PAIRS - 1, 0, 2)
 
     def kind_of(t):
         layer, j = at(t)
@@ -819,7 +925,7 @@
         pl.BlockSpec((1, width, width), lambda t: (tile_of(t)[0], 0, tile_of(t)[1])),
         pl.BlockSpec((1, width, width), lambda t: (tile_of(t)[0], tile_of(t)[1], 0)),
         of_layer((width, width)),
-        of_layer((1, width)), of_layer((1, width)),
+        whole((layers, width)), whole((layers, width)),
         pl.BlockSpec((1, tokens, LANES), lambda t: (head_of(t)[0], 0, head_of(t)[1])),
         pl.BlockSpec((1, 2 * tokens, LANES), lambda t: (head_of(t)[0], 0, head_of(t)[1])),
         pl.BlockSpec((1, 2 * tokens, LANES), lambda t: (head_of(t)[0], 0, head_of(t)[1] + PAIRS)),
@@ -827,7 +933,13 @@
         ANY,
         pl.BlockSpec((1, width, width), lambda t: (part_of(t)[0], 0, part_of(t)[1]), **once),
     ]
-    out_piece = sds((layers * STEPS, SHARE, width), F32) if hosted else sds((layers * STEPS,) + piece, BF16)
+    if hosted:
+        shapes = [
+            sds((layers, SHARE, 3 * width), F32), sds((layers, SHARE, width), F32),
+            sds((layers, SHARE, FFN_STEPS * width), F32), sds((layers, 4 * SHARE, width), F32),
+        ]
+    else:
+        shapes = [sds((layers * STEPS,) + piece, BF16)]
     dma = pltpu.SemaphoreType.DMA
 
     def some(*shape):
@@ -837,25 +949,28 @@
         functools.partial(back_kernel, layers, hosted),
         grid=(steps,),
         in_specs=in_specs,
-        out_specs=[ANY, whole((SMALL, width)), ANY, ANY],
-        out_shape=[
-            out_piece, sds((SMALL, width), F32), sds((tokens, width), BF16), sds((tokens, width), BF16),
+        out_specs=[ANY] * len(shapes) + [whole((SMALL, width)), ANY, ANY],
+        out_shape=shapes + [
+            sds((SMALL, width), F32), sds((tokens, width), BF16), sds((tokens, width), BF16),
         ],
         scratch_shapes=[
             pltpu.VMEM((tokens, width), F32),
-            some(tokens, width),
             pltpu.VMEM((tokens, width), F32),
             some(3, tokens, width),
             some(2, 2, tokens, LANES),
             some(2, 2, tokens, LANES),
-            some(2, tiles, BLOCK, 2 * BLOCK),
+            some(2, 2, tiles, BLOCK, 2 * BLOCK),
             some(7, *piece),
-            some(2, *piece[1:]), some(2, *piece[2:]), some(2, *piece[3:]), some(2, *piece[4:]),
-            some(2, *piece[1:]), some(2, *piece[2:]), some(2, *piece[3:]), some(2, *piece[4:]), some(2, *piece[4:]),
+            some(2, *part), some(2, *part[1:]), some(2, *part[2:]), some(2, *part[3:]),
+            some(2, *part), some(2, *part[1:]), some(2, *part[2:]), some(2, *part[3:]),
+            some(2, *piece[1:]),
+            some(2, *part[1:]), some(2, *part[2:]), some(2, *part[3:]), some(2, *part[3:]),
+            some(2, *part[1:]), some(2, *part[2:]), some(2, *part[3:]), some(count, *part[3:]),
             pltpu.VMEM((2, SHARE, width), F32),
             pltpu.VMEM((SMALL, width), F32),
             pltpu.VMEM((STAGES, SMALL, width), F32),
-            dma((2,)), dma, dma((2,)), dma((2,)), dma((STAGES, 2)), dma((STAGES, 2)), dma((2,)),
+            dma((2, 2)), dma, dma((2,)), dma((2,)), dma((2,)), dma((2,)), dma((4, 2)), dma((4, 2)), dma((3, 2)), dma((3, 2)),
+            dma((2, count)), dma((2, count)), dma((2,)),
             dma((STAGES,)), dma((STAGES,)), dma((2,)), dma((2,)), dma((2,)),
         ],
         compiler_params=params(1),
@@ -870,51 +985,36 @@
 ):
     row_count = lax.axis_size("rows")
     own_row = lax.axis_index("rows")
-    core = own_row % 2
     tokens, width = stream.shape[2], stream.shape[3]
     layers = triple_weight.shape[0]
     hosted = row_count == ROWS
 
-    embed = jnp.where(core == 0, pass_embed[0:1], pass_embed[1:2]).astype(F32)
-    first_gain, first_bias, second_gain, second_bias = (
-        v.astype(F32)[:, None] for v in (first_gain, first_bias, second_gain, second_bias)
-    )
     (normeds, scaleds, inverses, query, mixed, total, exps, act, slope, kv, done, cotangent, length) = forward(
-        stream.reshape(tokens, width), cotangent.reshape(tokens, width),
-        jnp.broadcast_to(lengths.reshape(1, 1), (8, LANES)), embed,
+        stream.reshape(tokens, width), cotangent.reshape(tokens, width), lengths, pass_embed,
         first_gain, first_bias, second_gain, second_bias, triple_weight, merge_weight, up_weight, down_weight,
     )
-    pieces, small, input_grad, output = back(
+    *weight_grads, small, input_grad, output = back(
         cotangent, done, length, act, slope, normeds, scaleds, inverses, mixed, up_weight, down_weight, merge_weight,
         first_gain, second_gain, query, kv.reshape(layers, 2 * tokens, 2 * width), total, exps, triple_weight, hosted,
     )
     input_grad = input_grad.reshape(stream.shape)
     output = output.reshape(stream.shape)
     if hosted:
-        pieces = pieces.reshape(layers, STEPS, SHARE, width)
+        triple_grad, merge_grad, up_grad, down_grad = weight_grads
     else:
-        pieces = pieces.reshape(layers, STEPS, 2, 2, 2, 2, SHARE, width).transpose(0, 1, 5, 4, 3, 2, 6, 7)
-    pieces = pieces[::-1]
-
-    def columns(first, last):
-        some = pieces[:, first:last]
-        some = some.reshape(layers, last - first, -1, width)
-        return some.transpose(0, 2, 1, 3).reshape(layers, -1, (last - first) * width)
-
-    up_grad = columns(0, 4)
-    merge_grad = columns(8, 9)
-    triple_grad = columns(10, 13)
-    down_grad = pieces[:, 4:8]
-    if hosted:
-        down_grad = down_grad.reshape(layers, 4 * SHARE, width)
-    else:
-        down_grad = down_grad.reshape(layers, 4, ROWS, SHARE, width).transpose(0, 2, 1, 3, 4).reshape(layers, -1, width)
+        pieces = weight_grads[0].transpose(0, 4, 3, 2, 1, 5, 6).reshape(layers, STEPS, -1, width)[::-1]
+
+        def columns(first, last):
+            return pieces[:, first:last].transpose(0, 2, 1, 3).reshape(layers, -1, (last - first) * width)
 
         def reduce(gradient):
             share = lax.psum_scatter(gradient, "rows", scatter_dimension=1, tiled=True)
             return lax.psum(share, "pass").astype(F32)
 
-        up_grad, merge_grad, triple_grad, down_grad = map(reduce, (up_grad, merge_grad, triple_grad, down_grad))
+        down_grad = pieces[:, 4:8].reshape(layers, 4, ROWS, SHARE, width).transpose(0, 2, 1, 3, 4)
+        triple_grad, merge_grad, up_grad, down_grad = map(
+            reduce, (columns(10, 13), columns(8, 9), columns(0, 4), down_grad.reshape(layers, -1, width))
+        )
         small = lax.psum(small, ("pass", "rows"))
     share = width // row_count
     small = lax.dynamic_slice_in_dim(small, own_row * share, share, 1)

time: 398 us -> 379 us (0.952)
  local copies, waits for them, and re-layouts: 20.9 us -> 10.9 us
  Pallas kernels: 373 us -> 366 us
    pallas_call x1, Pallas kernels: 244 us -> 238 us  [back(): pl.pallas_call(functools.partial(back_kernel, layers, hosted), grid=(step...]
    broadcast_in_dim x5 -> x0, local copies, waits for them, and re-layouts: 5.72 us -> none  [the longest x4 5.12 us: local(): v.astype(F32)[:, None]]
    slice x3 -> x0, local copies, waits for them, and re-layouts: 4.11 us -> none  [the longest x2 2.89 us: local(): down_grad = pieces[:, 4:8]]
    unnamed x9 -> x16, local copies, waits for them, and re-layouts: 4.79 us -> 8.04 us
where the time goes in v4:
time: 379 us; the launch traced here: 378 us
  Pallas kernels  366 us (97%)
  local copies, waits for them, and re-layouts  10.9 us (3%)
    pallas_call x1, Pallas kernels, back(): pl.pallas_call(functools.partial(back_kernel, layers, hosted), grid=(step...  238 us
    pallas_call x1, Pallas kernels, forward(): pl.pallas_call(functools.partial(forward_kernel, layers), grid=(layers *...  128 us
    unnamed x16, local copies, waits for them, and re-layouts  8.04 us

profile of v4, /device:TPU:0, one launch (start us, length us, event | category | flops | bytes accessed | tf_op | source)
XLA Modules:
  0.0 378.4 jit_solution(16502847262523991750)
XLA Ops:
  1.3 128.0 %forward.1 = (bf16[2,2,1024,768]{3,2,1,0:T(8,128)(2,1)}, bf16[2,2,1024,768]{3,2,1,0:T(8,128)(2,1)}, f32[2,2,1024,1]{3,2,1,0:T(8,128)}, bf16[2,1024,768]{2,1,0:T(...) custom-call(bf16[1024,768]{1,0:T(8,128)(2,1)} %bitcast.20, ...), custom_call_target="tpu_custom_call" | custom-call | tf_op jit(solution)/shard_map/forward/pallas_call | solution.py:367
  129.3 238.2 %back.1 = (f32[2,48,2304]{2,1,0:T(8,128)}, f32[2,48,768]{2,1,0:T(8,128)}, f32[2,48,3072]{2,1,0:T(8,128)}, f32[2,192,768]{2,1,0:T(8,128)}, f32[16,768]{1,0:T(8,12...) custom-call(bf16[1024,768]{1,0:T(8,128)(2,1)} %get-tuple-element.31.cot_ref, ...), custom_call_target="tpu_custom_call" | custom-call | tf_op jit(solution)/shard_map/back/pallas_call | solution.py:948
  367.5 0.0 copy-start
  367.5 0.9 dynamic-slice.1
  368.4 0.6 fusion
  369.0 1.3 constant_dynamic-slice_fusion
  370.3 2.7 copy.38
  373.0 0.0 copy-done
  373.0 0.0 copy-start.3
  373.0 0.0 copy-start.4
  373.0 0.0 copy-start.2
  373.0 1.1 copy.39
  374.1 0.6 copy-done.3
  374.7 0.0 copy-start.1
  374.7 0.9 copy.40
  375.6 0.0 copy-done.4
  375.6 0.7 copy.41
  376.3 0.0 copy-done.2
  376.3 1.0 copy.42
  377.3 0.0 copy-done.1
  377.3 1.0 copy.43
Async XLA Ops:
  367.5 5.5 %copy-start = (bf16[1024,768]{1,0:T(8,128)(2,1)S(1)}, bf16[1024,768]{1,0:T(8,128)(2,1)}, u32[]{:S(2)}) copy-start(bf16[1024,768]{1,0:T(8,128)(2,1)} %get-tuple-element.45) | copy-start | bytes 4718596
  373.0 1.7 copy-start.3
  373.0 2.6 copy-start.4
  373.0 3.4 copy-start.2
  374.7 2.6 copy-start.1

commit v5 on v4

--- a/solution.py
+++ b/solution.py
@@ -257,9 +257,9 @@
 
         def mix(block, head, exps):
             both = dot(exps, values[: (block + 1) * pair, :])
-            inverse = jnp.where(block * BLOCK < length, 1.0 / both[:, LANES : LANES + 1], 0.0)
+            inverse = jnp.where(block * BLOCK < length, 1.0 / both[:, LANES:], 0.0)
             rows = pl.ds(block * BLOCK, BLOCK)
-            total_ref[0, 0, rows, head : head + 1] = inverse
+            total_ref[0, 0, head : head + 1, rows] = inverse.T[:1]
             outs[head] = both[:, :LANES] * inverse
             if head == 1:
                 value = jnp.where(lane < HEAD_DIM, outs[0], outs[1]).astype(BF16)
@@ -372,7 +372,7 @@
             rows, rows, pl.BlockSpec((1, 1, TILE, 1), row_tile),
             pl.BlockSpec((1, TILE, width), query_tile),
             pl.BlockSpec((1, tokens, LANES), lambda t: (head(t)[0], 0, head(t)[1])),
-            pl.BlockSpec((1, 1, tokens, 2), lambda t: (*head(t), 0, 0)),
+            pl.BlockSpec((1, 1, 8, tokens), lambda t: (*head(t), 0, 0)),
             pl.BlockSpec((1, 2, tiles, BLOCK, 2 * BLOCK), lambda t: (*head(t), 0, 0, 0)),
             pl.BlockSpec((1, TILE, units), ffn_tile), pl.BlockSpec((1, TILE, units), ffn_tile),
             ANY,
@@ -385,7 +385,7 @@
             sds((layers, 2, tokens, 1), F32),
             sds((layers, tokens, width), BF16),
             sds((layers, tokens, width), BF16),
-            sds((layers, PAIRS, tokens, 2), F32),
+            sds((layers, PAIRS, 8, tokens), F32),
             sds((layers, 2 * PAIRS, tiles, BLOCK, 2 * BLOCK), BF16),
             sds((layers, tokens, units), BF16),
             sds((layers, tokens, units), BF16),
@@ -426,18 +426,19 @@
 
 def back_kernel(
     layers, hosted,
-    cot_ref, done_ref, length_ref, act_ref, slope_ref, normed_ref, scaled_ref, inverse_ref, mixed_ref, up_ref, down_ref, merge_ref,
-    first_gain_ref, second_gain_ref, query_ref, key_ref, value_ref, total_ref, exp_ref, weight_ref,
+    cot_ref, done_ref, length_ref, act_ref, slope_ref, normeds_ref, scaleds_ref, inverses_ref, mixes_ref, up_ref, down_ref,
+    merges_ref,
+    first_gain_ref, second_gain_ref, query_ref, key_ref, value_ref, total_ref, exp_ref, triples_ref,
     *refs,
 ):
     outs = refs[: 4 if hosted else 1]
     (
         small_ref, input_ref, output_ref,
-        grad, total, grads, pending, landing, exps,
+        normed_ref, scaled_ref, inverse_ref, mixed_ref, weights, grad, total, grads, pending, landing, exps,
         staged, left0, left1, left2, left3, right0, right1, right2, right3, got0,
         got_left1, got_left2, got_left3, got_left4, got_right1, got_right2, got_right3, got_late,
         final, small, small_got,
-        exp_sem, cot_sem, kv_send, kv_recv, core_send, core_recv, left_send, left_recv, right_send, right_recv,
+        load_sem, exp_sem, cot_sem, kv_send, kv_recv, core_send, core_recv, left_send, left_recv, right_send, right_recv,
         late_send, late_recv, out_sem, small_send, small_recv, swap_send, swap_recv, here_sem,
     ) = refs[len(outs) :]
     low = grads.at[1]
@@ -480,6 +481,33 @@
         small[...] = jnp.zeros_like(small)
 
 
+    def load(what, of_layer):
+        def weight_part(n):
+            return triples_ref.at[of_layer, :, n * width : (n + 1) * width]
+
+        source, target, sem = (
+            (normeds_ref.at[of_layer, 0], normed_ref, 0), (scaleds_ref.at[of_layer, 0], scaled_ref, 1),
+            (inverses_ref.at[of_layer, 0], inverse_ref, 2), (mixes_ref.at[of_layer], mixed_ref, 3),
+            (normeds_ref.at[of_layer, 1], normed_ref, 0), (scaleds_ref.at[of_layer, 1], scaled_ref, 1),
+            (inverses_ref.at[of_layer, 1], inverse_ref, 2), (merges_ref.at[of_layer], weights.at[0], 4),
+            (weight_part(0), weights.at[1], 5), (weight_part(1), weights.at[0], 4), (weight_part(2), weights.at[1], 5),
+        )[what]
+        return pltpu.make_async_copy(source, target, load_sem.at[sem])
+
+    def fetch(*which, of_layer=layer, when=True):
+        @pl.when(when)
+        def _():
+            for what in which:
+                load(what, of_layer).start()
+
+    def have(*which):
+        for what in which:
+            load(what, layer).wait()
+
+    more = layer > 0
+    fetch(0, 1, 2, 3, 7, when=t == 0)
+
+
     def exp_copy(head):
         at = (head // 2) % 2, head % 2
         return pltpu.make_async_copy(exp_ref.at[layer, head], exps.at[at], exp_sem.at[at])
@@ -492,6 +520,7 @@
         @pl.when(j == 0)
         def _():
             total[...] = jnp.zeros_like(total)
+            have(0)
 
         grad_low = low[...]
         down_grad = dot(act_ref[0], grad_low, TN).astype(BF16)
@@ -501,7 +530,7 @@
                 staged[i, q % 2, q // 2, j % 2, (j // 2) % 2] = down_grad[first : first + SHARE]
         grad_act = dot(grad_low, down_ref[0], NT)
         grad_pre = (slope_ref[0].astype(F32) * grad_act).astype(BF16)
-        up_grad = dot(normed_ref[0, 0], grad_pre, TN).astype(BF16)
+        up_grad = dot(normed_ref[...], grad_pre, TN).astype(BF16)
         for r in range(ROWS):
             put(4 + j % 2, r, up_grad[r * SHARE : (r + 1) * SHARE])
         total[...] += dot(grad_pre, up_ref[0], NT)
@@ -510,16 +539,17 @@
         def _():
             exp_copy(0).start()
             exp_copy(1).start()
+            have(1, 2, 3, 7)
 
             def rows(i, sums):
                 at = pl.ds(pl.multiple_of(i * TILE, TILE), TILE)
                 part = total[at, :]
-                scaled = scaled_ref[0, 0, at, :].astype(F32)
-                mid = grad[at, :] + norm_back(part, scaled, inverse_ref[0, 0, at, :], pick(second_gain_ref, layer))
+                scaled = scaled_ref[at, :].astype(F32)
+                mid = grad[at, :] + norm_back(part, scaled, inverse_ref[at, :], pick(second_gain_ref, layer))
                 grad[at, :] = mid
                 low_mid = mid.astype(BF16)
                 low[at, :] = low_mid
-                grads[0, at, :] = dot(low_mid, merge_ref[0], NT).astype(BF16)
+                grads[0, at, :] = dot(low_mid, weights[0], NT).astype(BF16)
                 return (
                     sums[0] + jnp.sum(part * scaled, 0, keepdims=True),
                     sums[1] + jnp.sum(part, 0, keepdims=True),
@@ -529,9 +559,10 @@
             gain_sum, bias_sum = lax.fori_loop(0, tokens // TILE, rows, (empty, empty))
             small[pl.ds(4 + 4 * layer, 1), :] = gain_sum
             small[pl.ds(5 + 4 * layer, 1), :] = bias_sum
-            merge_grad = dot(mixed_ref[0], low[...], TN).astype(BF16)
+            merge_grad = dot(mixed_ref[...], low[...], TN).astype(BF16)
             for r in range(ROWS):
                 put(6, r, merge_grad[r * SHARE : (r + 1) * SHARE])
+            fetch(4, 5, 6, 8, 9)
 
 
     def kv_copy(p):
@@ -553,17 +584,22 @@
         lanes = pl.ds(pl.multiple_of(p * LANES, LANES), LANES)
         lane = lax.broadcasted_iota(jnp.int32, (tokens, LANES), 1)
         out_grad = grads[0, :, lanes].astype(F32)
-        product = out_grad * mixed_ref[0, :, lanes].astype(F32)
+        product = out_grad * mixed_ref[:, lanes].astype(F32)
         query = query_ref[0]
+        inverses = total_ref[0, 0].T
+        weighted = out_grad * jnp.where(lane < HEAD_DIM, inverses[:, :1], inverses[:, 1:2])
+        weighted_across = weighted.T.astype(BF16)
+        weighted = weighted.astype(BF16)
+        query_across = query.astype(F32).T.astype(BF16)
+        across = lax.broadcasted_iota(jnp.int32, (LANES, tokens), 0)
         scaled, scaled_across, inner, chosen_across = [], [], [], []
         for head in range(2):
             mine = lane // HEAD_DIM == head
-            inverse = total_ref[0, 0, :, head : head + 1]
-            part = jnp.where(mine, out_grad * inverse, 0.0)
-            scaled.append(part.astype(BF16))
-            scaled_across.append(part.T.astype(BF16))
-            inner.append(jnp.sum(jnp.where(mine, product, 0.0), -1, keepdims=True) * inverse)
-            chosen_across.append(jnp.where(mine, query, jnp.zeros_like(query)).astype(F32).T.astype(BF16))
+            mine_across = across // HEAD_DIM == head
+            scaled.append(jnp.where(mine, weighted, jnp.zeros_like(weighted)))
+            scaled_across.append(jnp.where(mine_across, weighted_across, jnp.zeros_like(weighted_across)))
+            chosen_across.append(jnp.where(mine_across, query_across, jnp.zeros_like(query_across)))
+            inner.append(jnp.sum(jnp.where(mine, product, 0.0), -1, keepdims=True) * inverses[:, head : head + 1])
 
         def probs_grad(head, block):
             return dot(scaled[head][block * BLOCK :], value_ref[0, block * pair : (block + 1) * pair, :], NT)
@@ -630,6 +666,8 @@
     def _():
         total[...] = jnp.zeros_like(total)
         take(PAIRS - 1)
+        have(4)
+        fetch(3, of_layer=layer - 1, when=more)
 
     @pl.when(busy & (j >= FFN_STEPS + PAIRS))
     def _():
@@ -637,21 +675,33 @@
 
         @pl.when(n < 3)
         def _():
-            triple_grad = dot(normed_ref[0, 0], grads[n], TN).astype(BF16)
+            triple_grad = dot(normed_ref[...], grads[n], TN).astype(BF16)
             for r in range(ROWS):
                 put(4 + n, r, triple_grad[r * SHARE : (r + 1) * SHARE])
 
+        for part in range(3):
+            @pl.when(n == part + 1)
+            def _():
+                have(8 + part)
+
         @pl.when(n > 0)
         def _():
-            total[...] += dot(grads[n - 1], weight_ref[0], NT)
+            total[...] += dot(grads[n - 1], weights[n % 2], NT)
+
+        @pl.when(n == 1)
+        def _():
+            fetch(10)
+
+        fetch(7, 0, of_layer=layer - 1, when=more & (n == 2))
 
         @pl.when(n == 3)
         def _():
+            have(5, 6)
             def rows(i, sums):
                 at = pl.ds(pl.multiple_of(i * TILE, TILE), TILE)
                 part = total[at, :]
-                scaled = scaled_ref[0, 0, at, :].astype(F32)
-                hidden = grad[at, :] + norm_back(part, scaled, inverse_ref[0, 0, at, :], pick(first_gain_ref, layer))
+                scaled = scaled_ref[at, :].astype(F32)
+                hidden = grad[at, :] + norm_back(part, scaled, inverse_ref[at, :], pick(first_gain_ref, layer))
                 grad[at, :] = hidden
                 low[at, :] = hidden.astype(BF16)
                 return (
@@ -669,6 +719,8 @@
             def _():
                 small[pl.ds(core, 1), :] = hidden_sum
 
+            fetch(1, 2, of_layer=layer - 1, when=more)
+
 
     last = layers * STEPS - 1
     half_width = width // 2
@@ -696,14 +748,16 @@
     def left_stage(s, v):
         h = order(v) % 2
         src = (left0.at[h, 1 - x], left1.at[h, 1 - z0], left2.at[h, 1 - z1], left3.at[h])[s - 1]
-        dst = (got_left1, got_left2, got_left3, got_left4)[s - 1].at[h]
-        return send(src, dst, left_send.at[s - 1, h], left_recv.at[s - 1, h], mates[s])
+        d = order(v) % 4 if s == 1 else h
+        dst = (got_left1, got_left2, got_left3, got_left4)[s - 1].at[d]
+        return send(src, dst, left_send.at[s - 1, h], left_recv.at[s - 1, d], mates[s])
 
     def right_stage(s, v):
         h = order(v) % 2
         src = (right0.at[h, 1 - own_pass], right1.at[h, 1 - z0], right2.at[h, 1 - z1])[s - 1]
-        dst = (got_right1, got_right2, got_right3)[s - 1].at[h]
-        return send(src, dst, right_send.at[s - 1, h], right_recv.at[s - 1, h], (mates[4], mates[2], mates[3])[s - 1])
+        d = order(v) % 4 if s == 1 else h
+        dst = (got_right1, got_right2, got_right3)[s - 1].at[d]
+        return send(src, dst, right_send.at[s - 1, h], right_recv.at[s - 1, d], (mates[4], mates[2], mates[3])[s - 1])
 
     def late_stage(s, v):
         k = order(v)
@@ -755,13 +809,13 @@
             go(triple_out.at[at_layer, :, columns(i - FFN_STEPS - PAIRS)])
 
     if hosted:
+        @pl.when(whether(t - 8))
+        def _():
+            out_copies(t - 8, "wait")
+
         @pl.when(whether(t - 7))
         def _():
-            out_copies(t - 7, "wait")
-
-        @pl.when(whether(t - 6))
-        def _():
-            v = t - 6
+            v = t - 7
             h = order(v) % 2
 
             def receive():
@@ -771,9 +825,9 @@
             final[h, :, half_width:] = right3[h].astype(F32)
             out_copies(v, "start")
 
-        @pl.when(whether(t - 5))
-        def _():
-            v = t - 5
+        @pl.when(whether(t - 6))
+        def _():
+            v = t - 6
             h = order(v) % 2
 
             def receive():
@@ -784,9 +838,9 @@
             left_stage(4, v).wait()
             final[h, :, :half_width] = left3[h].astype(F32) + got_left4[h].astype(F32)
 
-        @pl.when(whether(t - 4))
-        def _():
-            v = t - 4
+        @pl.when(whether(t - 5))
+        def _():
+            v = t - 5
             h = order(v) % 2
             right_stage(3, v).wait()
             right3[h] = add(right2[h, z1], got_right3[h])
@@ -795,9 +849,9 @@
             left3[h] = add(left2[h, z1], got_left3[h])
             left_stage(4, v).start()
 
-        @pl.when(whether(t - 3))
-        def _():
-            v = t - 3
+        @pl.when(whether(t - 4))
+        def _():
+            v = t - 4
             h = order(v) % 2
             right_stage(2, v).wait()
             right2[h] = add(right1[h, z0], got_right2[h])
@@ -806,15 +860,15 @@
             left2[h] = add(left1[h, z0], got_left2[h])
             left_stage(3, v).start()
 
-        @pl.when(whether(t - 2))
-        def _():
-            v = t - 2
+        @pl.when(whether(t - 3))
+        def _():
+            v = t - 3
             h = order(v) % 2
             right_stage(1, v).wait()
-            right1[h] = add(right0[h, own_pass], got_right1[h])
+            right1[h] = add(right0[h, own_pass], got_right1[order(v) % 4])
             right_stage(2, v).start()
             left_stage(1, v).wait()
-            left1[h] = add(left0[h, x], got_left1[h])
+            left1[h] = add(left0[h, x], got_left1[order(v) % 4])
             left_stage(2, v).start()
 
         @pl.when(whether(t - 1))
@@ -885,7 +939,7 @@
          total, exps, weight, hosted):
     layers, tokens, width = query.shape
     tiles = exps.shape[2]
-    steps = layers * STEPS + (STAGES + 1 if hosted else 1)
+    steps = layers * STEPS + (STAGES + 2 if hosted else 1)
     piece = (2, 2, 2, 2, SHARE, width)
     part = (2, 2, 2, SHARE, width // 2)
     count = layers * PIECES
@@ -902,36 +956,19 @@
         layer, j = at(t)
         return layer, jnp.clip(j - FFN_STEPS, 0, PAIRS - 1)
 
-    def part_of(t):
-        layer, j = at(t)
-        return layer, jnp.clip(j - FFN_STEPS - PAIRS - 1, 0, 2)
-
-    def kind_of(t):
-        layer, j = at(t)
-        return layer, (j >= FFN_STEPS).astype(jnp.int32), 0, 0
-
-    once = dict(pipeline_mode=pl.Buffered(1))
-
-    def of_layer(shape):
-        return pl.BlockSpec((1,) + shape, lambda t: (at(t)[0],) + (0,) * len(shape), **once)
-
     units = pl.BlockSpec((1, tokens, width), lambda t: (tile_of(t)[0], 0, tile_of(t)[1]))
     in_specs = [
         ANY, ANY, whole(length.shape), units, units,
-        pl.BlockSpec((1, 1, tokens, width), kind_of, **once),
-        pl.BlockSpec((1, 1, tokens, width), kind_of, **once),
-        pl.BlockSpec((1, 1, tokens, 1), kind_of, **once),
-        of_layer((tokens, width)),
+        ANY, ANY, ANY, ANY,
         pl.BlockSpec((1, width, width), lambda t: (tile_of(t)[0], 0, tile_of(t)[1])),
         pl.BlockSpec((1, width, width), lambda t: (tile_of(t)[0], tile_of(t)[1], 0)),
-        of_layer((width, width)),
+        ANY,
         whole((layers, width)), whole((layers, width)),
         pl.BlockSpec((1, tokens, LANES), lambda t: (head_of(t)[0], 0, head_of(t)[1])),
         pl.BlockSpec((1, 2 * tokens, LANES), lambda t: (head_of(t)[0], 0, head_of(t)[1])),
         pl.BlockSpec((1, 2 * tokens, LANES), lambda t: (head_of(t)[0], 0, head_of(t)[1] + PAIRS)),
-        pl.BlockSpec((1, 1, tokens, 2), lambda t: (head_of(t)[0], head_of(t)[1], 0, 0)),
-        ANY,
-        pl.BlockSpec((1, width, width), lambda t: (part_of(t)[0], 0, part_of(t)[1]), **once),
+        pl.BlockSpec((1, 1, 8, tokens), lambda t: (head_of(t)[0], head_of(t)[1], 0, 0)),
+        ANY, ANY,
     ]
     if hosted:
         shapes = [
@@ -954,6 +991,8 @@
             sds((SMALL, width), F32), sds((tokens, width), BF16), sds((tokens, width), BF16),
         ],
         scratch_shapes=[
+            some(tokens, width), some(tokens, width), pltpu.VMEM((tokens, 1), F32), some(tokens, width),
+            some(2, width, width),
             pltpu.VMEM((tokens, width), F32),
             pltpu.VMEM((tokens, width), F32),
             some(3, tokens, width),
@@ -964,12 +1003,12 @@
             some(2, *part), some(2, *part[1:]), some(2, *part[2:]), some(2, *part[3:]),
             some(2, *part), some(2, *part[1:]), some(2, *part[2:]), some(2, *part[3:]),
             some(2, *piece[1:]),
-            some(2, *part[1:]), some(2, *part[2:]), some(2, *part[3:]), some(2, *part[3:]),
-            some(2, *part[1:]), some(2, *part[2:]), some(2, *part[3:]), some(count, *part[3:]),
+            some(4, *part[1:]), some(2, *part[2:]), some(2, *part[3:]), some(2, *part[3:]),
+            some(4, *part[1:]), some(2, *part[2:]), some(2, *part[3:]), some(count, *part[3:]),
             pltpu.VMEM((2, SHARE, width), F32),
             pltpu.VMEM((SMALL, width), F32),
             pltpu.VMEM((STAGES, SMALL, width), F32),
-            dma((2, 2)), dma, dma((2,)), dma((2,)), dma((2,)), dma((2,)), dma((4, 2)), dma((4, 2)), dma((3, 2)), dma((3, 2)),
+            dma((6,)), dma((2, 2)), dma, dma((2,)), dma((2,)), dma((2,)), dma((2,)), dma((4, 2)), dma((4, 4)), dma((3, 2)), dma((3, 4)),
             dma((2, count)), dma((2, count)), dma((2,)),
             dma((STAGES,)), dma((STAGES,)), dma((2,)), dma((2,)), dma((2,)),
         ],

time: 379 us -> 364 us (0.960)
  Pallas kernels: 366 us -> 352 us
    pallas_call x1, Pallas kernels: 238 us -> 224 us  [back(): pl.pallas_call(functools.partial(back_kernel, layers, hosted), grid=(step...]
where the time goes in v5:
time: 364 us
  Pallas kernels  352 us (97%)
  local copies, waits for them, and re-layouts  10.9 us (3%)
    pallas_call x1, Pallas kernels, back(): pl.pallas_call(functools.partial(back_kernel, layers, hosted), grid=(step...  224 us
    pallas_call x1, Pallas kernels, forward(): pl.pallas_call(functools.partial(forward_kernel, layers), grid=(layers *...  128 us
    unnamed x16, local copies, waits for them, and re-layouts  8.04 us

profile of v5, /device:TPU:0, one launch (start us, length us, event | category | flops | bytes accessed | tf_op | source)
XLA Modules:
  0.0 364.1 jit_solution(5368950000104931654)
XLA Ops:
  1.3 127.8 %forward.1 = (bf16[2,2,1024,768]{3,2,1,0:T(8,128)(2,1)}, bf16[2,2,1024,768]{3,2,1,0:T(8,128)(2,1)}, f32[2,2,1024,1]{3,2,1,0:T(8,128)}, bf16[2,1024,768]{2,1,0:T(...) custom-call(bf16[1024,768]{1,0:T(8,128)(2,1)} %bitcast.20, ...), custom_call_target="tpu_custom_call" | custom-call | tf_op jit(solution)/shard_map/forward/pallas_call | solution.py:367
  129.1 224.0 %back.1 = (f32[2,48,2304]{2,1,0:T(8,128)}, f32[2,48,768]{2,1,0:T(8,128)}, f32[2,48,3072]{2,1,0:T(8,128)}, f32[2,192,768]{2,1,0:T(8,128)}, f32[16,768]{1,0:T(8,12...) custom-call(bf16[1024,768]{1,0:T(8,128)(2,1)} %get-tuple-element.31.cot_ref, ...), custom_call_target="tpu_custom_call" | custom-call | tf_op jit(solution)/shard_map/back/pallas_call | solution.py:985
  353.2 0.0 copy-start
  353.2 0.9 dynamic-slice.1
  354.1 0.6 fusion
  354.7 1.3 constant_dynamic-slice_fusion
  356.0 2.7 copy.38
  358.7 0.0 copy-done
  358.7 0.0 copy-start.3
  358.7 0.0 copy-start.4
  358.7 0.0 copy-start.2
  358.7 1.1 copy.39
  359.8 0.6 copy-done.3
  360.4 0.0 copy-start.1
  360.4 0.9 copy.40
  361.3 0.0 copy-done.4
  361.3 0.7 copy.41
  362.0 0.0 copy-done.2
  362.0 1.0 copy.42
  363.1 0.0 copy-done.1
  363.1 1.0 copy.43
Async XLA Ops:
  353.2 5.5 %copy-start = (bf16[1024,768]{1,0:T(8,128)(2,1)S(1)}, bf16[1024,768]{1,0:T(8,128)(2,1)}, u32[]{:S(2)}) copy-start(bf16[1024,768]{1,0:T(8,128)(2,1)} %get-tuple-element.45) | copy-start | bytes 4718596
  358.7 1.7 copy-start.3
  358.7 2.6 copy-start.4
  358.7 3.4 copy-start.2
  360.4 2.6 copy-start.1

commit v6 on v5

--- a/solution.py
+++ b/solution.py
@@ -435,7 +435,7 @@
     (
         small_ref, input_ref, output_ref,
         normed_ref, scaled_ref, inverse_ref, mixed_ref, weights, grad, total, grads, pending, landing, exps,
-        staged, left0, left1, left2, left3, right0, right1, right2, right3, got0,
+        staged, left0, left1, left2, left3, right0, right1, right2, right3, right4, got0,
         got_left1, got_left2, got_left3, got_left4, got_right1, got_right2, got_right3, got_late,
         final, small, small_got,
         load_sem, exp_sem, cot_sem, kv_send, kv_recv, core_send, core_recv, left_send, left_recv, right_send, right_recv,
@@ -746,22 +746,21 @@
         return send(staged.at[slot(v), 1 - core], got0.at[h], core_send.at[h], core_recv.at[h], mates[0])
 
     def left_stage(s, v):
-        h = order(v) % 2
+        h, d = order(v) % 2, order(v) % 4
         src = (left0.at[h, 1 - x], left1.at[h, 1 - z0], left2.at[h, 1 - z1], left3.at[h])[s - 1]
-        d = order(v) % 4 if s == 1 else h
         dst = (got_left1, got_left2, got_left3, got_left4)[s - 1].at[d]
         return send(src, dst, left_send.at[s - 1, h], left_recv.at[s - 1, d], mates[s])
 
     def right_stage(s, v):
-        h = order(v) % 2
+        h, d = order(v) % 2, order(v) % 4
         src = (right0.at[h, 1 - own_pass], right1.at[h, 1 - z0], right2.at[h, 1 - z1])[s - 1]
-        d = order(v) % 4 if s == 1 else h
         dst = (got_right1, got_right2, got_right3)[s - 1].at[d]
         return send(src, dst, right_send.at[s - 1, h], right_recv.at[s - 1, d], (mates[4], mates[2], mates[3])[s - 1])
 
     def late_stage(s, v):
         k = order(v)
-        return send(right3.at[k % 2], got_late.at[k], late_send.at[s - 4, k], late_recv.at[s - 4, k], (mates[1], mates[4])[s - 4])
+        src = (right3, right4)[s - 4].at[k % 2]
+        return send(src, got_late.at[k], late_send.at[s - 4, k], late_recv.at[s - 4, k], (mates[1], mates[4])[s - 4])
 
     keeps = x == own_pass
 
@@ -781,7 +780,7 @@
             receive()
 
     def out_copies(v, act):
-        h = order(v) % 2
+        h = order(v) % 4
         i = v % STEPS
         at_layer = layers - 1 - v // STEPS
         triple_out, merge_out, up_out, down_out = outs
@@ -808,67 +807,68 @@
         def _():
             go(triple_out.at[at_layer, :, columns(i - FFN_STEPS - PAIRS)])
 
+
     if hosted:
-        @pl.when(whether(t - 8))
-        def _():
-            out_copies(t - 8, "wait")
-
-        @pl.when(whether(t - 7))
-        def _():
-            v = t - 7
-            h = order(v) % 2
+        @pl.when(whether(t - 12))
+        def _():
+            out_copies(t - 12, "wait")
+
+        @pl.when(whether(t - 11))
+        def _():
+            v = t - 11
+            h, d = order(v) % 2, order(v) % 4
 
             def receive():
-                right3[h] = got_late[order(v)]
+                right4[h] = got_late[order(v)]
 
             late_wait(5, v, receive)
-            final[h, :, half_width:] = right3[h].astype(F32)
+            final[d, :, half_width:] = right4[h].astype(F32)
             out_copies(v, "start")
 
-        @pl.when(whether(t - 6))
-        def _():
-            v = t - 6
-            h = order(v) % 2
+        @pl.when(whether(t - 9))
+        def _():
+            v = t - 9
+            h, d = order(v) % 2, order(v) % 4
 
             def receive():
-                right3[h] = add(right3[h], got_late[order(v)])
+                right4[h] = add(right3[h], got_late[order(v)])
 
             late_wait(4, v, receive)
             late_start(5, v)
             left_stage(4, v).wait()
-            final[h, :, :half_width] = left3[h].astype(F32) + got_left4[h].astype(F32)
-
-        @pl.when(whether(t - 5))
-        def _():
-            v = t - 5
-            h = order(v) % 2
+            final[d, :, :half_width] = left3[h].astype(F32) + got_left4[d].astype(F32)
+
+        @pl.when(whether(t - 7))
+        def _():
+            v = t - 7
+            h, d = order(v) % 2, order(v) % 4
             right_stage(3, v).wait()
-            right3[h] = add(right2[h, z1], got_right3[h])
+            right3[h] = add(right2[h, z1], got_right3[d])
             late_start(4, v)
             left_stage(3, v).wait()
-            left3[h] = add(left2[h, z1], got_left3[h])
+            left3[h] = add(left2[h, z1], got_left3[d])
             left_stage(4, v).start()
 
-        @pl.when(whether(t - 4))
-        def _():
-            v = t - 4
-            h = order(v) % 2
+        @pl.when(whether(t - 5))
+        def _():
+            v = t - 5
+            h, d = order(v) % 2, order(v) % 4
             right_stage(2, v).wait()
-            right2[h] = add(right1[h, z0], got_right2[h])
+            right2[h] = add(right1[h, z0], got_right2[d])
             right_stage(3, v).start()
             left_stage(2, v).wait()
-            left2[h] = add(left1[h, z0], got_left2[h])
+            left2[h] = add(left1[h, z0], got_left2[d])
             left_stage(3, v).start()
 
         @pl.when(whether(t - 3))
         def _():
             v = t - 3
-            h = order(v) % 2
+            h, d = order(v) % 2, order(v) % 4
             right_stage(1, v).wait()
-            right1[h] = add(right0[h, own_pass], got_right1[order(v) % 4])
+            right1[h] = add(right0[h, own_pass], got_right1[d])
             right_stage(2, v).start()
             left_stage(1, v).wait()
-            left1[h] = add(left0[h, x], got_left1[order(v) % 4])
+            left1[h] = add(left0[h, x], got_left1[d])
             left_stage(2, v).start()
 
         @pl.when(whether(t - 1))
@@ -939,7 +939,7 @@
          total, exps, weight, hosted):
     layers, tokens, width = query.shape
     tiles = exps.shape[2]
-    steps = layers * STEPS + (STAGES + 2 if hosted else 1)
+    steps = layers * STEPS + (2 * STAGES + 1 if hosted else 1)
     piece = (2, 2, 2, 2, SHARE, width)
     part = (2, 2, 2, SHARE, width // 2)
     count = layers * PIECES
@@ -1001,15 +1001,15 @@
             some(2, 2, tiles, BLOCK, 2 * BLOCK),
             some(7, *piece),
             some(2, *part), some(2, *part[1:]), some(2, *part[2:]), some(2, *part[3:]),
-            some(2, *part), some(2, *part[1:]), some(2, *part[2:]), some(2, *part[3:]),
+            some(2, *part), some(2, *part[1:]), some(2, *part[2:]), some(2, *part[3:]), some(2, *part[3:]),
             some(2, *piece[1:]),
-            some(4, *part[1:]), some(2, *part[2:]), some(2, *part[3:]), some(2, *part[3:]),
-            some(4, *part[1:]), some(2, *part[2:]), some(2, *part[3:]), some(count, *part[3:]),
-            pltpu.VMEM((2, SHARE, width), F32),
+            some(4, *part[1:]), some(4, *part[2:]), some(4, *part[3:]), some(4, *part[3:]),
+            some(4, *part[1:]), some(4, *part[2:]), some(4, *part[3:]), some(count, *part[3:]),
+            pltpu.VMEM((4, SHARE, width), F32),
             pltpu.VMEM((SMALL, width), F32),
             pltpu.VMEM((STAGES, SMALL, width), F32),
             dma((6,)), dma((2, 2)), dma, dma((2,)), dma((2,)), dma((2,)), dma((2,)), dma((4, 2)), dma((4, 4)), dma((3, 2)), dma((3, 4)),
-            dma((2, count)), dma((2, count)), dma((2,)),
+            dma((2, count)), dma((2, count)), dma((4,)),
             dma((STAGES,)), dma((STAGES,)), dma((2,)), dma((2,)), dma((2,)),
         ],
         compiler_params=params(1),

time: 364 us -> 358 us (0.984)
  Pallas kernels: 352 us -> 345 us
    pallas_call x1, Pallas kernels: 224 us -> 217 us  [back(): pl.pallas_call(functools.partial(back_kernel, layers, hosted), grid=(step...]
where the time goes in v6:
time: 358 us; the launch traced here: 357 us
  Pallas kernels  345 us (96%)
  local copies, waits for them, and re-layouts  10.9 us (3%)
    pallas_call x1, Pallas kernels, back(): pl.pallas_call(functools.partial(back_kernel, layers, hosted), grid=(step...  217 us
    pallas_call x1, Pallas kernels, forward(): pl.pallas_call(functools.partial(forward_kernel, layers), grid=(layers *...  128 us
    unnamed x16, local copies, waits for them, and re-layouts  8.04 us

profile of v6, /device:TPU:0, one launch (start us, length us, event | category | flops | bytes accessed | tf_op | source)
XLA Modules:
  0.0 357.3 jit_solution(12018207399876761182)
XLA Ops:
  1.3 127.8 %forward.1 = (bf16[2,2,1024,768]{3,2,1,0:T(8,128)(2,1)}, bf16[2,2,1024,768]{3,2,1,0:T(8,128)(2,1)}, f32[2,2,1024,1]{3,2,1,0:T(8,128)}, bf16[2,1024,768]{2,1,0:T(...) custom-call(bf16[1024,768]{1,0:T(8,128)(2,1)} %bitcast.20, ...), custom_call_target="tpu_custom_call" | custom-call | tf_op jit(solution)/shard_map/forward/pallas_call | solution.py:367
  129.1 217.3 %back.1 = (f32[2,48,2304]{2,1,0:T(8,128)}, f32[2,48,768]{2,1,0:T(8,128)}, f32[2,48,3072]{2,1,0:T(8,128)}, f32[2,192,768]{2,1,0:T(8,128)}, f32[16,768]{1,0:T(8,12...) custom-call(bf16[1024,768]{1,0:T(8,128)(2,1)} %get-tuple-element.31.cot_ref, ...), custom_call_target="tpu_custom_call" | custom-call | tf_op jit(solution)/shard_map/back/pallas_call | solution.py:985
  346.4 0.0 copy-start
  346.5 0.9 dynamic-slice.1
  347.4 0.6 fusion
  348.0 1.3 constant_dynamic-slice_fusion
  349.3 2.7 copy.38
  351.9 0.0 copy-done
  351.9 0.0 copy-start.3
  351.9 0.0 copy-start.4
  351.9 0.0 copy-start.2
  351.9 1.1 copy.39
  353.1 0.6 copy-done.3
  353.7 0.0 copy-start.1
  353.7 0.9 copy.40
  354.6 0.0 copy-done.4
  354.6 0.7 copy.41
  355.3 0.0 copy-done.2
  355.3 1.0 copy.42
  356.3 0.0 copy-done.1
  356.3 1.0 copy.43
Async XLA Ops:
  346.4 5.5 %copy-start = (bf16[1024,768]{1,0:T(8,128)(2,1)S(1)}, bf16[1024,768]{1,0:T(8,128)(2,1)}, u32[]{:S(2)}) copy-start(bf16[1024,768]{1,0:T(8,128)(2,1)} %get-tuple-element.45) | copy-start | bytes 4718596
  351.9 1.7 copy-start.3
  351.9 2.6 copy-start.4
  351.9 3.4 copy-start.2
  353.7 2.6 copy-start.1

commit v7 on v6

--- a/solution.py
+++ b/solution.py
@@ -65,7 +65,8 @@
 
 def bits():
     row = lax.axis_index("rows")
-    return row, row % 2, (row // 2) % 2, (row // 4) % 2, (row // 8) % 2, lax.axis_index("pass")
+    x, z0, z1 = (lax.rem(lax.div(row, 2**n), 2) for n in (1, 2, 3))
+    return row, lax.rem(row, 2), x, z0, z1, lax.axis_index("pass")
 
 
 def send(src, dst, send_sem, recv_sem, device):
@@ -102,9 +103,8 @@
     hidden, arrived, length_mine, length_here, queries, kv, values, mixes, triple, merge, up, down,
     weight_sem, kv_sem, kv_send, kv_recv, free_sem, swap_send, swap_recv, here_sem,
 ):
-    t = pl.program_id(0)
-    layer = t // FORWARD
-    j = t % FORWARD
+    layer, j = pl.program_id(0), pl.program_id(1)
+    t = layer * FORWARD + j
     row, core, _, _, _, own_pass = bits()
     tokens, width = hidden.shape
     blocks = tokens // BLOCK
@@ -329,7 +329,7 @@
             for which in range(1, 4):
                 weight_copies(which, layer + 1).start()
 
-    @pl.when(t == pl.num_programs(0) - 1)
+    @pl.when(t == layers * FORWARD - 1)
     def _():
         move(QKV_STEPS, "wait")
 
@@ -340,25 +340,18 @@
     blocks = tokens // BLOCK
     tiles = blocks * (blocks + 1) // 2
 
-    def phase(t):
-        return t // FORWARD, t % FORWARD
-
-    def row_tile(t):
-        layer, j = phase(t)
+    def row_tile(layer, j):
         late = j >= QKV_STEPS + PAIRS
         kind = jnp.where(late, 0, 1)
         return layer, kind, jnp.where(late, j - QKV_STEPS - PAIRS, jnp.minimum(j, QKV_STEPS - 1)), 0
 
-    def query_tile(t):
-        layer, j = phase(t)
+    def query_tile(layer, j):
         return layer, jnp.minimum(j, QKV_STEPS - 1), 0
 
-    def head(t):
-        layer, j = phase(t)
-        return layer, jnp.clip(j - QKV_STEPS, 0, PAIRS - 1)
-
-    def ffn_tile(t):
-        layer, j = phase(t)
+    def head(j):
+        return jnp.clip(j - QKV_STEPS, 0, PAIRS - 1)
+
+    def ffn_tile(layer, j):
         return layer, jnp.maximum(j - QKV_STEPS - PAIRS, 0), 0
 
     vector = whole((layers, width))
@@ -366,17 +359,17 @@
     dma = pltpu.SemaphoreType.DMA
     return pl.pallas_call(
         functools.partial(forward_kernel, layers),
-        grid=(layers * FORWARD,),
+        grid=(layers, FORWARD),
         in_specs=[ANY, ANY, pl.BlockSpec(memory_space=pltpu.SMEM), whole(embed.shape), vector, vector, vector, vector, ANY, ANY, ANY, ANY],
         out_specs=[
             rows, rows, pl.BlockSpec((1, 1, TILE, 1), row_tile),
             pl.BlockSpec((1, TILE, width), query_tile),
-            pl.BlockSpec((1, tokens, LANES), lambda t: (head(t)[0], 0, head(t)[1])),
-            pl.BlockSpec((1, 1, 8, tokens), lambda t: (*head(t), 0, 0)),
-            pl.BlockSpec((1, 2, tiles, BLOCK, 2 * BLOCK), lambda t: (*head(t), 0, 0, 0)),
+            pl.BlockSpec((1, tokens, LANES), lambda layer, j: (layer, 0, head(j))),
+            pl.BlockSpec((1, 1, 8, tokens), lambda layer, j: (layer, head(j), 0, 0)),
+            pl.BlockSpec((1, 2, tiles, BLOCK, 2 * BLOCK), lambda layer, j: (layer, head(j), 0, 0, 0)),
             pl.BlockSpec((1, TILE, units), ffn_tile), pl.BlockSpec((1, TILE, units), ffn_tile),
             ANY,
-            pl.BlockSpec((TILE, width), lambda t: (jnp.where(phase(t)[0] == layers - 1, ffn_tile(t)[1], 0), 0)),
+            pl.BlockSpec((TILE, width), lambda layer, j: (jnp.where(layer == layers - 1, ffn_tile(layer, j)[1], 0), 0)),
             ANY, whole((8, LANES)),
         ],
         out_shape=[
@@ -424,6 +417,10 @@
 SMALL = 16
 
 
+def left_part(width):
+    return 2 * width // 3
+
+
 def back_kernel(
     layers, hosted,
     cot_ref, done_ref, length_ref, act_ref, slope_ref, normeds_ref, scaleds_ref, inverses_ref, mixes_ref, up_ref, down_ref,
@@ -442,14 +439,14 @@
         late_send, late_recv, out_sem, small_send, small_recv, swap_send, swap_recv, here_sem,
     ) = refs[len(outs) :]
     low = grads.at[1]
-    t = pl.program_id(0)
-    j = t % STEPS
-    layer = layers - 1 - t // STEPS
+    turn, j = pl.program_id(0), pl.program_id(1)
+    t = turn * STEPS + j
+    layer = jnp.maximum(layers - 1 - turn, 0)
     row, core, x, z0, z1, own_pass = bits()
     tokens, width = grad.shape
     blocks = tokens // BLOCK
     pair = 2 * BLOCK
-    busy = t < layers * STEPS
+    busy = turn < layers
     core_mate = {"rows": row + 1 - 2 * core}
     mates = [
         core_mate, {"rows": row + 2 - 4 * x}, {"rows": row + 4 - 8 * z0}, {"rows": row + 8 - 16 * z1},
@@ -509,7 +506,7 @@
 
 
     def exp_copy(head):
-        at = (head // 2) % 2, head % 2
+        at = lax.rem(lax.div(head, 2), 2), lax.rem(head, 2)
         return pltpu.make_async_copy(exp_ref.at[layer, head], exps.at[at], exp_sem.at[at])
 
     def put(slot, r, value):
@@ -527,18 +524,18 @@
         for q in range(4):
             for i in range(4):
                 first = q * 4 * SHARE + i * SHARE
-                staged[i, q % 2, q // 2, j % 2, (j // 2) % 2] = down_grad[first : first + SHARE]
+                staged[i, q % 2, q // 2, lax.rem(j, 2), lax.div(j, 2)] = down_grad[first : first + SHARE]
         grad_act = dot(grad_low, down_ref[0], NT)
         grad_pre = (slope_ref[0].astype(F32) * grad_act).astype(BF16)
         up_grad = dot(normed_ref[...], grad_pre, TN).astype(BF16)
         for r in range(ROWS):
-            put(4 + j % 2, r, up_grad[r * SHARE : (r + 1) * SHARE])
+            put(4 + lax.rem(j, 2), r, up_grad[r * SHARE : (r + 1) * SHARE])
         total[...] += dot(grad_pre, up_ref[0], NT)
 
         @pl.when(j == FFN_STEPS - 1)
         def _():
-            exp_copy(0).start()
-            exp_copy(1).start()
+            exp_copy(jnp.int32(0)).start()
+            exp_copy(jnp.int32(1)).start()
             have(1, 2, 3, 7)
 
             def rows(i, sums):
@@ -567,7 +564,7 @@
 
     def kv_copy(p):
         return send(
-            pending.at[p % 2], landing.at[p % 2], kv_send.at[p % 2], kv_recv.at[p % 2], core_mate,
+            pending.at[lax.rem(p, 2)], landing.at[lax.rem(p, 2)], kv_send.at[lax.rem(p, 2)], kv_recv.at[lax.rem(p, 2)], core_mate,
         )
 
     def take(p):
@@ -575,7 +572,7 @@
         lanes = pl.ds(pl.multiple_of(p * LANES, LANES), LANES)
         for which in range(2):
             grads[1 + which, :, lanes] = (
-                grads[1 + which, :, lanes].astype(F32) + landing[p % 2, which].astype(F32)
+                grads[1 + which, :, lanes].astype(F32) + landing[lax.rem(p, 2), which].astype(F32)
             ).astype(BF16)
 
     @pl.when(busy & (j >= FFN_STEPS) & (j < FFN_STEPS + PAIRS))
@@ -606,7 +603,7 @@
 
         def score_grad(head, block, grad_prob):
             start = tile_index(blocks, block, block)
-            prob = exps[p % 2, head, start : start + blocks - block].reshape(tokens - block * BLOCK, pair)
+            prob = exps[lax.rem(p, 2), head, start : start + blocks - block].reshape(tokens - block * BLOCK, pair)
             return prob, (prob.astype(F32) * (grad_prob - inner[head][block * BLOCK :])).astype(BF16)
 
         sums = {}
@@ -628,7 +625,7 @@
                 both = (sums[block][which] + pairs[which]).T
                 zero, one = both[:BLOCK], both[BLOCK:]
                 grads[1 + which, at, lanes] = jnp.where(core == 0, zero, one).astype(BF16)
-                pending[p % 2, which, at, :] = jnp.where(core == 0, one, zero).astype(BF16)
+                pending[lax.rem(p, 2), which, at, :] = jnp.where(core == 0, one, zero).astype(BF16)
 
         exp_copy(2 * p).wait()
         exp_copy(2 * p + 1).wait()
@@ -665,7 +662,7 @@
     @pl.when(busy & (j == FFN_STEPS + PAIRS))
     def _():
         total[...] = jnp.zeros_like(total)
-        take(PAIRS - 1)
+        take(jnp.int32(PAIRS - 1))
         have(4)
         fetch(3, of_layer=layer - 1, when=more)
 
@@ -686,7 +683,7 @@
 
         @pl.when(n > 0)
         def _():
-            total[...] += dot(grads[n - 1], weights[n % 2], NT)
+            total[...] += dot(grads[n - 1], weights[lax.rem(n, 2)], NT)
 
         @pl.when(n == 1)
         def _():
@@ -723,43 +720,51 @@
 
 
     last = layers * STEPS - 1
-    half_width = width // 2
+    split = left_part(width)
+
+    def piece(ago):
+        before = j < ago
+        return turn - jnp.where(before, 1, 0), j - ago + jnp.where(before, STEPS, 0)
 
     def slot(v):
-        i = v % STEPS
+        _, i = v
         return jnp.where(
-            i < 4, 4 + i % 2, jnp.where(i < 8, i - 4, jnp.where(i == 8, 6, i - FFN_STEPS - PAIRS + 4))
+            i < 4, 4 + lax.rem(i, 2), jnp.where(i < 8, i - 4, jnp.where(i == 8, 6, i - FFN_STEPS - PAIRS + 4))
         )
 
-    def whether(v):
-        return (v >= 0) & (v <= last) & (v % STEPS != FFN_STEPS + PAIRS - 1) & (v % STEPS != STEPS - 1)
+    def whether(ago):
+        made, i = piece(ago)
+        return (made >= 0) & (made < layers) & (i != FFN_STEPS + PAIRS - 1) & (i != STEPS - 1)
 
     def order(v):
-        i = v % STEPS
-        return v // STEPS * PIECES + i - jnp.where(i >= FFN_STEPS + PAIRS, 1, 0)
+        made, i = v
+        return made * PIECES + i - jnp.where(i >= FFN_STEPS + PAIRS, 1, 0)
+
+    def turns(v, count):
+        return lax.rem(order(v), count)
 
     def add(a, b):
-        return (a.astype(F32) + b.astype(F32)).astype(BF16)
+        return a + b
 
     def core_stage(v):
-        h = order(v) % 2
+        h = turns(v, 2)
         return send(staged.at[slot(v), 1 - core], got0.at[h], core_send.at[h], core_recv.at[h], mates[0])
 
     def left_stage(s, v):
-        h, d = order(v) % 2, order(v) % 4
+        h, d = turns(v, 2), turns(v, 4)
         src = (left0.at[h, 1 - x], left1.at[h, 1 - z0], left2.at[h, 1 - z1], left3.at[h])[s - 1]
         dst = (got_left1, got_left2, got_left3, got_left4)[s - 1].at[d]
         return send(src, dst, left_send.at[s - 1, h], left_recv.at[s - 1, d], mates[s])
 
     def right_stage(s, v):
-        h, d = order(v) % 2, order(v) % 4
+        h, d = turns(v, 2), turns(v, 4)
         src = (right0.at[h, 1 - own_pass], right1.at[h, 1 - z0], right2.at[h, 1 - z1])[s - 1]
         dst = (got_right1, got_right2, got_right3)[s - 1].at[d]
         return send(src, dst, right_send.at[s - 1, h], right_recv.at[s - 1, d], (mates[4], mates[2], mates[3])[s - 1])
 
     def late_stage(s, v):
         k = order(v)
-        src = (right3, right4)[s - 4].at[k % 2]
+        src = (right3, right4)[s - 4].at[turns(v, 2)]
         return send(src, got_late.at[k], late_send.at[s - 4, k], late_recv.at[s - 4, k], (mates[1], mates[4])[s - 4])
 
     keeps = x == own_pass
@@ -780,9 +785,9 @@
             receive()
 
     def out_copies(v, act):
-        h = order(v) % 4
-        i = v % STEPS
-        at_layer = layers - 1 - v // STEPS
+        h = turns(v, 4)
+        made, i = v
+        at_layer = layers - 1 - made
         triple_out, merge_out, up_out, down_out = outs
 
         def columns(n):
@@ -809,26 +814,26 @@
 
 
     if hosted:
-        @pl.when(whether(t - 12))
-        def _():
-            out_copies(t - 12, "wait")
-
-        @pl.when(whether(t - 11))
-        def _():
-            v = t - 11
-            h, d = order(v) % 2, order(v) % 4
+        @pl.when(whether(12))
+        def _():
+            out_copies(piece(12), "wait")
+
+        @pl.when(whether(11))
+        def _():
+            v = piece(11)
+            h, d = turns(v, 2), turns(v, 4)
 
             def receive():
                 right4[h] = got_late[order(v)]
 
             late_wait(5, v, receive)
-            final[d, :, half_width:] = right4[h].astype(F32)
+            final[d, :, split:] = right4[h].astype(F32)
             out_copies(v, "start")
 
-        @pl.when(whether(t - 9))
-        def _():
-            v = t - 9
-            h, d = order(v) % 2, order(v) % 4
+        @pl.when(whether(9))
+        def _():
+            v = piece(9)
+            h, d = turns(v, 2), turns(v, 4)
 
             def receive():
                 right4[h] = add(right3[h], got_late[order(v)])
@@ -836,12 +841,12 @@
             late_wait(4, v, receive)
             late_start(5, v)
             left_stage(4, v).wait()
-            final[d, :, :half_width] = left3[h].astype(F32) + got_left4[d].astype(F32)
-
-        @pl.when(whether(t - 7))
-        def _():
-            v = t - 7
-            h, d = order(v) % 2, order(v) % 4
+            final[d, :, :split] = left3[h].astype(F32) + got_left4[d].astype(F32)
+
+        @pl.when(whether(7))
+        def _():
+            v = piece(7)
+            h, d = turns(v, 2), turns(v, 4)
             right_stage(3, v).wait()
             right3[h] = add(right2[h, z1], got_right3[d])
             late_start(4, v)
@@ -849,10 +854,10 @@
             left3[h] = add(left2[h, z1], got_left3[d])
             left_stage(4, v).start()
 
-        @pl.when(whether(t - 5))
-        def _():
-            v = t - 5
-            h, d = order(v) % 2, order(v) % 4
+        @pl.when(whether(5))
+        def _():
+            v = piece(5)
+            h, d = turns(v, 2), turns(v, 4)
             right_stage(2, v).wait()
             right2[h] = add(right1[h, z0], got_right2[d])
             right_stage(3, v).start()
@@ -860,10 +865,10 @@
             left2[h] = add(left1[h, z0], got_left2[d])
             left_stage(3, v).start()
 
-        @pl.when(whether(t - 3))
-        def _():
-            v = t - 3
-            h, d = order(v) % 2, order(v) % 4
+        @pl.when(whether(3))
+        def _():
+            v = piece(3)
+            h, d = turns(v, 2), turns(v, 4)
             right_stage(1, v).wait()
             right1[h] = add(right0[h, own_pass], got_right1[d])
             right_stage(2, v).start()
@@ -871,19 +876,19 @@
             left1[h] = add(left0[h, x], got_left1[d])
             left_stage(2, v).start()
 
-        @pl.when(whether(t - 1))
-        def _():
-            v = t - 1
-            h = order(v) % 2
+        @pl.when(whether(1))
+        def _():
+            v = piece(1)
+            h = turns(v, 2)
             core_stage(v).wait()
-            right0[h] = add(staged[slot(v), core, :, :, :, :, half_width:], got0[h, :, :, :, :, half_width:])
+            right0[h] = add(staged[slot(v), core, :, :, :, :, split:], got0[h, :, :, :, :, split:])
             right_stage(1, v).start()
-            left0[h] = add(staged[slot(v), core, :, :, :, :, :half_width], got0[h, :, :, :, :, :half_width])
+            left0[h] = add(staged[slot(v), core, :, :, :, :, :split], got0[h, :, :, :, :, :split])
             left_stage(1, v).start()
 
-        @pl.when(whether(t))
-        def _():
-            core_stage(t).start()
+        @pl.when(whether(0))
+        def _():
+            core_stage(piece(0)).start()
 
         for s in range(STAGES + 1):
             def small_copy(s):
@@ -898,15 +903,15 @@
                     small_copy(s).start()
     else:
         def piece_copy(v):
-            return pltpu.make_async_copy(staged.at[slot(v)], outs[0].at[v], out_sem.at[v % 2])
-
-        @pl.when(whether(t - 1))
-        def _():
-            piece_copy(t - 1).wait()
-
-        @pl.when(whether(t))
-        def _():
-            piece_copy(t).start()
+            return pltpu.make_async_copy(staged.at[slot(v)], outs[0].at[v[0] * STEPS + v[1]], out_sem.at[turns(v, 2)])
+
+        @pl.when(whether(1))
+        def _():
+            piece_copy(piece(1)).wait()
+
+        @pl.when(whether(0))
+        def _():
+            piece_copy(piece(0)).start()
 
 
     def swaps(i, act):
@@ -928,7 +933,7 @@
     def _():
         swaps(1, "start")
 
-    @pl.when(t == pl.num_programs(0) - 1)
+    @pl.when(t == (layers + 1) * STEPS - 1)
     def _():
         swaps(0, "wait")
         swaps(1, "wait")
@@ -939,35 +944,53 @@
          total, exps, weight, hosted):
     layers, tokens, width = query.shape
     tiles = exps.shape[2]
-    steps = layers * STEPS + (2 * STAGES + 1 if hosted else 1)
     piece = (2, 2, 2, 2, SHARE, width)
-    part = (2, 2, 2, SHARE, width // 2)
+    left = (2, 2, 2, SHARE, left_part(width))
+    right = (2, 2, 2, SHARE, width - left_part(width))
     count = layers * PIECES
 
-    def at(t):
-        t = jnp.minimum(t, layers * STEPS - 1)
-        return layers - 1 - t // STEPS, t % STEPS
-
-    def tile_of(t):
-        layer, j = at(t)
+    def at(turn, j):
+        return jnp.maximum(layers - 1 - turn, 0), jnp.where(turn < layers, j, STEPS - 1)
+
+    def tile(*step):
+        layer, j = at(*step)
         return layer, jnp.minimum(j, FFN_STEPS - 1)
 
-    def head_of(t):
-        layer, j = at(t)
+    def pair(*step):
+        layer, j = at(*step)
         return layer, jnp.clip(j - FFN_STEPS, 0, PAIRS - 1)
 
-    units = pl.BlockSpec((1, tokens, width), lambda t: (tile_of(t)[0], 0, tile_of(t)[1]))
+    def spec(shape, place):
+        return pl.BlockSpec(shape, lambda turn, j: place(turn, j))
+
+    def across(*step):
+        layer, n = tile(*step)
+        return layer, 0, n
+
+    def down_rows(*step):
+        layer, n = tile(*step)
+        return layer, n, 0
+
+    def lanes(*step):
+        layer, n = pair(*step)
+        return layer, 0, n
+
+    def value_lanes(*step):
+        layer, n = pair(*step)
+        return layer, 0, n + PAIRS
+
+    def totals(*step):
+        return (*pair(*step), 0, 0)
+
+    units = spec((1, tokens, width), across)
     in_specs = [
         ANY, ANY, whole(length.shape), units, units,
         ANY, ANY, ANY, ANY,
-        pl.BlockSpec((1, width, width), lambda t: (tile_of(t)[0], 0, tile_of(t)[1])),
-        pl.BlockSpec((1, width, width), lambda t: (tile_of(t)[0], tile_of(t)[1], 0)),
+        spec((1, width, width), across), spec((1, width, width), down_rows),
         ANY,
         whole((layers, width)), whole((layers, width)),
-        pl.BlockSpec((1, tokens, LANES), lambda t: (head_of(t)[0], 0, head_of(t)[1])),
-        pl.BlockSpec((1, 2 * tokens, LANES), lambda t: (head_of(t)[0], 0, head_of(t)[1])),
-        pl.BlockSpec((1, 2 * tokens, LANES), lambda t: (head_of(t)[0], 0, head_of(t)[1] + PAIRS)),
-        pl.BlockSpec((1, 1, 8, tokens), lambda t: (head_of(t)[0], head_of(t)[1], 0, 0)),
+        spec((1, tokens, LANES), lanes), spec((1, 2 * tokens, LANES), lanes), spec((1, 2 * tokens, LANES), value_lanes),
+        spec((1, 1, 8, tokens), totals),
         ANY, ANY,
     ]
     if hosted:
@@ -984,7 +1007,7 @@
 
     return pl.pallas_call(
         functools.partial(back_kernel, layers, hosted),
-        grid=(steps,),
+        grid=(layers + 1, STEPS),
         in_specs=in_specs,
         out_specs=[ANY] * len(shapes) + [whole((SMALL, width)), ANY, ANY],
         out_shape=shapes + [
@@ -1000,11 +1023,11 @@
             some(2, 2, tokens, LANES),
             some(2, 2, tiles, BLOCK, 2 * BLOCK),
             some(7, *piece),
-            some(2, *part), some(2, *part[1:]), some(2, *part[2:]), some(2, *part[3:]),
-            some(2, *part), some(2, *part[1:]), some(2, *part[2:]), some(2, *part[3:]), some(2, *part[3:]),
+            some(2, *left), some(2, *left[1:]), some(2, *left[2:]), some(2, *left[3:]),
+            some(2, *right), some(2, *right[1:]), some(2, *right[2:]), some(2, *right[3:]), some(2, *right[3:]),
             some(2, *piece[1:]),
-            some(4, *part[1:]), some(4, *part[2:]), some(4, *part[3:]), some(4, *part[3:]),
-            some(4, *part[1:]), some(4, *part[2:]), some(4, *part[3:]), some(count, *part[3:]),
+            some(4, *left[1:]), some(4, *left[2:]), some(4, *left[3:]), some(4, *left[3:]),
+            some(4, *right[1:]), some(4, *right[2:]), some(4, *right[3:]), some(count, *right[3:]),
             pltpu.VMEM((4, SHARE, width), F32),
             pltpu.VMEM((SMALL, width), F32),
             pltpu.VMEM((STAGES, SMALL, width), F32),

time: 358 us -> 352 us (0.983)
  Pallas kernels: 345 us -> 339 us
    pallas_call x2, Pallas kernels: 345 us -> 339 us  [the longest x1 212 us: back(): pl.pallas_call(functools.partial(back_kernel, layers, hosted), grid=(laye...]
where the time goes in v7:
time: 352 us
  Pallas kernels  339 us (96%)
  local copies, waits for them, and re-layouts  10.9 us (3%)
    pallas_call x1, Pallas kernels, back(): pl.pallas_call(functools.partial(back_kernel, layers, hosted), grid=(laye...  212 us
    pallas_call x1, Pallas kernels, forward(): pl.pallas_call(functools.partial(forward_kernel, layers), grid=(layers, F...  128 us
    unnamed x16, local copies, waits for them, and re-layouts  8.04 us

profile of v7, /device:TPU:0, one launch (start us, length us, event | category | flops | bytes accessed | tf_op | source)
XLA Modules:
  0.0 351.5 jit_solution(7430667363685454232)
XLA Ops:
  1.3 127.8 %forward.1 = (bf16[2,2,1024,768]{3,2,1,0:T(8,128)(2,1)}, bf16[2,2,1024,768]{3,2,1,0:T(8,128)(2,1)}, f32[2,2,1024,1]{3,2,1,0:T(8,128)}, bf16[2,1024,768]{2,1,0:T(...) custom-call(bf16[1024,768]{1,0:T(8,128)(2,1)} %bitcast.20, ...), custom_call_target="tpu_custom_call" | custom-call | tf_op jit(solution)/shard_map/forward/pallas_call | solution.py:360
  129.1 211.6 %back.1 = (f32[2,48,2304]{2,1,0:T(8,128)}, f32[2,48,768]{2,1,0:T(8,128)}, f32[2,48,3072]{2,1,0:T(8,128)}, f32[2,192,768]{2,1,0:T(8,128)}, f32[16,768]{1,0:T(8,12...) custom-call(bf16[1024,768]{1,0:T(8,128)(2,1)} %get-tuple-element.31.cot_ref, ...), custom_call_target="tpu_custom_call" | custom-call | tf_op jit(solution)/shard_map/back/pallas_call | solution.py:1008
  340.6 0.0 copy-start
  340.6 0.9 dynamic-slice.1
  341.6 0.6 fusion
  342.1 1.3 constant_dynamic-slice_fusion
  343.5 2.7 copy.38
  346.1 0.0 copy-done
  346.1 0.0 copy-start.3
  346.1 0.0 copy-start.4
  346.1 0.0 copy-start.2
  346.1 1.1 copy.39
  347.3 0.6 copy-done.3
  347.9 0.0 copy-start.1
  347.9 0.9 copy.40
  348.8 0.0 copy-done.4
  348.8 0.7 copy.41
  349.5 0.0 copy-done.2
  349.5 1.0 copy.42
  350.5 0.0 copy-done.1
  350.5 1.0 copy.43
Async XLA Ops:
  340.6 5.5 %copy-start = (bf16[1024,768]{1,0:T(8,128)(2,1)S(1)}, bf16[1024,768]{1,0:T(8,128)(2,1)}, u32[]{:S(2)}) copy-start(bf16[1024,768]{1,0:T(8,128)(2,1)} %get-tuple-element.45) | copy-start | bytes 4718596
  346.1 1.7 copy-start.3
  346.1 2.6 copy-start.4
  346.1 3.4 copy-start.2
  347.9 2.6 copy-start.1

commit v8 on v7

--- a/solution.py
+++ b/solution.py
@@ -438,7 +438,7 @@
         load_sem, exp_sem, cot_sem, kv_send, kv_recv, core_send, core_recv, left_send, left_recv, right_send, right_recv,
         late_send, late_recv, out_sem, small_send, small_recv, swap_send, swap_recv, here_sem,
     ) = refs[len(outs) :]
-    low = grads.at[1]
+    low = grads.at[0]
     turn, j = pl.program_id(0), pl.program_id(1)
     t = turn * STEPS + j
     layer = jnp.maximum(layers - 1 - turn, 0)
@@ -478,6 +478,22 @@
         small[...] = jnp.zeros_like(small)
 
 
+    def swaps(i, act):
+        if isinstance(i, int):
+            source, target = done_ref, output_ref
+        else:
+            rows = pl.ds(pl.multiple_of((i - 1) * TILE, TILE), TILE)
+            source, target = low.at[rows, :], input_ref.at[rows, :]
+
+        @pl.when(swapped)
+        def _():
+            getattr(send(source, target, swap_send.at[i], swap_recv.at[i], diagonal), act)()
+
+        @pl.when(jnp.logical_not(swapped))
+        def _():
+            getattr(pltpu.make_async_copy(source, target, here_sem.at[i]), act)()
+
+
     def load(what, of_layer):
         def weight_part(n):
             return triples_ref.at[of_layer, :, n * width : (n + 1) * width]
@@ -517,7 +533,6 @@
         @pl.when(j == 0)
         def _():
             total[...] = jnp.zeros_like(total)
-            have(0)
 
         grad_low = low[...]
         down_grad = dot(act_ref[0], grad_low, TN).astype(BF16)
@@ -527,6 +542,11 @@
                 staged[i, q % 2, q // 2, lax.rem(j, 2), lax.div(j, 2)] = down_grad[first : first + SHARE]
         grad_act = dot(grad_low, down_ref[0], NT)
         grad_pre = (slope_ref[0].astype(F32) * grad_act).astype(BF16)
+
+        @pl.when(j == 0)
+        def _():
+            have(0)
+
         up_grad = dot(normed_ref[...], grad_pre, TN).astype(BF16)
         for r in range(ROWS):
             put(4 + lax.rem(j, 2), r, up_grad[r * SHARE : (r + 1) * SHARE])
@@ -545,7 +565,7 @@
                 mid = grad[at, :] + norm_back(part, scaled, inverse_ref[at, :], pick(second_gain_ref, layer))
                 grad[at, :] = mid
                 low_mid = mid.astype(BF16)
-                low[at, :] = low_mid
+                grads[1, at, :] = low_mid
                 grads[0, at, :] = dot(low_mid, weights[0], NT).astype(BF16)
                 return (
                     sums[0] + jnp.sum(part * scaled, 0, keepdims=True),
@@ -556,7 +576,7 @@
             gain_sum, bias_sum = lax.fori_loop(0, tokens // TILE, rows, (empty, empty))
             small[pl.ds(4 + 4 * layer, 1), :] = gain_sum
             small[pl.ds(5 + 4 * layer, 1), :] = bias_sum
-            merge_grad = dot(mixed_ref[...], low[...], TN).astype(BF16)
+            merge_grad = dot(mixed_ref[...], grads[1], TN).astype(BF16)
             for r in range(ROWS):
                 put(6, r, merge_grad[r * SHARE : (r + 1) * SHARE])
             fetch(4, 5, 6, 8, 9)
@@ -661,46 +681,41 @@
 
     @pl.when(busy & (j == FFN_STEPS + PAIRS))
     def _():
-        total[...] = jnp.zeros_like(total)
         take(jnp.int32(PAIRS - 1))
-        have(4)
+        have(8)
+        total[...] = dot(grads[0], weights[1], NT)
+        fetch(10)
         fetch(3, of_layer=layer - 1, when=more)
-
-    @pl.when(busy & (j >= FFN_STEPS + PAIRS))
-    def _():
-        n = j - FFN_STEPS - PAIRS
-
-        @pl.when(n < 3)
-        def _():
-            triple_grad = dot(normed_ref[...], grads[n], TN).astype(BF16)
-            for r in range(ROWS):
-                put(4 + n, r, triple_grad[r * SHARE : (r + 1) * SHARE])
-
-        for part in range(3):
-            @pl.when(n == part + 1)
-            def _():
-                have(8 + part)
-
-        @pl.when(n > 0)
-        def _():
-            total[...] += dot(grads[n - 1], weights[lax.rem(n, 2)], NT)
-
-        @pl.when(n == 1)
-        def _():
-            fetch(10)
-
-        fetch(7, 0, of_layer=layer - 1, when=more & (n == 2))
-
-        @pl.when(n == 3)
-        def _():
-            have(5, 6)
+        have(4, 9)
+        total[...] += dot(grads[1], weights[0], NT)
+        fetch(7, of_layer=layer - 1, when=more)
+
+    @pl.when(busy & (j > FFN_STEPS + PAIRS))
+    def _():
+        n = j - FFN_STEPS - PAIRS - 1
+
+        triple_grad = dot(normed_ref[...], grads[n], TN).astype(BF16)
+        for r in range(ROWS):
+            put(4 + n, r, triple_grad[r * SHARE : (r + 1) * SHARE])
+
+        fetch(0, of_layer=layer - 1, when=more & (n == 2))
+
+        @pl.when(n == 0)
+        def _():
+            have(5, 6, 10)
+
             def rows(i, sums):
                 at = pl.ds(pl.multiple_of(i * TILE, TILE), TILE)
-                part = total[at, :]
+                part = total[at, :] + dot(grads[2, at, :], weights[1], NT)
                 scaled = scaled_ref[at, :].astype(F32)
                 hidden = grad[at, :] + norm_back(part, scaled, inverse_ref[at, :], pick(first_gain_ref, layer))
                 grad[at, :] = hidden
                 low[at, :] = hidden.astype(BF16)
+
+                @pl.when(turn == layers - 1)
+                def _():
+                    swaps(1 + i, "start")
+
                 return (
                     sums[0] + jnp.sum(part * scaled, 0, keepdims=True),
                     sums[1] + jnp.sum(part, 0, keepdims=True),
@@ -729,16 +744,16 @@
     def slot(v):
         _, i = v
         return jnp.where(
-            i < 4, 4 + lax.rem(i, 2), jnp.where(i < 8, i - 4, jnp.where(i == 8, 6, i - FFN_STEPS - PAIRS + 4))
+            i < 4, 4 + lax.rem(i, 2), jnp.where(i < 8, i - 4, jnp.where(i == 8, 6, i - FFN_STEPS - PAIRS + 3))
         )
 
     def whether(ago):
         made, i = piece(ago)
-        return (made >= 0) & (made < layers) & (i != FFN_STEPS + PAIRS - 1) & (i != STEPS - 1)
+        return (made >= 0) & (made < layers) & ((i < FFN_STEPS + PAIRS - 1) | (i > FFN_STEPS + PAIRS))
 
     def order(v):
         made, i = v
-        return made * PIECES + i - jnp.where(i >= FFN_STEPS + PAIRS, 1, 0)
+        return made * PIECES + i - jnp.where(i > FFN_STEPS + PAIRS, 2, 0)
 
     def turns(v, count):
         return lax.rem(order(v), count)
@@ -808,9 +823,9 @@
         def _():
             go(merge_out.at[at_layer])
 
-        @pl.when(i >= FFN_STEPS + PAIRS)
-        def _():
-            go(triple_out.at[at_layer, :, columns(i - FFN_STEPS - PAIRS)])
+        @pl.when(i > FFN_STEPS + PAIRS)
+        def _():
+            go(triple_out.at[at_layer, :, columns(i - FFN_STEPS - PAIRS - 1)])
 
 
     if hosted:
@@ -894,7 +909,7 @@
             def small_copy(s):
                 return send(small, small_got.at[s], small_send.at[s], small_recv.at[s], mates[s])
 
-            @pl.when(t == last + s)
+            @pl.when(t == last - 2 + s)
             def _():
                 if s:
                     small_copy(s - 1).wait()
@@ -913,30 +928,14 @@
         def _():
             piece_copy(piece(0)).start()
 
-
-    def swaps(i, act):
-        source, target = ((done_ref, output_ref), (low, input_ref))[i]
-
-        @pl.when(swapped)
-        def _():
-            getattr(send(source, target, swap_send.at[i], swap_recv.at[i], diagonal), act)()
-
-        @pl.when(jnp.logical_not(swapped))
-        def _():
-            getattr(pltpu.make_async_copy(source, target, here_sem.at[i]), act)()
-
     @pl.when(t == 0)
     def _():
         swaps(0, "start")
 
-    @pl.when(t == last)
-    def _():
-        swaps(1, "start")
-
     @pl.when(t == (layers + 1) * STEPS - 1)
     def _():
-        swaps(0, "wait")
-        swaps(1, "wait")
+        for i in range(1 + tokens // TILE):
+            swaps(jnp.int32(i) if i else 0, "wait")
         small_ref[...] = small[...]
 
 
@@ -948,6 +947,7 @@
     left = (2, 2, 2, SHARE, left_part(width))
     right = (2, 2, 2, SHARE, width - left_part(width))
     count = layers * PIECES
+    moved = 1 + tokens // TILE
 
     def at(turn, j):
         return jnp.maximum(layers - 1 - turn, 0), jnp.where(turn < layers, j, STEPS - 1)
@@ -1033,7 +1033,7 @@
             pltpu.VMEM((STAGES, SMALL, width), F32),
             dma((6,)), dma((2, 2)), dma, dma((2,)), dma((2,)), dma((2,)), dma((2,)), dma((4, 2)), dma((4, 4)), dma((3, 2)), dma((3, 4)),
             dma((2, count)), dma((2, count)), dma((4,)),
-            dma((STAGES,)), dma((STAGES,)), dma((2,)), dma((2,)), dma((2,)),
+            dma((STAGES,)), dma((STAGES,)), dma((moved,)), dma((moved,)), dma((moved,)),
         ],
         compiler_params=params(1),
         name="back",
@@ -1075,7 +1075,7 @@
 
         down_grad = pieces[:, 4:8].reshape(layers, 4, ROWS, SHARE, width).transpose(0, 2, 1, 3, 4)
         triple_grad, merge_grad, up_grad, down_grad = map(
-            reduce, (columns(10, 13), columns(8, 9), columns(0, 4), down_grad.reshape(layers, -1, width))
+            reduce, (columns(11, 14), columns(8, 9), columns(0, 4), down_grad.reshape(layers, -1, width))
         )
         small = lax.psum(small, ("pass", "rows"))
     share = width // row_count

time: 352 us -> 353 us (level)
  no operation moved by 1% of the time
where the time goes in v8:
time: 353 us
  Pallas kernels  341 us (97%)
  local copies, waits for them, and re-layouts  10.9 us (3%)
    pallas_call x1, Pallas kernels, back(): pl.pallas_call(functools.partial(back_kernel, layers, hosted), grid=(laye...  213 us
    pallas_call x1, Pallas kernels, forward(): pl.pallas_call(functools.partial(forward_kernel, layers), grid=(layers, F...  128 us
    unnamed x16, local copies, waits for them, and re-layouts  8.04 us

profile of v8, /device:TPU:0, one launch (start us, length us, event | category | flops | bytes accessed | tf_op | source)
XLA Modules:
  0.0 352.8 jit_solution(6682027047103406188)
XLA Ops:
  1.3 127.8 %forward.1 = (bf16[2,2,1024,768]{3,2,1,0:T(8,128)(2,1)}, bf16[2,2,1024,768]{3,2,1,0:T(8,128)(2,1)}, f32[2,2,1024,1]{3,2,1,0:T(8,128)}, bf16[2,1024,768]{2,1,0:T(...) custom-call(bf16[1024,768]{1,0:T(8,128)(2,1)} %bitcast.20, ...), custom_call_target="tpu_custom_call" | custom-call | tf_op jit(solution)/shard_map/forward/pallas_call | solution.py:360
  129.1 212.9 %back.1 = (f32[2,48,2304]{2,1,0:T(8,128)}, f32[2,48,768]{2,1,0:T(8,128)}, f32[2,48,3072]{2,1,0:T(8,128)}, f32[2,192,768]{2,1,0:T(8,128)}, f32[16,768]{1,0:T(8,12...) custom-call(bf16[1024,768]{1,0:T(8,128)(2,1)} %get-tuple-element.31.cot_ref, ...), custom_call_target="tpu_custom_call" | custom-call | tf_op jit(solution)/shard_map/back/pallas_call | solution.py:1008
  341.9 0.0 copy-start
  341.9 0.9 dynamic-slice.1
  342.9 0.6 fusion
  343.4 1.3 constant_dynamic-slice_fusion
  344.8 2.7 copy.38
  347.4 0.0 copy-done
  347.4 0.0 copy-start.3
  347.4 0.0 copy-start.4
  347.4 0.0 copy-start.2
  347.4 1.1 copy.39
  348.6 0.6 copy-done.3
  349.2 0.0 copy-start.1
  349.2 0.9 copy.40
  350.1 0.0 copy-done.4
  350.1 0.7 copy.41
  350.8 0.0 copy-done.2
  350.8 1.0 copy.42
  351.8 0.0 copy-done.1
  351.8 1.0 copy.43
Async XLA Ops:
  341.9 5.5 %copy-start = (bf16[1024,768]{1,0:T(8,128)(2,1)S(1)}, bf16[1024,768]{1,0:T(8,128)(2,1)}, u32[]{:S(2)}) copy-start(bf16[1024,768]{1,0:T(8,128)(2,1)} %get-tuple-element.45) | copy-start | bytes 4718596
  347.4 1.7 copy-start.3
  347.4 2.6 copy-start.4
  347.4 3.4 copy-start.2
  349.2 2.6 copy-start.1

commit v9 on v8

--- a/solution.py
+++ b/solution.py
@@ -409,8 +409,8 @@
 
 
 FFN_STEPS = 4
-STEPS = FFN_STEPS + PAIRS + 4
-PIECES = STEPS - 2
+STEPS = FFN_STEPS + PAIRS + 3
+PIECES = STEPS - 1
 STAGES = 5
 ROWS = 16
 SHARE = 48
@@ -682,17 +682,17 @@
     @pl.when(busy & (j == FFN_STEPS + PAIRS))
     def _():
         take(jnp.int32(PAIRS - 1))
-        have(8)
+        have(4, 8)
         total[...] = dot(grads[0], weights[1], NT)
         fetch(10)
         fetch(3, of_layer=layer - 1, when=more)
-        have(4, 9)
+        have(9)
         total[...] += dot(grads[1], weights[0], NT)
         fetch(7, of_layer=layer - 1, when=more)
 
-    @pl.when(busy & (j > FFN_STEPS + PAIRS))
-    def _():
-        n = j - FFN_STEPS - PAIRS - 1
+    @pl.when(busy & (j >= FFN_STEPS + PAIRS))
+    def _():
+        n = j - FFN_STEPS - PAIRS
 
         triple_grad = dot(normed_ref[...], grads[n], TN).astype(BF16)
         for r in range(ROWS):
@@ -700,7 +700,7 @@
 
         fetch(0, of_layer=layer - 1, when=more & (n == 2))
 
-        @pl.when(n == 0)
+        @pl.when(n == 1)
         def _():
             have(5, 6, 10)
 
@@ -711,11 +711,6 @@
                 hidden = grad[at, :] + norm_back(part, scaled, inverse_ref[at, :], pick(first_gain_ref, layer))
                 grad[at, :] = hidden
                 low[at, :] = hidden.astype(BF16)
-
-                @pl.when(turn == layers - 1)
-                def _():
-                    swaps(1 + i, "start")
-
                 return (
                     sums[0] + jnp.sum(part * scaled, 0, keepdims=True),
                     sums[1] + jnp.sum(part, 0, keepdims=True),
@@ -744,16 +739,16 @@
     def slot(v):
         _, i = v
         return jnp.where(
-            i < 4, 4 + lax.rem(i, 2), jnp.where(i < 8, i - 4, jnp.where(i == 8, 6, i - FFN_STEPS - PAIRS + 3))
+            i < 4, 4 + lax.rem(i, 2), jnp.where(i < 8, i - 4, jnp.where(i == 8, 6, i - FFN_STEPS - PAIRS + 4))
         )
 
     def whether(ago):
         made, i = piece(ago)
-        return (made >= 0) & (made < layers) & ((i < FFN_STEPS + PAIRS - 1) | (i > FFN_STEPS + PAIRS))
+        return (made >= 0) & (made < layers) & (i != FFN_STEPS + PAIRS - 1)
 
     def order(v):
         made, i = v
-        return made * PIECES + i - jnp.where(i > FFN_STEPS + PAIRS, 2, 0)
+        return made * PIECES + i - jnp.where(i >= FFN_STEPS + PAIRS, 1, 0)
 
     def turns(v, count):
         return lax.rem(order(v), count)
@@ -823,9 +818,9 @@
         def _():
             go(merge_out.at[at_layer])
 
-        @pl.when(i > FFN_STEPS + PAIRS)
-        def _():
-            go(triple_out.at[at_layer, :, columns(i - FFN_STEPS - PAIRS - 1)])
+        @pl.when(i >= FFN_STEPS + PAIRS)
+        def _():
+            go(triple_out.at[at_layer, :, columns(i - FFN_STEPS - PAIRS)])
 
 
     if hosted:
@@ -909,7 +904,7 @@
             def small_copy(s):
                 return send(small, small_got.at[s], small_send.at[s], small_recv.at[s], mates[s])
 
-            @pl.when(t == last - 2 + s)
+            @pl.when(t == last - 1 + s)
             def _():
                 if s:
                     small_copy(s - 1).wait()
@@ -931,6 +926,11 @@
     @pl.when(t == 0)
     def _():
         swaps(0, "start")
+
+    for i in range(tokens // TILE):
+        @pl.when(t == last - 1 + i)
+        def _():
+            swaps(jnp.int32(1 + i), "start")
 
     @pl.when(t == (layers + 1) * STEPS - 1)
     def _():
@@ -1075,7 +1075,7 @@
 
         down_grad = pieces[:, 4:8].reshape(layers, 4, ROWS, SHARE, width).transpose(0, 2, 1, 3, 4)
         triple_grad, merge_grad, up_grad, down_grad = map(
-            reduce, (columns(11, 14), columns(8, 9), columns(0, 4), down_grad.reshape(layers, -1, width))
+            reduce, (columns(10, 13), columns(8, 9), columns(0, 4), down_grad.reshape(layers, -1, width))
         )
         small = lax.psum(small, ("pass", "rows"))
     share = width // row_count

time: 353 us -> 348 us (0.986)
  Pallas kernels: 341 us -> 335 us
    pallas_call x1, Pallas kernels: 213 us -> 208 us  [back(): pl.pallas_call(functools.partial(back_kernel, layers, hosted), grid=(laye...]
where the time goes in v9:
time: 348 us
  Pallas kernels  335 us (96%)
  local copies, waits for them, and re-layouts  10.9 us (3%)
    pallas_call x1, Pallas kernels, back(): pl.pallas_call(functools.partial(back_kernel, layers, hosted), grid=(laye...  208 us
    pallas_call x1, Pallas kernels, forward(): pl.pallas_call(functools.partial(forward_kernel, layers), grid=(layers, F...  128 us
    unnamed x16, local copies, waits for them, and re-layouts  8.04 us

profile of v9, /device:TPU:0, one launch (start us, length us, event | category | flops | bytes accessed | tf_op | source)
XLA Modules:
  0.0 347.6 jit_solution(17362574661101987790)
XLA Ops:
  1.3 127.8 %forward.1 = (bf16[2,2,1024,768]{3,2,1,0:T(8,128)(2,1)}, bf16[2,2,1024,768]{3,2,1,0:T(8,128)(2,1)}, f32[2,2,1024,1]{3,2,1,0:T(8,128)}, bf16[2,1024,768]{2,1,0:T(...) custom-call(bf16[1024,768]{1,0:T(8,128)(2,1)} %bitcast.20, ...), custom_call_target="tpu_custom_call" | custom-call | tf_op jit(solution)/shard_map/forward/pallas_call | solution.py:360
  129.1 207.6 %back.1 = (f32[2,48,2304]{2,1,0:T(8,128)}, f32[2,48,768]{2,1,0:T(8,128)}, f32[2,48,3072]{2,1,0:T(8,128)}, f32[2,192,768]{2,1,0:T(8,128)}, f32[16,768]{1,0:T(8,12...) custom-call(bf16[1024,768]{1,0:T(8,128)(2,1)} %get-tuple-element.31.cot_ref, ...), custom_call_target="tpu_custom_call" | custom-call | tf_op jit(solution)/shard_map/back/pallas_call | solution.py:1008
  336.7 0.0 copy-start
  336.7 0.9 dynamic-slice.1
  337.6 0.6 fusion
  338.2 1.3 constant_dynamic-slice_fusion
  339.5 2.7 copy.38
  342.2 0.0 copy-done
  342.2 0.0 copy-start.3
  342.2 0.0 copy-start.4
  342.2 0.0 copy-start.2
  342.2 1.1 copy.39
  343.3 0.6 copy-done.3
  343.9 0.0 copy-start.1
  343.9 0.9 copy.40
  344.8 0.0 copy-done.4
  344.8 0.7 copy.41
  345.5 0.0 copy-done.2
  345.5 1.0 copy.42
  346.6 0.0 copy-done.1
  346.6 1.0 copy.43
Async XLA Ops:
  336.7 5.5 %copy-start = (bf16[1024,768]{1,0:T(8,128)(2,1)S(1)}, bf16[1024,768]{1,0:T(8,128)(2,1)}, u32[]{:S(2)}) copy-start(bf16[1024,768]{1,0:T(8,128)(2,1)} %get-tuple-element.45) | copy-start | bytes 4718596
  342.2 1.7 copy-start.3
  342.2 2.6 copy-start.4
  342.2 3.4 copy-start.2
  343.9 2.6 copy-start.1

commit v10 on v9

--- a/solution.py
+++ b/solution.py
@@ -902,7 +902,7 @@
 
         for s in range(STAGES + 1):
             def small_copy(s):
-                return send(small, small_got.at[s], small_send.at[s], small_recv.at[s], mates[s])
+                return send(small, small_got.at[s], small_send.at[s], small_recv.at[s], mates[s - 1])
 
             @pl.when(t == last - 1 + s)
             def _():

time: 348 us -> 348 us (level)
  no operation moved by 1% of the time
where the time goes in v10:
time: 348 us
  Pallas kernels  336 us (97%)
  local copies, waits for them, and re-layouts  10.9 us (3%)
    pallas_call x1, Pallas kernels, back(): pl.pallas_call(functools.partial(back_kernel, layers, hosted), grid=(laye...  208 us
    pallas_call x1, Pallas kernels, forward(): pl.pallas_call(functools.partial(forward_kernel, layers), grid=(layers, F...  128 us
    unnamed x16, local copies, waits for them, and re-layouts  8.04 us

profile of v10, /device:TPU:0, one launch (start us, length us, event | category | flops | bytes accessed | tf_op | source)
XLA Modules:
  0.0 348.0 jit_solution(16496483630078612197)
XLA Ops:
  1.3 127.8 %forward.1 = (bf16[2,2,1024,768]{3,2,1,0:T(8,128)(2,1)}, bf16[2,2,1024,768]{3,2,1,0:T(8,128)(2,1)}, f32[2,2,1024,1]{3,2,1,0:T(8,128)}, bf16[2,1024,768]{2,1,0:T(...) custom-call(bf16[1024,768]{1,0:T(8,128)(2,1)} %bitcast.20, ...), custom_call_target="tpu_custom_call" | custom-call | tf_op jit(solution)/shard_map/forward/pallas_call | solution.py:360
  129.1 208.0 %back.1 = (f32[2,48,2304]{2,1,0:T(8,128)}, f32[2,48,768]{2,1,0:T(8,128)}, f32[2,48,3072]{2,1,0:T(8,128)}, f32[2,192,768]{2,1,0:T(8,128)}, f32[16,768]{1,0:T(8,12...) custom-call(bf16[1024,768]{1,0:T(8,128)(2,1)} %get-tuple-element.31.cot_ref, ...), custom_call_target="tpu_custom_call" | custom-call | tf_op jit(solution)/shard_map/back/pallas_call | solution.py:1008
  337.1 0.0 copy-start
  337.1 0.9 dynamic-slice.1
  338.0 0.6 fusion
  338.6 1.3 constant_dynamic-slice_fusion
  339.9 2.7 copy.38
  342.6 0.0 copy-done
  342.6 0.0 copy-start.3
  342.6 0.0 copy-start.4
  342.6 0.0 copy-start.2
  342.6 1.1 copy.39
  343.7 0.6 copy-done.3
  344.3 0.0 copy-start.1
  344.3 0.9 copy.40
  345.2 0.0 copy-done.4
  345.2 0.7 copy.41
  345.9 0.0 copy-done.2
  345.9 1.0 copy.42
  347.0 0.0 copy-done.1
  347.0 1.0 copy.43
Async XLA Ops:
  337.1 5.5 %copy-start = (bf16[1024,768]{1,0:T(8,128)(2,1)S(1)}, bf16[1024,768]{1,0:T(8,128)(2,1)}, u32[]{:S(2)}) copy-start(bf16[1024,768]{1,0:T(8,128)(2,1)} %get-tuple-element.45) | copy-start | bytes 4718596
  342.6 1.7 copy-start.3
  342.6 2.6 copy-start.4
  342.6 3.4 copy-start.2
  344.3 2.6 copy-start.1
